TPU v7x, 32 devices: a whole 2x2x4 slice. The times are simulated.
32 devices in a mesh: groups: 2 (over x), tensor: 4 (over y, core), rows: 4 (over z).
Axes of the slice: x: 2, y: 2, z: 4, core: 2. Of those that a mesh axis runs over, the one named last changes fastest.
Arguments:
- tokens: bfloat16 [2048, 8192], P(('groups', 'rows'), 'tensor'), parts along dimension 0, may hold values from -6 to 6
- norm_gain: bfloat16 [8192], replicated, may hold values from 0.099609375 to 1.8984375
- w_query: bfloat16 [8192, 4096], P(None, 'tensor'), may hold values from -0.0625 to 0.0625
- w_key: bfloat16 [8192, 512], P('tensor'), may hold values from -0.0625 to 0.0625
- w_value: bfloat16 [8192, 512], P('tensor'), may hold values from -0.0625 to 0.0625
- w_out: bfloat16 [4096, 8192], P('tensor'), may hold values from -0.75 to 0.75
- doc_ids: int32 [2048], P('groups'), parts along dimension 0, may hold values from 0 to 7, never falling along the last dimension, each value on 1 to 512 neighbouring positions
- assign: int32 [32, 1], P('groups'), parts along dimension 0, may hold values from 0 to 3; in each aligned block of 4 rows (0 to 3, 4 to 7, ...) at most 2 rows name the same one
- res_len: int32 [8], P('groups'), parts along dimension 0, may hold values from 1 to 512, 1280 in all
- res_mem: bfloat16 [8, 2, 512, 512], P(('groups', 'rows')), parts along dimension 0, may hold values from -160 to 160
Outputs:
- mixed: bfloat16 [2048, 8192], P(('groups', 'rows'), 'tensor'), parts along dimension 0
There are 2 independent parts, one for each index of `groups`. A program takes and returns all parts, laid end to end along the dimension named above; an argument that names none is the same for every part. Nothing has to cross between parts.
Inputs may be any that keep to these rules, and one draw needn't show every extreme that they name: `doc_ids`: documents never fall along the pack; each holds at most 512 tokens and one holds exactly that many. `assign`: among the 4 blocks of one index of rows, no server is named more than 2 times.
All inputs are finite; a program needn't handle non-finite values.
Results may differ from a plain program's by a relative error of at most 0.017.
The roundings to bfloat16 on the way count: a program that leaves them out, or rounds other values in their place, can miss the bound.
Values may be sent and summed in bfloat16 or wider, within the bound.
No kernel may reach another device: no remote copies, remote signals or barrier semaphores. Data moves between devices by JAX's collectives and lax.ppermute only.
A program may use at most 128 MiB of HBM per device.

v0:
```python
import math

import jax
import jax.numpy as jnp
from jax import lax
from jax.sharding import PartitionSpec as P

HD = 128
BLK = 64
CAP = 2


norm_eps = 1e-05
rope_base = 500000.0
masked_score = -1e30


def rotate(field, positions):
    half_dim = field.shape[-1] // 2
    frequency = rope_base ** (-(jnp.arange(half_dim, dtype=jnp.float32) / half_dim))
    angles = positions.astype(jnp.float32)[:, None] * frequency[None, :]
    cosine = jnp.cos(angles)[:, None, :]
    sine = jnp.sin(angles)[:, None, :]
    first = field[..., :half_dim]
    second = field[..., half_dim:]
    return jnp.concatenate([first * cosine - second * sine, first * sine + second * cosine], -1)


def attend(queries, block_ids, key_rows, value_rows, doc_ids, mem_keys, mem_values, mem_len):
    block_rows = queries.shape[1]
    score_scale = 1.0 / math.sqrt(queries.shape[3])
    q_pos = block_ids[:, None] * block_rows + jnp.arange(block_rows, dtype=jnp.int32)[None, :]
    q_doc = doc_ids[q_pos]
    all_rows = key_rows.shape[0]
    doc_scores = (
        jnp.einsum("bxhd,td->bhxt", queries, key_rows, preferred_element_type=jnp.float32)
        * score_scale
    )
    doc_mask = (doc_ids[None, None, :] == q_doc[:, :, None]) & (
        jnp.arange(all_rows, dtype=jnp.int32)[None, None, :] <= q_pos[:, :, None]
    )
    doc_scores = jnp.where(doc_mask[:, None], doc_scores, masked_score)
    mem_scores = (
        jnp.einsum("bxhd,bmd->bhxm", queries, mem_keys, preferred_element_type=jnp.float32)
        * score_scale
    )
    mem_mask = jnp.arange(mem_keys.shape[1], dtype=jnp.int32)[None, :] < mem_len[:, None]
    mem_scores = jnp.where(mem_mask[:, None, None, :], mem_scores, masked_score)
    row_max = jnp.maximum(jnp.max(doc_scores, -1), jnp.max(mem_scores, -1))[..., None]
    doc_exp = jnp.exp(doc_scores - row_max)
    mem_exp = jnp.exp(mem_scores - row_max)
    row_total = jnp.sum(doc_exp, -1, keepdims=True) + jnp.sum(mem_exp, -1, keepdims=True)
    doc_weights = (doc_exp / row_total).astype(jnp.bfloat16)
    mem_weights = (mem_exp / row_total).astype(jnp.bfloat16)
    mixed = jnp.einsum("bhxt,td->bxhd", doc_weights, value_rows, preferred_element_type=jnp.float32)
    mixed = mixed + jnp.einsum(
        "bhxm,bmd->bxhd", mem_weights, mem_values, preferred_element_type=jnp.float32
    )
    return mixed.astype(jnp.bfloat16).reshape(queries.shape[0], block_rows, -1)


def run_groups(
    queries, block_ids, mem_keys, mem_values, mem_len, group_size, key_rows, value_rows, doc_ids
):
    count = queries.shape[0]
    steps = count // group_size

    def one_group(items):
        return attend(
            items[0], items[1], key_rows, value_rows, doc_ids, items[2], items[3], items[4]
        )

    shaped = tuple(
        (
            member.reshape((steps, group_size) + member.shape[1:])
            for member in (queries, block_ids, mem_keys, mem_values, mem_len)
        )
    )
    result = lax.map(one_group, shaped)
    return result.reshape((count,) + result.shape[2:])


def on_device(tokens, norm_gain, w_query, w_key, w_value, w_out, doc_ids, assign, res_len, res_mem):
    n_tensor = lax.axis_size("tensor")
    n_rows = lax.axis_size("rows")
    tensor_index = lax.axis_index("tensor")
    row_index = lax.axis_index("rows")
    rows_dev, part_width = tokens.shape
    heads_local = w_query.shape[1] // HD
    kv_heads = w_key.shape[1] // HD
    whole = lax.all_gather(tokens, "tensor", axis=1, tiled=True)
    whole_f = whole.astype(jnp.float32)
    normed = (
        whole_f
        * lax.rsqrt(jnp.mean(whole_f * whole_f, -1, keepdims=True) + norm_eps)
        * norm_gain.astype(jnp.float32)
    ).astype(jnp.bfloat16)
    positions = row_index * rows_dev + jnp.arange(rows_dev, dtype=jnp.int32)
    query = jnp.dot(normed, w_query, preferred_element_type=jnp.float32).reshape(
        rows_dev, heads_local, HD
    )
    query = rotate(query, positions).astype(jnp.bfloat16)
    own_features = lax.dynamic_slice_in_dim(normed, tensor_index * part_width, part_width, 1)
    key_sum, value_sum = (
        lax.psum(
            jnp.dot(own_features, w_key, preferred_element_type=jnp.float32).astype(jnp.bfloat16),
            "tensor",
        ).astype(jnp.float32),
        lax.psum(
            jnp.dot(own_features, w_value, preferred_element_type=jnp.float32).astype(jnp.bfloat16),
            "tensor",
        ).astype(jnp.float32),
    )
    head_group = tensor_index // (n_tensor // kv_heads)
    key_own = lax.dynamic_slice_in_dim(key_sum, head_group * HD, HD, 1)
    key_own = rotate(key_own[:, None, :], positions)[:, 0, :].astype(jnp.bfloat16)
    value_own = lax.dynamic_slice_in_dim(value_sum, head_group * HD, HD, 1).astype(jnp.bfloat16)
    gathered = lax.all_gather(jnp.concatenate([key_own, value_own], 1), "rows", axis=0, tiled=True)
    key_rows = gathered[:, :HD]
    value_rows = gathered[:, HD:]
    blocks_dev = rows_dev // BLK
    query_width = heads_local * HD
    query_blocks = query.reshape(blocks_dev, BLK, query_width)
    mem_local = lax.dynamic_slice_in_dim(res_mem[0], head_group * HD, HD, 2)
    listed = assign[:, 0]
    own_servers = lax.dynamic_slice_in_dim(listed, row_index * blocks_dev, blocks_dev, 0)
    earlier = jnp.arange(blocks_dev)[:, None] > jnp.arange(blocks_dev)[None, :]
    per_step = max(1, 512 // BLK)
    same_server = own_servers[:, None] == own_servers[None, :]
    slot_rank = jnp.sum(same_server & earlier, axis=1)
    onehot = (
        (own_servers[None, None, :] == jnp.arange(n_rows)[:, None, None])
        & (slot_rank[None, None, :] == jnp.arange(CAP)[None, :, None])
    ).astype(jnp.bfloat16)
    outgoing = jnp.einsum(
        "pcb,bxq->pcxq", onehot, query_blocks, preferred_element_type=jnp.float32
    ).astype(jnp.bfloat16)
    received = lax.all_to_all(outgoing, "rows", split_axis=0, concat_axis=0, tiled=True)
    server_table = listed.reshape(n_rows, blocks_dev)
    arriving = server_table == row_index
    arrive_rank = jnp.sum(arriving[:, None, :] & earlier[None], -1)
    arrive_pick = arriving[:, None, :] & (arrive_rank[:, None, :] == jnp.arange(CAP)[None, :, None])
    block_numbers = (
        jnp.arange(n_rows, dtype=jnp.int32)[:, None] * blocks_dev
        + jnp.arange(blocks_dev, dtype=jnp.int32)[None, :]
    )
    slot_blocks = jnp.sum(jnp.where(arrive_pick, block_numbers[:, None, :], 0), -1)
    slots = n_rows * CAP
    slot_queries = received.reshape(slots, BLK, heads_local, HD)
    mem_keys = jnp.broadcast_to(mem_local[0][None], (slots,) + mem_local.shape[1:])
    mem_values = jnp.broadcast_to(mem_local[1][None], (slots,) + mem_local.shape[1:])
    mem_len = jnp.full((slots,), res_len[row_index], jnp.int32)
    results = run_groups(
        slot_queries,
        slot_blocks.reshape(slots),
        mem_keys,
        mem_values,
        mem_len,
        math.gcd(slots, per_step),
        key_rows,
        value_rows,
        doc_ids,
    )
    returned = lax.all_to_all(
        results.reshape(n_rows, CAP, BLK, query_width),
        "rows",
        split_axis=0,
        concat_axis=0,
        tiled=True,
    )
    attended = jnp.einsum(
        "pcb,pcxq->bxq", onehot, returned, preferred_element_type=jnp.float32
    ).astype(jnp.bfloat16)
    attended = attended.reshape(rows_dev, query_width)
    term = jnp.dot(attended, w_out, preferred_element_type=jnp.float32)
    mixed = lax.psum_scatter(term.astype(jnp.bfloat16), "tensor", scatter_dimension=1, tiled=True)
    return mixed


def solution(mesh):
    in_specs = (
        P(("groups", "rows"), "tensor"),
        P(),
        P(None, "tensor"),
        P("tensor", None),
        P("tensor", None),
        P("tensor", None),
        P("groups"),
        P("groups", None),
        P("groups"),
        P(("groups", "rows"), None, None, None),
    )
    out_specs = P(("groups", "rows"), "tensor")
    return jax.shard_map(
        on_device, mesh=mesh, in_specs=in_specs, out_specs=out_specs, check_vma=False
    )
```

profile of v0, /device:TPU:0, one launch (start us, length us, event | category | flops | bytes accessed | tf_op | source)
XLA Modules:
  0.0 245.4 jit_solution(4032531245582613089)
XLA Ops:
  6.5 0.7 all-gather.2.cloned.1.call-update
  7.3 0.7 compare_reduce_fusion
  8.0 0.7 fusion.40
  9.6 0.7 convert_element_type.71
  10.3 1.2 dynamic_slice.35
  12.4 1.0 dynamic-slice_bitcast_fusion
  14.1 32.1 %all-gather.2.cloned.1.call-done = bf16[256,8192]{1,0:T(8,128)(2,1)} async-done(((bf16[256,2048]{1,0:T(8,128)(2,1)}), bf16[256,8192]{1,0:T(8,128)(2,1)}) %all-gather.2.cloned.1.call-update) | async-done | bytes 4194320 | tf_op jit(solution)/shard_map/all_gather | solution.py:91
  46.1 3.1 %fusion.2 = f32[256]{0:T(256)S(1)} fusion(bf16[256,8192]{1,0:T(8,128)(2,1)} %all-gather.2.cloned.1.call-done), kind=kLoop, calls=%fused_computation.9 | loop fusion | flops 6291200 | bytes 4195328 | tf_op jit(solution)/shard_map/reduce_sum | solution.py:95
  49.3 3.4 %fusion.4 = bf16[256,8192]{1,0:T(8,128)(2,1)S(1)} fusion(bf16[256,8192]{1,0:T(8,128)(2,1)} %all-gather.2.cloned.1.call-done, f32[8192]{0:T(1024)S(1)} %convert_element_type.71, f32[256]{0:T(256)S(1)} %add_rsqrt_fusion), kind=kLoop, calls=%fused_computation.11 | loop fusion | flops 8388608 | bytes 8422400 | tf_op jit(solution)/shard_map/convert_element_type | solution.py:97
  52.6 9.8 %convolution_bitcast_fusion = f32[32,8,8,128]{3,1,2,0:T(8,128)S(1)} fusion(bf16[256,8192]{1,0:T(8,128)(2,1)S(1)} %fusion.4, bf16[8192,1024]{1,0:T(8,128)(2,1)} %param.12), kind=kOutput, calls=%fused_computation.25 | convolution fusion | flops 4294967296 | bytes 22020096 | tf_op jit(solution)/shard_map/dot_general | solution.py:99
  63.7 1.1 convolution_convert_fusion.1
  64.8 1.3 copy.49
  66.1 4.6 %all-to-all-start = ((bf16[4,2,64,1024]{3,2,1,0:T(8,128)(2,1)}), bf16[4,2,64,1024]{3,2,1,0:T(8,128)(2,1)S(1)}, u32[]{:S(2)}, u32[]{:S(2)}) async-start(bf16[4,2,64,1024]{3,2,1,0:T(8,128)(2,1)} %copy.49), calls=%async_computation | async-start | bytes 2097152 | tf_op jit(solution)/shard_map/all_to_all | solution.py:138
  70.7 2.8 %convolution_convert_fusion.2 = bf16[256,512]{0,1:T(8,128)(2,1)} fusion(bf16[2048,512]{1,0:T(8,128)(2,1)S(1)} %copy-done, bf16[256,8192]{1,0:T(8,128)(2,1)} %copy-done.3, s32[]{:T(128)S(6)} %select_n.46), kind=kOutput, calls=%fused_computation.28 | convolution fusion | flops 537001984 | bytes 3407876 | tf_op jit(solution)/shard_map/dot_general | solution.py:110
  73.6 3.3 %convolution_convert_fusion.3 = bf16[256,512]{1,0:T(8,128)(2,1)} fusion(bf16[2048,512]{1,0:T(8,128)(2,1)} %param.13, bf16[256,8192]{1,0:T(8,128)(2,1)} %copy-done.3, s32[]{:T(128)S(6)} %select_n.46), kind=kOutput, calls=%fused_computation.29 | convolution fusion | flops 537001984 | bytes 3407876 | tf_op jit(solution)/shard_map/dot_general | solution.py:106
  77.0 2.3 gather_fusion
  80.0 30.8 %all-reduce.3.cloned.1.call-done = (bf16[256,512]{0,1:T(8,128)(2,1)}, bf16[256,512]{1,0:T(8,128)(2,1)}) async-done(((bf16[256,512]{0,1:T(8,128)(2,1)}, bf16[256,512]{1,0:T(8,128)(2,1)}), (bf16[256,512]{0,1:T(8,128)(2,1)}, bf16[256,512]{1,0:T(8,128)(2,1)})) %all-reduce.3.cloned.1.call-update) | async-done | bytes 524304 | tf_op jit(solution)/shard_map/psum | solution.py:109
  110.8 0.8 dynamic-slice_convert_fusion
  111.7 0.9 convert_convert_fusion
  112.9 15.0 %all_gather.7 = bf16[1024,256]{0,1:T(8,128)(2,1)S(1)} all-gather(bf16[256,256]{0,1:T(8,128)(2,1)S(1)} %pad_maximum_fusion.1), channel_id=1, replica_groups=mesh['groups'=2,'tensor'=4,'rows'=4] {'rows'}, dimensions={0}, use_global_device_ids=true | all-gather | bytes 655360 | tf_op jit(solution)/shard_map/all_gather | solution.py:118
  128.2 4.5 %bitcast_reduce_fusion = (f32[8,8,64]{2,1,0:T(8,128)S(1)}, f32[8,512,64,8]{1,2,3,0:T(8,128)}) fusion(pred[8,512]{1,0:T(8,128)(4,1)S(1)} %iota_compare_fusion.1, bf16[8,64,8,128]{3,2,1,0:T(8,128)(2,1)S(1)} %bitcast.89, bf16[512,128]{1,0:T(8,128)(2,1)S(1)} %get-tuple-element.28), kind=kOutput, calls=%fused_computation.13 | convolution fusion | flops 543158272 | bytes 9588736 | tf_op jit(solution)/shard_map/while/body/eval_jaxpr/bxhd,bmd->bhxm/dot_general | solution.py:44
  132.7 2.8 %fusion.1 = (f32[8,8,64]{2,1,0:T(8,128)S(1)}, f32[1024,8,64,8]{0,2,3,1:T(8,128)S(1)}) fusion(pred[8,64,1024]{2,1,0:T(8,128)(4,1)S(1)} %fusion.10, bf16[8,64,8,128]{3,2,1,0:T(8,128)(2,1)S(1)} %bitcast.90, bf16[1024,256]{0,1:T(8,128)(2,1)S(1)} %all_gather.7), kind=kOutput, calls=%fused_computation.5 | convolution fusion | flops 1086320640 | bytes 18628608 | tf_op jit(solution)/shard_map/while/body/eval_jaxpr/bxhd,td->bhxt/dot_general | solution.py:36
  135.6 4.6 %fusion.7 = f32[8,8,64]{2,1,0:T(8,128)S(1)} fusion(f32[8,512,64,8]{1,2,3,0:T(8,128)} %get-tuple-element.48, f32[8,8,64]{2,1,0:T(8,128)S(1)} %max.8, pred[8,512]{1,0:T(8,128)(4,1)S(1)} %iota_compare_fusion.1), kind=kLoop, calls=%fused_computation.18 | loop fusion | flops 8384512 | bytes 8425472 | tf_op jit(solution)/shard_map/while/body/eval_jaxpr/reduce_sum | solution.py:52
  140.2 4.3 %fusion = f32[8,8,64]{2,1,0:T(8,128)S(1)} fusion(f32[1024,8,64,8]{0,2,3,1:T(8,128)S(1)} %get-tuple-element.46, f32[8,8,64]{2,1,0:T(8,128)S(1)} %max.8, pred[8,64,1024]{2,1,0:T(8,128)(4,1)S(1)} %fusion.10), kind=kLoop, calls=%fused_computation.4 | loop fusion | flops 16773120 | bytes 17334272 | tf_op jit(solution)/shard_map/while/body/eval_jaxpr/reduce_sum | solution.py:52
  144.5 4.5 %fusion.6 = f32[128,8,8,64]{0,3,2,1:T(8,128)S(1)} fusion(f32[1024,8,64,8]{0,2,3,1:T(8,128)S(1)} %get-tuple-element.46, f32[8,8,64]{2,1,0:T(8,128)S(1)} %add.144, f32[8,8,64]{2,1,0:T(8,128)S(1)} %max.8, pred[8,64,1024]{2,1,0:T(8,128)(4,1)S(1)} %fusion.10, bf16[1024,256]{0,1:T(8,128)(2,1)S(1)} %all_gather.7), kind=kOutput, calls=%fused_computation.17 | convolution fusion | flops 1094713344 | bytes 19726336 | tf_op jit(solution)/shard_map/while/body/eval_jaxpr/bhxt,td->bxhd/dot_general | solution.py:55
  149.0 4.6 %fusion.9 = bf16[8,64,8,128]{3,1,2,0:T(8,128)(2,1)S(1)} fusion(f32[128,8,8,64]{0,3,2,1:T(8,128)S(1)} %fusion.6, f32[8,512,64,8]{1,2,3,0:T(8,128)} %get-tuple-element.48, f32[8,8,64]{2,1,0:T(8,128)S(1)} %add.144, f32[8,8,64]{2,1,0:T(8,128)S(1)} %max.8, pred[8,512]{1,0:T(8,128)(4,1)S(1)} %iota_compare_fusion.1, bf16[512,128]{1,0:T(8,128)(2,1)S(1)} %get-tuple-element.27), kind=kOutput, calls=%fused_computation.21 | convolution fusion | flops 548405248 | bytes 11702272 | tf_op jit(solution)/shard_map/while/body/eval_jaxpr/bhxm,bmd->bxhd/dot_general | solution.py:56
  153.6 0.7 copy.54
  154.8 1.1 copy.55
  155.9 26.5 %all_to_all.10 = bf16[4,2,64,1024]{3,1,2,0:T(2,128)(2,1)S(1)} all-to-all(bf16[4,2,64,1024]{3,1,2,0:T(2,128)(2,1)S(1)} %copy.55), channel_id=1, replica_groups=mesh['groups'=2,'tensor'=4,'rows'=4] {'rows'}, dimensions={0} | all-to-all | bytes 2097152 | tf_op jit(solution)/shard_map/all_to_all | solution.py:164
  182.5 1.4 fusion.11
  184.1 12.0 %convolution_convert_fusion = bf16[256,8192]{1,0:T(8,128)(2,1)} fusion(bf16[256,1024]{1,0:T(8,128)(2,1)S(1)} %bitcast.92, bf16[1024,8192]{1,0:T(8,128)(2,1)} %param.15), kind=kOutput, calls=%fused_computation.8 | convolution fusion | flops 4297064448 | bytes 21495808 | tf_op jit(solution)/shard_map/dot_general | solution.py:175
  196.0 42.8 %reduce-scatter.2.cloned.1.call-done = bf16[256,2048]{1,0:T(8,128)(2,1)} async-done(((bf16[256,8192]{1,0:T(8,128)(2,1)}), bf16[256,2048]{1,0:T(8,128)(2,1)}) %reduce-scatter.2.cloned.1.call-update) | async-done | bytes 1048592 | tf_op jit(solution)/shard_map/reduce_scatter | solution.py:176
  (51 shorter events, 5.7 us)
Async XLA Ops:
  6.5 64.2 %copy-start = (bf16[2048,512]{1,0:T(8,128)(2,1)S(1)}, bf16[2048,512]{1,0:T(8,128)(2,1)}, u32[]{:S(2)}) copy-start(bf16[2048,512]{1,0:T(8,128)(2,1)} %param.14) | copy-start | bytes 6291460
  6.5 39.6 %all-gather.2.cloned.1.call-start = ((), (), s32[]{:S(2)}) async-start(), calls=%async_computation.3 | async-start | bytes 5242880 | tf_op jit(solution)/shard_map/all_gather | solution.py:91
  52.6 9.8 %copy-start.3 = (bf16[256,8192]{1,0:T(8,128)(2,1)}, bf16[256,8192]{1,0:T(8,128)(2,1)S(1)}, u32[]{:S(2)}) copy-start(bf16[256,8192]{1,0:T(8,128)(2,1)S(1)} %fusion.4) | copy-start | bytes 12582916
  63.2 13.8 %copy-start.2 = (s32[1024]{0:T(1024)S(1)}, s32[1024]{0:T(1024)}, u32[]{:S(2)}) copy-start(s32[1024]{0:T(1024)} %param.16) | copy-start | bytes 12292
  66.1 61.8 %all-to-all-start = ((bf16[4,2,64,1024]{3,2,1,0:T(8,128)(2,1)}), bf16[4,2,64,1024]{3,2,1,0:T(8,128)(2,1)S(1)}, u32[]{:S(2)}, u32[]{:S(2)}) async-start(bf16[4,2,64,1024]{3,2,1,0:T(8,128)(2,1)} %copy.49), calls=%async_computation | async-start | bytes 2097152 | tf_op jit(solution)/shard_map/all_to_all | solution.py:138
  70.7 40.0 %all-reduce.3.cloned.1.call-start = ((), (), s32[]{:S(2)}) async-start(), calls=%async_computation.5 | async-start | bytes 1048576 | tf_op jit(solution)/shard_map/psum | solution.py:109
  76.9 161.9 %reduce-scatter.2.cloned.1.call-start = ((), (), s32[]{:S(2)}) async-start(), calls=%async_computation.4 | async-start | bytes 5242880 | tf_op jit(solution)/shard_map/reduce_scatter | solution.py:176
  184.0 54.8 %copy-start.1 = (bf16[2048,512]{1,0:T(8,128)(2,1)S(1)}, bf16[2048,512]{1,0:T(8,128)(2,1)}, u32[]{:S(2)}) copy-start(bf16[2048,512]{1,0:T(8,128)(2,1)} %param.14) | copy-start | bytes 6291460
Sparse Core Ops, SparseCore 0:
  8.9 37.1 all-gather.1
  77.0 33.6 all-reduce.2
  196.2 42.6 reduce-scatter.1
where the time goes:
time: 246 us; the launch traced here: 245 us
  waiting for transfers between devices  106 us (43%)
  matrix products  46.9 us (19%)
  blocking collectives  41.6 us (17%)
  other arithmetic  22.1 us (9%)
  between operations  13.4 us (5%)
  local copies, waits for them, and re-layouts  10.3 us (4%)
  starting transfers between devices  4.65 us (2%)
    reduce_scatter x1, waiting for transfers between devices, on_device(): lax.psum_scatter(term.astype(jnp.bfloat16), 'tensor', scatter_dimension=1...  42.8 us
    all_gather x1, waiting for transfers between devices, on_device(): whole = lax.all_gather(tokens, 'tensor', axis=1, tiled=True)  32.1 us
    psum x1, waiting for transfers between devices, on_device(): lax.psum(jnp.dot(own_features, w_value, preferred_element_type=jnp.float3...  30.8 us
    all_to_all x1, blocking collectives, on_device(): lax.all_to_all(results.reshape(n_rows, CAP, BLK, query_width), 'rows', sp...  26.5 us
    all_gather x1, blocking collectives, on_device(): lax.all_gather(jnp.concatenate([key_own, value_own], 1), 'rows', axis=0,...  15 us
    dot_general x1, matrix products, on_device(): term = jnp.dot(attended, w_out, preferred_element_type=jnp.float32)  12 us
    dot_general x1, matrix products, on_device(): jnp.dot(normed, w_query, preferred_element_type=jnp.float32)  9.8 us
  transfers between devices with their start and end apart: 4, of which 3 were waited for; matrix products, arithmetic and copies ran while one was open for 7% of the time, Pallas kernels for 0%

commit v1 on v0

v1 whole, which is shorter than its diff:
```python
import functools
import math

import jax
import jax.numpy as jnp
from jax import lax
from jax.experimental import pallas as pl
from jax.experimental.pallas import tpu as pltpu
from jax.sharding import PartitionSpec as P

HD = 128
BLK = 64
HALVES = 2

norm_eps = 1e-05
rope_base = 500000.0
masked_score = -1e30
MIB = 1 << 20
f32 = jnp.float32
bf16 = jnp.bfloat16
NT = (((1,), (1,)), ((), ()))


def params(mib):
    return pltpu.CompilerParams(vmem_limit_bytes=mib * MIB)


def whole(shape):
    return pl.BlockSpec(shape, lambda *_: (0,) * len(shape))


def cost(flops, moved, exps=0):
    return pl.CostEstimate(flops=flops, bytes_accessed=moved, transcendentals=exps)


def prep_kernel(x_ref, *out_refs):
    stat_ref = out_refs[-1]
    rows, width = x_ref.shape
    part = rows // (len(out_refs) - 1)
    for at, out_ref in enumerate(out_refs[:-1]):
        out_ref[...] = x_ref[at * part : (at + 1) * part, :]
    lanes = jnp.zeros((rows, HD), f32)
    for at in range(width // HD):
        piece = x_ref[:, at * HD : (at + 1) * HD].astype(f32)
        lanes = lanes + piece * piece
    total = jnp.sum(lanes, -1, keepdims=True)
    stat_ref[...] = jnp.broadcast_to(total, (rows, HD)).T[:8, :]


def prep(tokens):
    rows, width = tokens.shape
    halves = [jax.ShapeDtypeStruct((rows // HALVES, width), bf16)] * HALVES
    return pl.pallas_call(
        prep_kernel,
        out_shape=halves + [jax.ShapeDtypeStruct((8, rows), f32)],
        compiler_params=params(16),
        cost_estimate=cost(2 * rows * width, 4 * rows * width),
        name="prep",
    )(tokens)


def inverse_rms(stat_refs, features):
    total = stat_refs[0][...]
    for ref in stat_refs[1:]:
        total = total + ref[...]
    return lax.rsqrt(total / features + norm_eps).T[:, :1]


def normalise(x, inverse, gain):
    return (x.astype(f32) * inverse * gain.astype(f32)).astype(bf16)


def kv_kernel(heads_ref, features, n_stats, *refs):
    stats = refs[:n_stats]
    x_ref, gain_ref, wk_ref, wv_ref, own_ref, send_ref, acc_k, acc_v, inv_ref = refs[n_stats:]
    step = pl.program_id(0)

    @pl.when(step == 0)
    def _():
        inv_ref[...] = jnp.broadcast_to(inverse_rms(stats, features), inv_ref.shape)
        acc_k[...] = jnp.zeros_like(acc_k)
        acc_v[...] = jnp.zeros_like(acc_v)

    normed = normalise(x_ref[...], inv_ref[:, :1], gain_ref[0])
    acc_k[...] += jnp.dot(normed, wk_ref[...], preferred_element_type=f32)
    acc_v[...] += jnp.dot(normed, wv_ref[...], preferred_element_type=f32)

    @pl.when(step == pl.num_programs(0) - 1)
    def _():
        chips = own_ref.shape[0]
        for at, out_ref in enumerate((own_ref, send_ref)):
            for chip in range(chips):
                head = heads_ref[at * chips + chip]
                columns = pl.ds(pl.multiple_of(head * HD, HD), HD)
                out_ref[chip, :, :HD] = acc_k[:, columns].astype(bf16)
                out_ref[chip, :, HD:] = acc_v[:, columns].astype(bf16)


def kv_partial(heads, stats, tokens, gain, w_key, w_value, me, features, chips):
    rows, width = tokens.shape
    kv_width = w_key.shape[1]
    tile = min(width, 512)
    steps = width // tile
    out = jax.ShapeDtypeStruct((chips, rows, 2 * HD), bf16)

    def body(scalars, *refs):
        kv_kernel(scalars, features, len(stats), *refs)

    gains = gain.reshape(features // tile, 1, tile)
    scalars = jnp.concatenate([heads, me[None]]).astype(jnp.int32)
    return pl.pallas_call(
        body,
        out_shape=[out, out],
        grid_spec=pltpu.PrefetchScalarGridSpec(
            num_scalar_prefetch=1,
            grid=(steps,),
            in_specs=[whole((8, rows))] * len(stats)
            + [
                pl.BlockSpec((rows, tile), lambda k, s: (0, k)),
                pl.BlockSpec((1, 1, tile), lambda k, s: (s[2 * chips] * steps + k, 0, 0)),
                pl.BlockSpec((tile, kv_width), lambda k, s: (k, 0)),
                pl.BlockSpec((tile, kv_width), lambda k, s: (k, 0)),
            ],
            out_specs=[whole(out.shape)] * 2,
            scratch_shapes=[
                pltpu.VMEM((rows, kv_width), f32),
                pltpu.VMEM((rows, kv_width), f32),
                pltpu.VMEM((rows, HD), f32),
            ],
        ),
        compiler_params=params(24),
        cost_estimate=cost(4 * rows * width * kv_width, 4 * width * kv_width + 2 * rows * width),
        name="kv_partial",
    )(scalars, *stats, tokens, gains, w_key, w_value)


def turn(x, cosine, sine):
    return x * cosine + pltpu.roll(x, HD // 2, 1) * sine


def kv_final(own, arrived, others, cosine, sine, chip):
    _, rows, width = own.shape

    def body(chip_ref, own_ref, arrived_ref, *refs):
        cos_ref, sin_ref, out_ref = refs[-3:]
        total = own_ref[0].astype(f32) + arrived_ref[0].astype(f32)
        for ref in refs[:-3]:
            total = total + ref[...].astype(f32)
        out_ref[:, :HD] = turn(total[:, :HD], cos_ref[...], sin_ref[...]).astype(bf16)
        out_ref[:, HD:] = total[:, HD:].astype(bf16)

    mine = pl.BlockSpec((1, rows, width), lambda i, s: (s[0], 0, 0))
    return pl.pallas_call(
        body,
        out_shape=jax.ShapeDtypeStruct((rows, width), bf16),
        grid_spec=pltpu.PrefetchScalarGridSpec(
            num_scalar_prefetch=1,
            grid=(1,),
            in_specs=[mine, mine]
            + [whole((rows, width))] * len(others)
            + [whole((rows, HD))] * 2,
            out_specs=whole((rows, width)),
        ),
        compiler_params=params(16),
        cost_estimate=cost(8 * rows * width, 8 * rows * width),
        name="kv_final",
    )(chip[None], own, arrived, *others, cosine, sine)


def query_kernel(order_ref, features, n_stats, n_sources, per_source, *refs):
    stats = refs[:n_stats]
    sources = refs[n_stats : n_stats + n_sources]
    gain_ref, w_ref, cos_ref, sin_ref, out_ref, acc_ref, inv_ref = refs[n_stats + n_sources :]
    step = pl.program_id(0)

    @pl.when(step == 0)
    def _():
        inv_ref[...] = jnp.broadcast_to(inverse_rms(stats, features), inv_ref.shape)
        acc_ref[...] = jnp.zeros_like(acc_ref)

    for at, x_ref in enumerate(sources):

        @pl.when(step // per_source == at)
        def _():
            normed = normalise(x_ref[...], inv_ref[:, :1], gain_ref[0])
            acc_ref[...] += jnp.dot(normed, w_ref[...], preferred_element_type=f32)

    @pl.when(step == pl.num_programs(0) - 1)
    def _():
        for head in range(out_ref.shape[1] // HD):
            columns = slice(head * HD, (head + 1) * HD)
            rotated = turn(acc_ref[:, columns], cos_ref[...], sin_ref[...])
            out_ref[:, columns] = rotated.astype(bf16)


def query_half(half, order, stats, sources, gain, w_query, cosine, sine):
    rows, width = sources[0].shape
    features, columns = w_query.shape
    tile = min(width, 1024)
    per_source = width // tile

    def body(order_ref, *refs):
        query_kernel(order_ref, features, len(stats), len(sources), per_source, *refs)

    def source_spec(at):
        return pl.BlockSpec(
            (rows, tile), lambda k, s: (0, jnp.clip(k - at * per_source, 0, per_source - 1))
        )

    def place(k, s):
        return s[k // per_source] * per_source + k % per_source

    table = pl.BlockSpec((rows, HD), lambda k, s: (half, 0))
    return pl.pallas_call(
        body,
        out_shape=jax.ShapeDtypeStruct((rows, columns), bf16),
        grid_spec=pltpu.PrefetchScalarGridSpec(
            num_scalar_prefetch=1,
            grid=(features // tile,),
            in_specs=[pl.BlockSpec((8, rows), lambda k, s: (0, half))] * len(stats)
            + [source_spec(at) for at in range(len(sources))]
            + [
                pl.BlockSpec((1, 1, tile), lambda k, s: (place(k, s), 0, 0)),
                pl.BlockSpec((tile, columns), lambda k, s: (place(k, s), 0)),
                table,
                table,
            ],
            out_specs=whole((rows, columns)),
            scratch_shapes=[pltpu.VMEM((rows, columns), f32), pltpu.VMEM((rows, HD), f32)],
        ),
        compiler_params=params(24),
        cost_estimate=cost(2 * rows * features * columns, 2 * features * columns),
        name="query_half",
    )(order, *stats, *sources, gain.reshape(features // tile, 1, tile), w_query, cosine, sine)


def attend_kernel(half, pick_ref, q_ref, qdoc_ref, kdoc_ref, *refs):
    rows, columns = q_ref.shape
    heads = columns // HD
    n_kv = kdoc_ref.shape[1] // refs[0].shape[0]
    out_ref = refs[-1]
    kv_refs, mem_refs = refs[:n_kv], refs[n_kv:-1]
    rows_dev = kv_refs[0].shape[0]
    back = (n_kv - 1) * rows_dev
    low, high = half * rows, back + (half + 1) * rows
    keys, values = [], []
    for at, ref in enumerate(kv_refs):
        first, last = max(low, at * rows_dev), min(high, (at + 1) * rows_dev)
        if first < last:
            part = slice(first - at * rows_dev, last - at * rows_dev)
            keys.append(ref[part, :HD])
            values.append(ref[part, HD:])
    keys, values = jnp.concatenate(keys, 0), jnp.concatenate(values, 0)
    span = high - low
    scale = math.log2(math.e) / math.sqrt(HD)
    blocks = rows // BLK
    for block in range(blocks):
        tokens = slice(block * BLK, (block + 1) * BLK)
        query = jnp.concatenate(
            [q_ref[tokens, h * HD : (h + 1) * HD] for h in range(heads)], 0
        )
        slot = pick_ref[block]
        mem_keys, mem_values = mem_refs[0][0], mem_refs[0][1]
        for at, ref in enumerate(mem_refs[1:]):
            mem_keys = jnp.where(slot == at + 1, ref[0], mem_keys)
            mem_values = jnp.where(slot == at + 1, ref[1], mem_values)
        column = lax.broadcasted_iota(jnp.int32, (BLK, span), 1)
        row = lax.broadcasted_iota(jnp.int32, (BLK, span), 0)
        mask = (column - back <= row + block * BLK) & (
            kdoc_ref[:, low:high] == qdoc_ref[tokens, :1]
        )
        live = lax.broadcasted_iota(jnp.int32, (1, mem_keys.shape[0]), 1) < pick_ref[blocks + block]
        doc = lax.dot_general(query, keys, NT, preferred_element_type=f32)
        mem = lax.dot_general(query, mem_keys, NT, preferred_element_type=f32)
        doc = jnp.where(mask[None], (doc * scale).reshape(heads, BLK, span), masked_score)
        doc = doc.reshape(heads * BLK, span)
        mem = jnp.where(live, mem * scale, masked_score)
        top = jnp.maximum(jnp.max(doc, -1, keepdims=True), jnp.max(mem, -1, keepdims=True))
        doc, mem = jnp.exp2(doc - top), jnp.exp2(mem - top)
        total = jnp.sum(doc, -1, keepdims=True) + jnp.sum(mem, -1, keepdims=True)
        share = 1.0 / total
        mixed = jnp.dot((doc * share).astype(bf16), values, preferred_element_type=f32)
        mixed = mixed + jnp.dot(
            (mem * share).astype(bf16), mem_values, preferred_element_type=f32
        )
        mixed = mixed.astype(bf16)
        for h in range(heads):
            out_ref[tokens, h * HD : (h + 1) * HD] = mixed[h * BLK : (h + 1) * BLK]


def attend_half(half, pick, query, q_doc, k_doc, kv, memories):
    rows, columns = query.shape
    slots = memories[0].shape
    span = k_doc.shape[1] + slots[1]
    return pl.pallas_call(
        functools.partial(attend_kernel, half),
        out_shape=jax.ShapeDtypeStruct(query.shape, bf16),
        grid_spec=pltpu.PrefetchScalarGridSpec(
            num_scalar_prefetch=1,
            grid=(1,),
            in_specs=[
                whole((rows, columns)),
                pl.BlockSpec((rows, HD), lambda i, s: (half, 0)),
                whole(k_doc.shape),
            ]
            + [whole(kv[0].shape)] * len(kv)
            + [whole(slots)] * len(memories),
            out_specs=whole((rows, columns)),
        ),
        compiler_params=params(40),
        cost_estimate=cost(
            4 * rows * columns * span, 4 * rows * columns, rows * columns // HD * span
        ),
        name="attend_half",
    )(pick, query, q_doc, k_doc, *kv, *memories)


def project(attended, w_out, target, width, added=(), kind=bf16):
    rows, depth = attended.shape
    tile = min(width, 512)
    steps = width // tile

    def body(target_ref, a_ref, w_ref, *refs):
        total = jnp.dot(a_ref[...], w_ref[...], preferred_element_type=f32)
        for ref in refs[:-1]:
            total = total + ref[...].astype(f32)
        refs[-1][...] = total.astype(kind)

    piece = pl.BlockSpec((rows, tile), lambda k, s: (0, k))
    return pl.pallas_call(
        body,
        out_shape=jax.ShapeDtypeStruct((rows, width), kind),
        grid_spec=pltpu.PrefetchScalarGridSpec(
            num_scalar_prefetch=1,
            grid=(steps,),
            in_specs=[
                whole((rows, depth)),
                pl.BlockSpec((depth, tile), lambda k, s: (0, s[0] * steps + k)),
            ]
            + [piece] * len(added),
            out_specs=piece,
        ),
        compiler_params=params(16),
        cost_estimate=cost(2 * rows * depth * width, 2 * depth * width),
        name="project",
    )(target[None], attended, w_out, *added)


def on_device(tokens, norm_gain, w_query, w_key, w_value, w_out, doc_ids, assign, res_len, res_mem):
    n_tensor = lax.axis_size("tensor")
    n_rows = lax.axis_size("rows")
    chips = n_tensor // 2
    tensor_index = lax.axis_index("tensor").astype(jnp.int32)
    row_index = lax.axis_index("rows").astype(jnp.int32)
    chip, core = tensor_index // 2, tensor_index % 2
    rows_dev, width = tokens.shape
    features = norm_gain.shape[0]
    kv_heads = w_key.shape[1] // HD
    sharers = n_tensor // kv_heads

    def to_core(x):
        return lax.ppermute(x, "tensor", [(i, i ^ 1) for i in range(n_tensor)])

    def to_chip(x, ahead):
        pairs = [(i, (i + 2 * ahead) % n_tensor) for i in range(n_tensor)]
        return lax.ppermute(x, "tensor", pairs)

    def up(x):
        return lax.ppermute(x, "rows", [(i, i + 1) for i in range(n_rows - 1)])

    def down(x):
        return lax.ppermute(x, "rows", [(i + 1, i) for i in range(n_rows - 1)])

    away = range(1, chips)

    *halves, stat = prep(tokens)
    chip_stats = [to_chip(stat, ahead) for ahead in away]
    stats = [stat, to_core(stat)] + chip_stats + [to_core(s) for s in chip_stats]
    sources = []
    for part in halves:
        arrived = [to_chip(part, ahead) for ahead in away]
        sources.append([part, to_core(part)] + arrived + [to_core(a) for a in arrived])
    order = [tensor_index, tensor_index ^ 1]
    order += [(tensor_index - 2 * ahead) % n_tensor for ahead in away]
    order += [((tensor_index ^ 1) - 2 * ahead) % n_tensor for ahead in away]
    order = jnp.stack(order).astype(jnp.int32)

    head_group = tensor_index // sharers
    memory = lax.dynamic_slice_in_dim(res_mem[0], head_group * HD, HD, 2)
    memories, rising, falling = [memory], memory, memory
    lifted, lowered = [], []
    for _ in range(n_rows - 1):
        rising, falling = up(rising), down(falling)
        lifted.append(rising)
        lowered.append(falling)
    memories = [memory] + lifted + lowered

    positions = (row_index * rows_dev + jnp.arange(rows_dev, dtype=jnp.int32)).astype(f32)
    half_dim = HD // 2
    frequency = rope_base ** (-(jnp.arange(half_dim, dtype=f32) / half_dim))
    angles = positions[:, None] * frequency[None, :]
    cosine, sine = jnp.cos(angles), jnp.sin(angles)
    cosine = jnp.concatenate([cosine, cosine], 1)
    sine = jnp.concatenate([-sine, sine], 1)

    targets = jnp.arange(chips, dtype=jnp.int32) * 2
    heads = jnp.concatenate([(targets + core) // sharers, (targets + 1 - core) // sharers])
    own, send = kv_partial(
        heads, stats, tokens, norm_gain, w_key, w_value, tensor_index, features, chips
    )
    arrived = to_core(send)
    others = []
    for ahead in away:
        target = (chip + ahead) % chips
        pair = lax.dynamic_index_in_dim(own, target, 0, False).astype(f32)
        pair = pair + lax.dynamic_index_in_dim(arrived, target, 0, False).astype(f32)
        others.append(to_chip(pair.astype(bf16), ahead))
    kv = [kv_final(own, arrived, others, cosine, sine, chip)]
    total_rows = n_rows * rows_dev
    longest = total_rows // 2
    back = -(-(longest - 1) // rows_dev)
    for _ in range(back):
        kv.insert(0, up(kv[0]))

    padded = jnp.concatenate([jnp.full((back * rows_dev,), -1, jnp.int32), doc_ids])
    k_doc = lax.dynamic_slice_in_dim(padded, row_index * rows_dev, (back + 1) * rows_dev)[None]
    q_doc = jnp.broadcast_to(k_doc[0, back * rows_dev :, None], (rows_dev, HD))
    blocks_dev = rows_dev // BLK
    servers = lax.dynamic_slice_in_dim(assign[:, 0], row_index * blocks_dev, blocks_dev)
    apart = row_index - servers
    slots = jnp.where(apart >= 0, apart, n_rows - 1 - apart).astype(jnp.int32)
    lives = res_len[servers].astype(jnp.int32)
    per_half = blocks_dev // HALVES

    outs = []
    for half in range(HALVES):
        query = query_half(half, order, stats, sources[half], norm_gain, w_query, cosine, sine)
        mine = slice(half * per_half, (half + 1) * per_half)
        pick = jnp.concatenate([slots[mine], lives[mine]])
        attended = attend_half(half, pick, query, q_doc, k_doc, kv, memories)
        arrived = []
        for ahead in away:
            far = ((chip + ahead) % chips) * 2
            other = to_core(project(attended, w_out, far + 1 - core, width))
            pair = project(attended, w_out, far + core, width, (other,))
            arrived.append(to_chip(pair, ahead))
        near = to_core(project(attended, w_out, tensor_index ^ 1, width))
        part = project(attended, w_out, tensor_index, width, (near,), f32)
        for piece in arrived:
            part = part + piece.astype(f32)
        outs.append(part.astype(bf16))
    return jnp.concatenate(outs, 0)


def solution(mesh):
    in_specs = (
        P(("groups", "rows"), "tensor"),
        P(),
        P(None, "tensor"),
        P("tensor", None),
        P("tensor", None),
        P("tensor", None),
        P("groups"),
        P("groups", None),
        P("groups"),
        P(("groups", "rows"), None, None, None),
    )
    out_specs = P(("groups", "rows"), "tensor")
    return jax.shard_map(
        on_device, mesh=mesh, in_specs=in_specs, out_specs=out_specs, check_vma=False
    )
```

time: 246 us -> 140 us (0.57)
  waiting for transfers between devices: 106 us -> 31.2 us
  matrix products: 46.9 us -> 0 us
  Pallas kernels: 0 us -> 43.1 us
  blocking collectives: 41.6 us -> 0 us
  starting transfers between devices: 4.65 us -> 34.8 us
  other arithmetic: 22.1 us -> 5.02 us
  local copies, waits for them, and re-layouts: 10.3 us -> 24.9 us
  between operations: 13.4 us -> 0.51 us
    dot_general x10 -> x0, matrix products: 46.9 us -> none  [the longest x1 12 us: on_device(): term = jnp.dot(attended, w_out, preferred_element_type=jnp.float32)]
    pallas_call x0 -> x15, Pallas kernels: none -> 43.1 us  [the longest x2 15.9 us: query_half(): pl.pallas_call(body, out_shape=jax.ShapeDtypeStruct((rows, columns), bf16...]
    reduce_scatter x1 -> x0, waiting for transfers between devices: 42.8 us -> none  [on_device(): lax.psum_scatter(term.astype(jnp.bfloat16), 'tensor', scatter_dimension=1...]
    ppermute x0 -> x25, starting transfers between devices: none -> 34.8 us  [the longest x5 21.4 us: up(): return lax.ppermute(x, 'rows', [(i, i + 1) for i in range(n_rows - 1)])]
    all_gather x1 -> x0, waiting for transfers between devices: 32.1 us -> none  [on_device(): whole = lax.all_gather(tokens, 'tensor', axis=1, tiled=True)]
    ppermute x0 -> x25, waiting for transfers between devices: none -> 31.2 us  [the longest x6 28.3 us: to_chip(): return lax.ppermute(x, 'tensor', pairs)]
    psum x1 -> x0, waiting for transfers between devices: 30.8 us -> none  [on_device(): lax.psum(jnp.dot(own_features, w_value, preferred_element_type=jnp.float3...]
    all_to_all x1 -> x0, blocking collectives: 26.5 us -> none  [on_device(): lax.all_to_all(results.reshape(n_rows, CAP, BLK, query_width), 'rows', sp...]
  transfers between devices with their start and end apart: 4 -> 25, of which waited for: 3 -> 5; matrix products, arithmetic and copies ran while one was open for 7% -> 4% of each run, Pallas kernels for 0% -> 30%
where the time goes in v1:
time: 140 us
  Pallas kernels  43.1 us (31%)
  starting transfers between devices  34.8 us (25%)
  waiting for transfers between devices  31.2 us (22%)
  local copies, waits for them, and re-layouts  24.9 us (18%)
  other arithmetic  5.02 us (4%)
    ppermute x6, waiting for transfers between devices, to_chip(): return lax.ppermute(x, 'tensor', pairs)  28.3 us
    unnamed x36, local copies, waits for them, and re-layouts  23.2 us
    ppermute x5, starting transfers between devices, up(): return lax.ppermute(x, 'rows', [(i, i + 1) for i in range(n_rows - 1)])  21.4 us
    pallas_call x2, Pallas kernels, query_half(): pl.pallas_call(body, out_shape=jax.ShapeDtypeStruct((rows, columns), bf16...  15.9 us
    pallas_call x8, Pallas kernels, project(): pl.pallas_call(body, out_shape=jax.ShapeDtypeStruct((rows, width), kind),...  15.3 us
    ppermute x6, starting transfers between devices, to_chip(): return lax.ppermute(x, 'tensor', pairs)  7.26 us
    pallas_call x2, Pallas kernels, attend_half(): pl.pallas_call(functools.partial(attend_kernel, half), out_shape=jax.Shap...  6.96 us
    ppermute x3, starting transfers between devices, down(): return lax.ppermute(x, 'rows', [(i + 1, i) for i in range(n_rows - 1)])  3.86 us
  transfers between devices with their start and end apart: 25, of which 5 were waited for; matrix products, arithmetic and copies ran while one was open for 4% of the time, Pallas kernels for 30%

profile of v1, /device:TPU:0, one launch (start us, length us, event | category | flops | bytes accessed | tf_op | source)
XLA Modules:
  0.0 139.6 jit_solution(18394263723584818457)
XLA Ops:
  0.0 1.3 copy-done.4
  3.2 3.0 %collective-permute-start.1 = (f32[8,256]{1,0:T(8,128)S(1)}, f32[8,256]{1,0:T(8,128)S(1)}, u32[]{:S(2)}, u32[]{:S(2)}) collective-permute-start(f32[8,256]{1,0:T(8,128)S(1)} %get-tuple-element.10.refs_0_), channel_id=1, source_target_pairs={{0,8},{4,12},{8,0},{12,4},{1,9},{5,13},{9,1},{13,5},{2,10},{6,14},... | collective-permute-start | bytes 24584 | tf_op jit(solution)/shard_map/ppermute | solution.py:366
  6.7 3.7 %collective-permute-start.10 = (bf16[2,512,128]{2,1,0:T(8,128)(2,1)S(1)}, bf16[2,512,128]{2,1,0:T(8,128)(2,1)S(1)}, u32[]{:S(2)}, u32[]{:S(2)}) collective-permute-start(bf16[2,512,128]{2,1,0:T(8,128)(2,1)S(1)} %dynamic-slice_bitcast_fusion.refs_3_), channel_id=1, source_target_pairs={{0,1},{1,2},{2,3},{4,5},{5,6},{6,7},{8,9},{9,10},{10,11},{12,13},{... | collective-permute-start | bytes 786440 | tf_op jit(solution)/shard_map/ppermute | solution.py:369
  10.5 1.3 fusion.1
  14.7 1.6 %copy-done.6 = bf16[2048,512]{1,0:T(8,128)(2,1)S(1)} copy-done((bf16[2048,512]{1,0:T(8,128)(2,1)S(1)}, bf16[2048,512]{1,0:T(8,128)(2,1)}, u32[]{:S(2)}) %copy-start.6) | copy-done | bytes 2097176
  16.3 1.6 %copy-done.7 = bf16[2048,512]{1,0:T(8,128)(2,1)S(1)} copy-done((bf16[2048,512]{1,0:T(8,128)(2,1)S(1)}, bf16[2048,512]{1,0:T(8,128)(2,1)}, u32[]{:S(2)}) %copy-start.7) | copy-done | bytes 2097176
  17.9 3.8 %kv_partial.1 = (bf16[2,256,256]{2,1,0:T(8,128)(2,1)S(1)}, bf16[2,256,256]{2,1,0:T(8,128)(2,1)}) custom-call(s32[5]{0:T(128)S(1)} %pad_add_fusion.2.scalars, f32[8,256]{1,0:T(8,128)S(1)} %get-tuple-element.10.refs_0_, f32[8,256]{1,0:T(8,128)S(1)} %collective-permute-done.refs_1_, f32[8,256]{1,0:T(8,128)S(1)} %collective-permute-done.1.refs_2_, ...), custom_call_target="tpu_custom_call" | custom-call | flops 1073741824 | bytes 5242880 | tf_op jit(solution)/shard_map/kv_partial/pallas_call | solution.py:111
  23.5 1.5 %collective-permute-start.20 = (bf16[128,2048]{1,0:T(8,128)(2,1)}, bf16[128,2048]{1,0:T(8,128)(2,1)}, u32[]{:S(2)}, u32[]{:S(2)}) collective-permute-start(bf16[128,2048]{1,0:T(8,128)(2,1)} %copy-done.8), channel_id=1, source_target_pairs={{0,8},{4,12},{8,0},{12,4},{1,9},{5,13},{9,1},{13,5},{2,10},{6,14},... | collective-permute-start | bytes 1572872 | tf_op jit(solution)/shard_map/ppermute | solution.py:366
  25.8 4.4 %collective-permute-start.11 = (bf16[2,512,128]{2,1,0:T(8,128)(2,1)S(1)}, bf16[2,512,128]{2,1,0:T(8,128)(2,1)S(1)}, u32[]{:S(2)}, u32[]{:S(2)}) collective-permute-start(bf16[2,512,128]{2,1,0:T(8,128)(2,1)S(1)} %collective-permute-done.10.refs_4_), channel_id=1, source_target_pairs={{0,1},{1,2},{2,3},{4,5},{5,6},{6,7},{8,9},{9,10},{10,11},{12,13},{... | collective-permute-start | bytes 786440 | tf_op jit(solution)/shard_map/ppermute | solution.py:369
  30.2 10.6 %collective-permute-done.7.refs_0_ = bf16[256,256]{1,0:T(8,128)(2,1)S(1)} collective-permute-done((bf16[256,256]{1,0:T(8,128)(2,1)S(1)}, bf16[256,256]{1,0:T(8,128)(2,1)S(1)}, u32[]{:S(2)}, u32[]{:S(2)}) %collective-permute-start.7) | collective-permute-done | bytes 131104 | tf_op jit(solution)/shard_map/ppermute | solution.py:366
  43.4 4.9 %collective-permute-start.8 = (bf16[256,256]{1,0:T(8,128)(2,1)S(1)}, bf16[256,256]{1,0:T(8,128)(2,1)S(1)}, u32[]{:S(2)}, u32[]{:S(2)}) collective-permute-start(bf16[256,256]{1,0:T(8,128)(2,1)S(1)} %kv_final.1.refs_2_), channel_id=1, source_target_pairs={{0,1},{1,2},{2,3},{4,5},{5,6},{6,7},{8,9},{9,10},{10,11},{12,13},{... | collective-permute-start | bytes 393224 | tf_op jit(solution)/shard_map/ppermute | solution.py:369
  48.6 2.3 %collective-permute-done.14.refs_8_ = bf16[2,512,128]{2,1,0:T(8,128)(2,1)S(1)} collective-permute-done((bf16[2,512,128]{2,1,0:T(8,128)(2,1)S(1)}, bf16[2,512,128]{2,1,0:T(8,128)(2,1)S(1)}, u32[]{:S(2)}, u32[]{:S(2)}) %collective-permute-start.14) | collective-permute-done | bytes 262176 | tf_op jit(solution)/shard_map/ppermute | solution.py:372
  50.9 3.6 %collective-permute-start.12 = (bf16[2,512,128]{2,1,0:T(8,128)(2,1)S(1)}, bf16[2,512,128]{2,1,0:T(8,128)(2,1)S(1)}, u32[]{:S(2)}, u32[]{:S(2)}) collective-permute-start(bf16[2,512,128]{2,1,0:T(8,128)(2,1)S(1)} %collective-permute-done.11.refs_5_), channel_id=1, source_target_pairs={{0,1},{1,2},{2,3},{4,5},{5,6},{6,7},{8,9},{9,10},{10,11},{12,13},{... | collective-permute-start | bytes 786440 | tf_op jit(solution)/shard_map/ppermute | solution.py:369
  56.0 4.7 %collective-permute-start.9 = (bf16[256,256]{1,0:T(8,128)(2,1)S(1)}, bf16[256,256]{1,0:T(8,128)(2,1)S(1)}, u32[]{:S(2)}, u32[]{:S(2)}) collective-permute-start(bf16[256,256]{1,0:T(8,128)(2,1)S(1)} %collective-permute-done.8.refs_1_), channel_id=1, source_target_pairs={{0,1},{1,2},{2,3},{4,5},{5,6},{6,7},{8,9},{9,10},{10,11},{12,13},{... | collective-permute-start | bytes 393224 | tf_op jit(solution)/shard_map/ppermute | solution.py:369
  60.7 5.8 %copy-done.2 = bf16[8192,1024]{1,0:T(8,128)(2,1)S(1)} copy-done((bf16[8192,1024]{1,0:T(8,128)(2,1)S(1)}, bf16[8192,1024]{1,0:T(8,128)(2,1)}, u32[]{:S(2)}) %copy-start.2) | copy-done | bytes 16777240
  66.5 7.8 %query_half.2.q_ref = bf16[128,1024]{1,0:T(8,128)(2,1)S(1)} custom-call(s32[4]{0:T(128)S(1)} %pad_add_fusion.1.order_ref, f32[8,256]{1,0:T(8,128)S(1)} %get-tuple-element.10.refs_0_, f32[8,256]{1,0:T(8,128)S(1)} %collective-permute-done.refs_1_, f32[8,256]{1,0:T(8,128)S(1)} %collective-permute-done.1.refs_2_, f32[8,256]{1,0:T(8,128)S(1)} %collective-permute-done.2.refs_3_, ...), custom_call_target="tpu_custom_call" | custom-call | flops 2147483648 | bytes 16777216 | tf_op jit(solution)/shard_map/query_half/pallas_call | solution.py:214
  74.4 3.5 %attend_half.2.a_ref = bf16[128,1024]{1,0:T(8,128)(2,1)S(1)} custom-call(s32[4]{0:T(128)S(1)} %pad_add_fusion.pick_ref, bf16[128,1024]{1,0:T(8,128)(2,1)S(1)} %query_half.2.q_ref, s32[256,128]{1,0:T(8,128)S(1)} %broadcast_in_dim.17.qdoc_ref, s32[1,768]{1,0:T(1,128)S(1)} %broadcast_in_dim.15.kdoc_ref, bf16[256,256]{1,0:T(8,128)(2,1)S(1)} %collective-permute-done.9.refs_0_, ...), custom_call_target="tpu_custom_call" | custom-call | flops 671088640 | bytes 524288 | tf_op jit(solution)/shard_map/attend_half/pallas_call | solution.py:295
  77.9 5.8 %copy-done.1 = bf16[1024,8192]{1,0:T(8,128)(2,1)S(1)} copy-done((bf16[1024,8192]{1,0:T(8,128)(2,1)S(1)}, bf16[1024,8192]{1,0:T(8,128)(2,1)}, u32[]{:S(2)}) %copy-start.1) | copy-done | bytes 16777240
  83.7 1.7 %project.10 = bf16[128,2048]{1,0:T(8,128)(2,1)S(1)} custom-call(s32[1]{0:T(128)} %bitcast.11.target_ref, bf16[128,1024]{1,0:T(8,128)(2,1)S(1)} %attend_half.2.a_ref, bf16[1024,8192]{1,0:T(8,128)(2,1)S(1)} %copy-done.1), custom_call_target="tpu_custom_call" | custom-call | flops 536870912 | bytes 4194304 | tf_op jit(solution)/shard_map/project/pallas_call | solution.py:330
  85.8 6.3 %copy-done.3 = bf16[8192,1024]{1,0:T(8,128)(2,1)S(1)} copy-done((bf16[8192,1024]{1,0:T(8,128)(2,1)S(1)}, bf16[8192,1024]{1,0:T(8,128)(2,1)}, u32[]{:S(2)}) %copy-start.3) | copy-done | bytes 16777240
  92.1 8.1 %query_half.3.q_ref = bf16[128,1024]{1,0:T(8,128)(2,1)S(1)} custom-call(s32[4]{0:T(128)S(1)} %pad_add_fusion.1.order_ref, f32[8,256]{1,0:T(8,128)S(1)} %get-tuple-element.10.refs_0_, f32[8,256]{1,0:T(8,128)S(1)} %collective-permute-done.refs_1_, f32[8,256]{1,0:T(8,128)S(1)} %collective-permute-done.1.refs_2_, f32[8,256]{1,0:T(8,128)S(1)} %collective-permute-done.2.refs_3_, ...), custom_call_target="tpu_custom_call" | custom-call | flops 2147483648 | bytes 16777216 | tf_op jit(solution)/shard_map/query_half/pallas_call | solution.py:214
  100.2 3.5 %attend_half.3.a_ref = bf16[128,1024]{1,0:T(8,128)(2,1)S(1)} custom-call(s32[4]{0:T(128)S(1)} %pad_add_fusion.3.pick_ref, bf16[128,1024]{1,0:T(8,128)(2,1)S(1)} %query_half.3.q_ref, s32[256,128]{1,0:T(8,128)S(1)} %broadcast_in_dim.17.qdoc_ref, s32[1,768]{1,0:T(1,128)S(1)} %broadcast_in_dim.15.kdoc_ref, bf16[256,256]{1,0:T(8,128)(2,1)S(1)} %collective-permute-done.9.refs_0_, ...), custom_call_target="tpu_custom_call" | custom-call | flops 671088640 | bytes 524288 | tf_op jit(solution)/shard_map/attend_half/pallas_call | solution.py:295
  103.8 1.7 %project.14 = bf16[128,2048]{1,0:T(8,128)(2,1)S(1)} custom-call(s32[1]{0:T(128)} %bitcast.11.target_ref, bf16[128,1024]{1,0:T(8,128)(2,1)S(1)} %attend_half.3.a_ref, bf16[1024,8192]{1,0:T(8,128)(2,1)S(1)} %bitcast.17), custom_call_target="tpu_custom_call" | custom-call | flops 536870912 | bytes 4194304 | tf_op jit(solution)/shard_map/project/pallas_call | solution.py:330
  105.8 1.7 %project.8 = bf16[128,2048]{1,0:T(8,128)(2,1)S(1)} custom-call(s32[1]{0:T(128)} %bitcast.3.target_ref, bf16[128,1024]{1,0:T(8,128)(2,1)S(1)} %attend_half.2.a_ref, bf16[1024,8192]{1,0:T(8,128)(2,1)S(1)} %bitcast.17), custom_call_target="tpu_custom_call" | custom-call | flops 536870912 | bytes 4194304 | tf_op jit(solution)/shard_map/project/pallas_call | solution.py:330
  107.9 1.7 %project.12 = bf16[128,2048]{1,0:T(8,128)(2,1)S(1)} custom-call(s32[1]{0:T(128)} %bitcast.3.target_ref, bf16[128,1024]{1,0:T(8,128)(2,1)S(1)} %attend_half.3.a_ref, bf16[1024,8192]{1,0:T(8,128)(2,1)S(1)} %bitcast.17), custom_call_target="tpu_custom_call" | custom-call | flops 536870912 | bytes 4194304 | tf_op jit(solution)/shard_map/project/pallas_call | solution.py:330
  109.9 3.1 %project.11 = bf16[128,2048]{1,0:T(8,128)(2,1)S(1)} custom-call(s32[1]{0:T(128)} %bitcast.10.target_ref, bf16[128,1024]{1,0:T(8,128)(2,1)S(1)} %attend_half.2.a_ref, bf16[1024,8192]{1,0:T(8,128)(2,1)S(1)} %bitcast.17, bf16[128,2048]{1,0:T(8,128)(2,1)} %collective-permute-done.17.refs_0_), custom_call_target="tpu_custom_call" | custom-call | flops 536870912 | bytes 4194304 | tf_op jit(solution)/shard_map/project/pallas_call | solution.py:330
  113.0 1.6 %collective-permute-start.18 = (bf16[128,2048]{1,0:T(8,128)(2,1)S(1)}, bf16[128,2048]{1,0:T(8,128)(2,1)S(1)}, u32[]{:S(2)}, u32[]{:S(2)}) collective-permute-start(bf16[128,2048]{1,0:T(8,128)(2,1)S(1)} %project.11), channel_id=1, source_target_pairs={{0,8},{4,12},{8,0},{12,4},{1,9},{5,13},{9,1},{13,5},{2,10},{6,14},... | collective-permute-start | bytes 1572872 | tf_op jit(solution)/shard_map/ppermute | solution.py:366
  114.6 1.7 %project.15 = bf16[128,2048]{1,0:T(8,128)(2,1)S(1)} custom-call(s32[1]{0:T(128)} %bitcast.10.target_ref, bf16[128,1024]{1,0:T(8,128)(2,1)S(1)} %attend_half.3.a_ref, bf16[1024,8192]{1,0:T(8,128)(2,1)S(1)} %bitcast.17, bf16[128,2048]{1,0:T(8,128)(2,1)S(1)} %collective-permute-done.23.refs_0_), custom_call_target="tpu_custom_call" | custom-call | flops 536870912 | bytes 4194304 | tf_op jit(solution)/shard_map/project/pallas_call | solution.py:330
  116.9 1.8 %project.9 = f32[128,2048]{1,0:T(8,128)S(1)} custom-call(s32[1]{0:T(128)} %bitcast.target_ref, bf16[128,1024]{1,0:T(8,128)(2,1)S(1)} %attend_half.2.a_ref, bf16[1024,8192]{1,0:T(8,128)(2,1)S(1)} %bitcast.17, bf16[128,2048]{1,0:T(8,128)(2,1)S(1)} %collective-permute-done.16.refs_0_), custom_call_target="tpu_custom_call" | custom-call | flops 536870912 | bytes 4194304 | tf_op jit(solution)/shard_map/project/pallas_call | solution.py:330
  118.7 1.8 %project.13 = f32[128,2048]{1,0:T(8,128)S(1)} custom-call(s32[1]{0:T(128)} %bitcast.target_ref, bf16[128,1024]{1,0:T(8,128)(2,1)S(1)} %attend_half.3.a_ref, bf16[1024,8192]{1,0:T(8,128)(2,1)S(1)} %bitcast.17, bf16[128,2048]{1,0:T(8,128)(2,1)S(1)} %collective-permute-done.22.refs_0_), custom_call_target="tpu_custom_call" | custom-call | flops 536870912 | bytes 4194304 | tf_op jit(solution)/shard_map/project/pallas_call | solution.py:330
  120.5 7.3 %collective-permute-done.18 = bf16[128,2048]{1,0:T(8,128)(2,1)S(1)} collective-permute-done((bf16[128,2048]{1,0:T(8,128)(2,1)S(1)}, bf16[128,2048]{1,0:T(8,128)(2,1)S(1)}, u32[]{:S(2)}, u32[]{:S(2)}) %collective-permute-start.18) | collective-permute-done | bytes 524320 | tf_op jit(solution)/shard_map/ppermute | solution.py:366
  127.9 10.5 %collective-permute-done.24 = bf16[128,2048]{1,0:T(8,128)(2,1)S(1)} collective-permute-done((bf16[128,2048]{1,0:T(8,128)(2,1)S(1)}, bf16[128,2048]{1,0:T(8,128)(2,1)S(1)}, u32[]{:S(2)}, u32[]{:S(2)}) %collective-permute-start.24) | collective-permute-done | bytes 524320 | tf_op jit(solution)/shard_map/ppermute | solution.py:366
  (96 shorter events, 15.5 us)
Async XLA Ops:
  1.3 13.4 %copy-start.5 = (bf16[256,2048]{1,0:T(8,128)(2,1)S(1)}, bf16[256,2048]{1,0:T(8,128)(2,1)}, u32[]{:S(2)}) copy-start(bf16[256,2048]{1,0:T(8,128)(2,1)} %refs_4_.1) | copy-start | bytes 3145732
  3.2 9.3 %collective-permute-start.1 = (f32[8,256]{1,0:T(8,128)S(1)}, f32[8,256]{1,0:T(8,128)S(1)}, u32[]{:S(2)}, u32[]{:S(2)}) collective-permute-start(f32[8,256]{1,0:T(8,128)S(1)} %get-tuple-element.10.refs_0_), channel_id=1, source_target_pairs={{0,8},{4,12},{8,0},{12,4},{1,9},{5,13},{9,1},{13,5},{2,10},{6,14},... | collective-permute-start | bytes 24584 | tf_op jit(solution)/shard_map/ppermute | solution.py:366
  6.1 7.2 %collective-permute-start = (f32[8,256]{1,0:T(8,128)S(1)}, f32[8,256]{1,0:T(8,128)S(1)}, u32[]{:S(2)}, u32[]{:S(2)}) collective-permute-start(f32[8,256]{1,0:T(8,128)S(1)} %get-tuple-element.10.refs_0_), channel_id=1, source_target_pairs={{0,4},{4,0},{8,12},{12,8},{1,5},{5,1},{9,13},{13,9},{2,6},{6,2},{1... | collective-permute-start | bytes 24584 | tf_op jit(solution)/shard_map/ppermute | solution.py:362
  6.1 19.6 %collective-permute-start.4 = (bf16[128,2048]{1,0:T(8,128)(2,1)}, bf16[128,2048]{1,0:T(8,128)(2,1)}, u32[]{:S(2)}, u32[]{:S(2)}) collective-permute-start(bf16[128,2048]{1,0:T(8,128)(2,1)} %get-tuple-element.11.refs_4_), channel_id=1, source_target_pairs={{0,8},{4,12},{8,0},{12,4},{1,9},{5,13},{9,1},{13,5},{2,10},{6,14},... | collective-permute-start | bytes 1572872 | tf_op jit(solution)/shard_map/ppermute | solution.py:366
  6.2 37.2 %collective-permute-start.3 = (bf16[128,2048]{1,0:T(8,128)(2,1)}, bf16[128,2048]{1,0:T(8,128)(2,1)}, u32[]{:S(2)}, u32[]{:S(2)}) collective-permute-start(bf16[128,2048]{1,0:T(8,128)(2,1)} %get-tuple-element.11.refs_4_), channel_id=1, source_target_pairs={{0,4},{4,0},{8,12},{12,8},{1,5},{5,1},{9,13},{13,9},{2,6},{6,2},{1... | collective-permute-start | bytes 1572872 | tf_op jit(solution)/shard_map/ppermute | solution.py:362
  6.7 18.4 %collective-permute-start.10 = (bf16[2,512,128]{2,1,0:T(8,128)(2,1)S(1)}, bf16[2,512,128]{2,1,0:T(8,128)(2,1)S(1)}, u32[]{:S(2)}, u32[]{:S(2)}) collective-permute-start(bf16[2,512,128]{2,1,0:T(8,128)(2,1)S(1)} %dynamic-slice_bitcast_fusion.refs_3_), channel_id=1, source_target_pairs={{0,1},{1,2},{2,3},{4,5},{5,6},{6,7},{8,9},{9,10},{10,11},{12,13},{... | collective-permute-start | bytes 786440 | tf_op jit(solution)/shard_map/ppermute | solution.py:369
  12.5 2.2 %collective-permute-start.2 = (f32[8,256]{1,0:T(8,128)S(1)}, f32[8,256]{1,0:T(8,128)S(1)}, u32[]{:S(2)}, u32[]{:S(2)}) collective-permute-start(f32[8,256]{1,0:T(8,128)S(1)} %collective-permute-done.1.refs_2_), channel_id=1, source_target_pairs={{0,4},{4,0},{8,12},{12,8},{1,5},{5,1},{9,13},{13,9},{2,6},{6,2},{1... | collective-permute-start | bytes 24584 | tf_op jit(solution)/shard_map/ppermute | solution.py:362
  13.4 12.4 %collective-permute-start.13 = (bf16[2,512,128]{2,1,0:T(8,128)(2,1)S(1)}, bf16[2,512,128]{2,1,0:T(8,128)(2,1)S(1)}, u32[]{:S(2)}, u32[]{:S(2)}) collective-permute-start(bf16[2,512,128]{2,1,0:T(8,128)(2,1)S(1)} %dynamic-slice_bitcast_fusion.refs_3_), channel_id=1, source_target_pairs={{1,0},{2,1},{3,2},{5,4},{6,5},{7,6},{9,8},{10,9},{11,10},{13,12},{... | collective-permute-start | bytes 786440 | tf_op jit(solution)/shard_map/ppermute | solution.py:372
  21.7 26.7 %copy-start.12 = (s32[1024]{0:T(1024)S(1)}, s32[1024]{0:T(1024)}, u32[]{:S(2)}) copy-start(s32[1024]{0:T(1024)} %param.16) | copy-start | bytes 12292
  21.7 26.8 %copy-start.11 = (bf16[8192]{0:T(1024)(128)(2,1)S(1)}, bf16[8192]{0:T(1024)(128)(2,1)}, u32[]{:S(2)}) copy-start(bf16[8192]{0:T(1024)(128)(2,1)} %param.11) | copy-start | bytes 49156
  21.7 1.9 %collective-permute-start.6 = (bf16[2,256,256]{2,1,0:T(8,128)(2,1)}, bf16[2,256,256]{2,1,0:T(8,128)(2,1)S(1)}, u32[]{:S(2)}, u32[]{:S(2)}) collective-permute-start(bf16[2,256,256]{2,1,0:T(8,128)(2,1)} %get-tuple-element.13), channel_id=1, source_target_pairs={{0,4},{4,0},{8,12},{12,8},{1,5},{5,1},{9,13},{13,9},{2,6},{6,2},{1... | collective-permute-start | bytes 786440 | tf_op jit(solution)/shard_map/ppermute | solution.py:362
  23.5 31.0 %collective-permute-start.20 = (bf16[128,2048]{1,0:T(8,128)(2,1)}, bf16[128,2048]{1,0:T(8,128)(2,1)}, u32[]{:S(2)}, u32[]{:S(2)}) collective-permute-start(bf16[128,2048]{1,0:T(8,128)(2,1)} %copy-done.8), channel_id=1, source_target_pairs={{0,8},{4,12},{8,0},{12,4},{1,9},{5,13},{9,1},{13,5},{2,10},{6,14},... | collective-permute-start | bytes 1572872 | tf_op jit(solution)/shard_map/ppermute | solution.py:366
  25.1 15.6 %collective-permute-start.7 = (bf16[256,256]{1,0:T(8,128)(2,1)S(1)}, bf16[256,256]{1,0:T(8,128)(2,1)S(1)}, u32[]{:S(2)}, u32[]{:S(2)}) collective-permute-start(bf16[256,256]{1,0:T(8,128)(2,1)S(1)} %fusion), channel_id=1, source_target_pairs={{0,8},{4,12},{8,0},{12,4},{1,9},{5,13},{9,1},{13,5},{2,10},{6,14},... | collective-permute-start | bytes 393224 | tf_op jit(solution)/shard_map/ppermute | solution.py:366
  25.7 30.3 %collective-permute-start.5 = (bf16[128,2048]{1,0:T(8,128)(2,1)}, bf16[128,2048]{1,0:T(8,128)(2,1)}, u32[]{:S(2)}, u32[]{:S(2)}) collective-permute-start(bf16[128,2048]{1,0:T(8,128)(2,1)} %collective-permute-done.4.refs_6_), channel_id=1, source_target_pairs={{0,4},{4,0},{8,12},{12,8},{1,5},{5,1},{9,13},{13,9},{2,6},{6,2},{1... | collective-permute-start | bytes 1572872 | tf_op jit(solution)/shard_map/ppermute | solution.py:362
  25.8 22.8 %collective-permute-start.11 = (bf16[2,512,128]{2,1,0:T(8,128)(2,1)S(1)}, bf16[2,512,128]{2,1,0:T(8,128)(2,1)S(1)}, u32[]{:S(2)}, u32[]{:S(2)}) collective-permute-start(bf16[2,512,128]{2,1,0:T(8,128)(2,1)S(1)} %collective-permute-done.10.refs_4_), channel_id=1, source_target_pairs={{0,1},{1,2},{2,3},{4,5},{5,6},{6,7},{8,9},{9,10},{10,11},{12,13},{... | collective-permute-start | bytes 786440 | tf_op jit(solution)/shard_map/ppermute | solution.py:369
  40.8 10.1 %collective-permute-start.14 = (bf16[2,512,128]{2,1,0:T(8,128)(2,1)S(1)}, bf16[2,512,128]{2,1,0:T(8,128)(2,1)S(1)}, u32[]{:S(2)}, u32[]{:S(2)}) collective-permute-start(bf16[2,512,128]{2,1,0:T(8,128)(2,1)S(1)} %collective-permute-done.13.refs_7_), channel_id=1, source_target_pairs={{1,0},{2,1},{3,2},{5,4},{6,5},{7,6},{9,8},{10,9},{11,10},{13,12},{... | collective-permute-start | bytes 786440 | tf_op jit(solution)/shard_map/ppermute | solution.py:372
  43.4 12.4 %collective-permute-start.8 = (bf16[256,256]{1,0:T(8,128)(2,1)S(1)}, bf16[256,256]{1,0:T(8,128)(2,1)S(1)}, u32[]{:S(2)}, u32[]{:S(2)}) collective-permute-start(bf16[256,256]{1,0:T(8,128)(2,1)S(1)} %kv_final.1.refs_2_), channel_id=1, source_target_pairs={{0,1},{1,2},{2,3},{4,5},{5,6},{6,7},{8,9},{9,10},{10,11},{12,13},{... | collective-permute-start | bytes 393224 | tf_op jit(solution)/shard_map/ppermute | solution.py:369
  48.6 37.2 %collective-permute-start.19 = (bf16[128,2048]{1,0:T(8,128)(2,1)}, bf16[128,2048]{1,0:T(8,128)(2,1)S(1)}, u32[]{:S(2)}, u32[]{:S(2)}) collective-permute-start(bf16[128,2048]{1,0:T(8,128)(2,1)} %copy-done.8), channel_id=1, source_target_pairs={{0,4},{4,0},{8,12},{12,8},{1,5},{5,1},{9,13},{13,9},{2,6},{6,2},{1... | collective-permute-start | bytes 1572872 | tf_op jit(solution)/shard_map/ppermute | solution.py:362
  50.9 23.4 %collective-permute-start.12 = (bf16[2,512,128]{2,1,0:T(8,128)(2,1)S(1)}, bf16[2,512,128]{2,1,0:T(8,128)(2,1)S(1)}, u32[]{:S(2)}, u32[]{:S(2)}) collective-permute-start(bf16[2,512,128]{2,1,0:T(8,128)(2,1)S(1)} %collective-permute-done.11.refs_5_), channel_id=1, source_target_pairs={{0,1},{1,2},{2,3},{4,5},{5,6},{6,7},{8,9},{9,10},{10,11},{12,13},{... | collective-permute-start | bytes 786440 | tf_op jit(solution)/shard_map/ppermute | solution.py:369
  54.5 19.8 %collective-permute-start.15 = (bf16[2,512,128]{2,1,0:T(8,128)(2,1)S(1)}, bf16[2,512,128]{2,1,0:T(8,128)(2,1)S(1)}, u32[]{:S(2)}, u32[]{:S(2)}) collective-permute-start(bf16[2,512,128]{2,1,0:T(8,128)(2,1)S(1)} %collective-permute-done.14.refs_8_), channel_id=1, source_target_pairs={{1,0},{2,1},{3,2},{5,4},{6,5},{7,6},{9,8},{10,9},{11,10},{13,12},{... | collective-permute-start | bytes 786440 | tf_op jit(solution)/shard_map/ppermute | solution.py:372
  55.8 29.9 %collective-permute-start.21 = (bf16[128,2048]{1,0:T(8,128)(2,1)}, bf16[128,2048]{1,0:T(8,128)(2,1)}, u32[]{:S(2)}, u32[]{:S(2)}) collective-permute-start(bf16[128,2048]{1,0:T(8,128)(2,1)} %collective-permute-done.20.refs_6_), channel_id=1, source_target_pairs={{0,4},{4,0},{8,12},{12,8},{1,5},{5,1},{9,13},{13,9},{2,6},{6,2},{1... | collective-permute-start | bytes 1572872 | tf_op jit(solution)/shard_map/ppermute | solution.py:362
  56.0 18.3 %collective-permute-start.9 = (bf16[256,256]{1,0:T(8,128)(2,1)S(1)}, bf16[256,256]{1,0:T(8,128)(2,1)S(1)}, u32[]{:S(2)}, u32[]{:S(2)}) collective-permute-start(bf16[256,256]{1,0:T(8,128)(2,1)S(1)} %collective-permute-done.8.refs_1_), channel_id=1, source_target_pairs={{0,1},{1,2},{2,3},{4,5},{5,6},{6,7},{8,9},{9,10},{10,11},{12,13},{... | collective-permute-start | bytes 393224 | tf_op jit(solution)/shard_map/ppermute | solution.py:369
  83.7 20.1 %slice-start = ((s8[16777216]{0:T(1024)(128)(4,1)}), s8[4194304]{0:T(1024)(128)(4,1)S(1)}, s32[]{:S(2)}) async-start(s8[16777216]{0:T(1024)(128)(4,1)} %bitcast.16), calls=%async_computation | async-start | bytes 8388608
  83.7 20.1 %slice-start.1 = ((s8[16777216]{0:T(1024)(128)(4,1)}), s8[4194304]{0:T(1024)(128)(4,1)S(1)}, s32[]{:S(2)}) async-start(s8[16777216]{0:T(1024)(128)(4,1)} %bitcast.16), calls=%async_computation.1 | async-start | bytes 8388608
  85.4 24.5 %collective-permute-start.17 = (bf16[128,2048]{1,0:T(8,128)(2,1)S(1)}, bf16[128,2048]{1,0:T(8,128)(2,1)}, u32[]{:S(2)}, u32[]{:S(2)}) collective-permute-start(bf16[128,2048]{1,0:T(8,128)(2,1)S(1)} %project.10), channel_id=1, source_target_pairs={{0,4},{4,0},{8,12},{12,8},{1,5},{5,1},{9,13},{13,9},{2,6},{6,2},{1... | collective-permute-start | bytes 1572872 | tf_op jit(solution)/shard_map/ppermute | solution.py:362
  85.8 18.0 %slice-start.2 = ((s8[16777216]{0:T(1024)(128)(4,1)}), s8[4194304]{0:T(1024)(128)(4,1)S(1)}, s32[]{:S(2)}) async-start(s8[16777216]{0:T(1024)(128)(4,1)} %bitcast.16), calls=%async_computation.2 | async-start | bytes 8388608
  85.8 18.0 %slice-start.3 = ((s8[16777216]{0:T(1024)(128)(4,1)}), s8[4194304]{0:T(1024)(128)(4,1)S(1)}, s32[]{:S(2)}) async-start(s8[16777216]{0:T(1024)(128)(4,1)} %bitcast.16), calls=%async_computation.3 | async-start | bytes 8388608
  105.5 9.0 %collective-permute-start.23 = (bf16[128,2048]{1,0:T(8,128)(2,1)S(1)}, bf16[128,2048]{1,0:T(8,128)(2,1)S(1)}, u32[]{:S(2)}, u32[]{:S(2)}) collective-permute-start(bf16[128,2048]{1,0:T(8,128)(2,1)S(1)} %project.14), channel_id=1, source_target_pairs={{0,4},{4,0},{8,12},{12,8},{1,5},{5,1},{9,13},{13,9},{2,6},{6,2},{1... | collective-permute-start | bytes 1572872 | tf_op jit(solution)/shard_map/ppermute | solution.py:362
  107.5 9.4 %collective-permute-start.16 = (bf16[128,2048]{1,0:T(8,128)(2,1)S(1)}, bf16[128,2048]{1,0:T(8,128)(2,1)S(1)}, u32[]{:S(2)}, u32[]{:S(2)}) collective-permute-start(bf16[128,2048]{1,0:T(8,128)(2,1)S(1)} %project.8), channel_id=1, source_target_pairs={{0,4},{4,0},{8,12},{12,8},{1,5},{5,1},{9,13},{13,9},{2,6},{6,2},{1... | collective-permute-start | bytes 1572872 | tf_op jit(solution)/shard_map/ppermute | solution.py:362
  109.6 9.1 %collective-permute-start.22 = (bf16[128,2048]{1,0:T(8,128)(2,1)S(1)}, bf16[128,2048]{1,0:T(8,128)(2,1)S(1)}, u32[]{:S(2)}, u32[]{:S(2)}) collective-permute-start(bf16[128,2048]{1,0:T(8,128)(2,1)S(1)} %project.12), channel_id=1, source_target_pairs={{0,4},{4,0},{8,12},{12,8},{1,5},{5,1},{9,13},{13,9},{2,6},{6,2},{1... | collective-permute-start | bytes 1572872 | tf_op jit(solution)/shard_map/ppermute | solution.py:362
  113.0 14.8 %collective-permute-start.18 = (bf16[128,2048]{1,0:T(8,128)(2,1)S(1)}, bf16[128,2048]{1,0:T(8,128)(2,1)S(1)}, u32[]{:S(2)}, u32[]{:S(2)}) collective-permute-start(bf16[128,2048]{1,0:T(8,128)(2,1)S(1)} %project.11), channel_id=1, source_target_pairs={{0,8},{4,12},{8,0},{12,4},{1,9},{5,13},{9,1},{13,5},{2,10},{6,14},... | collective-permute-start | bytes 1572872 | tf_op jit(solution)/shard_map/ppermute | solution.py:366
  116.3 22.1 %collective-permute-start.24 = (bf16[128,2048]{1,0:T(8,128)(2,1)S(1)}, bf16[128,2048]{1,0:T(8,128)(2,1)S(1)}, u32[]{:S(2)}, u32[]{:S(2)}) collective-permute-start(bf16[128,2048]{1,0:T(8,128)(2,1)S(1)} %project.15), channel_id=1, source_target_pairs={{0,8},{4,12},{8,0},{12,4},{1,9},{5,13},{9,1},{13,5},{2,10},{6,14},... | collective-permute-start | bytes 1572872 | tf_op jit(solution)/shard_map/ppermute | solution.py:366
  (11 other events, 51.3 us)

commit v2 on v1

v2 whole, which is shorter than its diff:
```python
import functools
import math

import jax
import jax.numpy as jnp
from jax import lax
from jax.experimental import pallas as pl
from jax.experimental.pallas import tpu as pltpu
from jax.sharding import PartitionSpec as P

HD = 128
BLK = 64
HALVES = 2
STREAMS = 8
CHEAP = 100
DEPTH = 6

norm_eps = 1e-05
rope_base = 500000.0
masked_score = -1e30
MIB = 1 << 20
f32 = jnp.float32
bf16 = jnp.bfloat16
NT = (((1,), (1,)), ((), ()))


def params(mib):
    return pltpu.CompilerParams(vmem_limit_bytes=mib * MIB)


def whole(shape):
    return pl.BlockSpec(shape, lambda *_: (0,) * len(shape))


def resident(x):
    return pltpu.with_memory_space_constraint(x, pltpu.VMEM)


def placed(space, shape):
    return space(shape, bf16)


def in_hbm(x):
    return pltpu.with_memory_space_constraint(x, pltpu.HBM)


VMEM = pl.BlockSpec(memory_space=pltpu.VMEM)
ANY = pl.BlockSpec(memory_space=pl.ANY)


def after(x, *first):
    return lax.optimization_barrier((x, *first))[0]


def cost(flops, moved, exps=0):
    return pl.CostEstimate(
        flops=flops // CHEAP, bytes_accessed=moved // CHEAP, transcendentals=exps // CHEAP
    )


def streamed(copies, at, depth=DEPTH):
    if at == 0:
        for copy in copies[:depth]:
            copy.start()
    copies[at].wait()
    if at + depth < len(copies):
        copies[at + depth].start()


def prep(tokens, sizes):
    rows, width = tokens.shape
    count, parts = len(sizes), 4
    size = rows // parts

    def body(x_ref, *refs):
        *out_refs, held_ref, stat_ref, sems = refs
        firsts = [at * size for at in range(parts)]
        reads = []
        for at, first in enumerate(firsts):
            part = pl.ds(first, size)
            reads.append(
                pltpu.make_async_copy(x_ref.at[part, :], held_ref.at[part, :], sems.at[at])
            )
            reads[at].start()
        begin, copies, totals = 0, [], []
        for at, first in enumerate(firsts):
            reads[at].wait()
            while len(copies) < count and begin + sizes[len(copies)] <= first + size:
                part = pl.ds(begin, sizes[len(copies)])
                sem = sems.at[parts + len(copies)]
                out_ref = out_refs[len(copies)]
                begin += sizes[len(copies)]
                copies.append(pltpu.make_async_copy(held_ref.at[part, :], out_ref, sem))
                copies[-1].start()
            lanes = jnp.zeros((size, HD), f32)
            for k in range(width // HD):
                piece = held_ref[first : first + size, k * HD : (k + 1) * HD].astype(f32)
                lanes = lanes + piece * piece
            totals.append(jnp.sum(lanes, -1, keepdims=True))
        total = jnp.concatenate(totals, 0)
        stat_ref[...] = jnp.broadcast_to(total, (rows, HD)).T[:8, :]
        for copy in copies:
            copy.wait()

    return pl.pallas_call(
        body,
        out_shape=[placed(pltpu.HBM, (piece, width)) for piece in sizes]
        + [placed(pltpu.VMEM, (rows, width)), jax.ShapeDtypeStruct((8, rows), f32)],
        in_specs=[ANY],
        out_specs=[ANY] * count + [VMEM] * 2,
        scratch_shapes=[pltpu.SemaphoreType.DMA((parts + count,))],
        compiler_params=params(2),
        cost_estimate=cost(2 * rows * width, 4 * rows * width),
        name="prep",
    )(in_hbm(tokens))


def inverse_rms(stat_refs, features):
    total = stat_refs[0][...]
    for ref in stat_refs[1:]:
        total = total + ref[...]
    return lax.rsqrt(total / features + norm_eps).T[:, :1]


def normalise(x, inverse, gain):
    return (x.astype(f32) * inverse * gain).astype(bf16)


def load(arrays):
    def body(*refs):
        count = len(arrays)
        sems = refs[-1]
        copies = [
            pltpu.make_async_copy(refs[at], refs[count + at], sems.at[at]) for at in range(count)
        ]
        for copy in copies:
            copy.start()
        for copy in copies:
            copy.wait()

    moved = sum(a.size * 2 for a in arrays)
    return pl.pallas_call(
        body,
        out_shape=[placed(pltpu.VMEM, a.shape) for a in arrays],
        in_specs=[ANY] * len(arrays),
        out_specs=[VMEM] * len(arrays),
        scratch_shapes=[pltpu.SemaphoreType.DMA((len(arrays),))],
        compiler_params=params(2),
        cost_estimate=cost(0, moved),
        name="load",
    )(*[in_hbm(a) for a in arrays])


def kv_partial(scalars, stats, gain, tokens, w_key, w_value, chips):
    rows, width = tokens.shape
    features = gain.shape[1]
    kv_width = w_key.shape[1]
    tile = min(width, 512)
    out = jax.ShapeDtypeStruct((chips, rows, 2 * HD), bf16)

    def body(scalars_ref, *refs):
        gain_ref, x_ref, wk_ref, wv_ref, own_ref, send_ref, acc_k, acc_v = refs[len(stats) :]
        inverse = inverse_rms(refs[: len(stats)], features)
        base = scalars_ref[2 * chips] * width
        for k in range(width // tile):
            part = slice(k * tile, (k + 1) * tile)
            gains = gain_ref[:, pl.ds(pl.multiple_of(base + k * tile, tile), tile)]
            normed = normalise(x_ref[:, part], inverse, gains)
            keys = jnp.dot(normed, wk_ref[part, :], preferred_element_type=f32)
            values = jnp.dot(normed, wv_ref[part, :], preferred_element_type=f32)
            acc_k[...] = keys if k == 0 else acc_k[...] + keys
            acc_v[...] = values if k == 0 else acc_v[...] + values
        for at, out_ref in enumerate((own_ref, send_ref)):
            for chip in range(chips):
                head = scalars_ref[at * chips + chip]
                columns = pl.ds(pl.multiple_of(head * HD, HD), HD)
                out_ref[chip, :, :HD] = acc_k[:, columns].astype(bf16)
                out_ref[chip, :, HD:] = acc_v[:, columns].astype(bf16)

    return pl.pallas_call(
        body,
        out_shape=[out, out],
        grid_spec=pltpu.PrefetchScalarGridSpec(
            num_scalar_prefetch=1,
            grid=(1,),
            in_specs=[VMEM] * (len(stats) + 4),
            out_specs=[VMEM] * 2,
            scratch_shapes=[pltpu.VMEM((rows, kv_width), f32)] * 2,
        ),
        compiler_params=params(8),
        cost_estimate=cost(4 * rows * width * kv_width, 2 * rows * width),
        name="kv_partial",
    )(scalars, *stats, gain, resident(tokens), resident(w_key), resident(w_value))


def turn(x, cosine, sine):
    return x * cosine + pltpu.roll(x, HD // 2, 1) * sine


def kv_final(own, arrived, others, cosine, sine, chip):
    _, rows, width = own.shape

    def body(chip_ref, own_ref, arrived_ref, *refs):
        cos_ref, sin_ref, out_ref = refs[-3:]
        total = own_ref[0].astype(f32) + arrived_ref[0].astype(f32)
        for ref in refs[:-3]:
            total = total + ref[...].astype(f32)
        out_ref[:, :HD] = turn(total[:, :HD], cos_ref[...], sin_ref[...]).astype(bf16)
        out_ref[:, HD:] = total[:, HD:].astype(bf16)

    mine = pl.BlockSpec((1, rows, width), lambda i, s: (s[0], 0, 0))
    return pl.pallas_call(
        body,
        out_shape=jax.ShapeDtypeStruct((rows, width), bf16),
        grid_spec=pltpu.PrefetchScalarGridSpec(
            num_scalar_prefetch=1,
            grid=(1,),
            in_specs=[mine, mine]
            + [whole((rows, width))] * len(others)
            + [whole((rows, HD))] * 2,
            out_specs=whole((rows, width)),
        ),
        compiler_params=params(16),
        cost_estimate=cost(8 * rows * width, 8 * rows * width),
        name="kv_final",
    )(chip[None], own, arrived, *others, cosine, sine)


def query_near(scalars, stats, gain, own, other, w_query):
    rows, width = own.shape
    features, columns = gain.shape[1], w_query.shape[1]
    steps = max(2, STREAMS)
    tile = 2 * width // steps
    n_stats = len(stats)

    def body(scalars_ref, *refs):
        gain_ref, own_ref, other_ref, w_ref, out_ref, x_held, w_held, sems, x_sem = refs[n_stats:]
        other_copy = pltpu.make_async_copy(other_ref, x_held, x_sem)
        places, copies = [], []
        for k in range(steps):
            base = scalars_ref[k * tile // width] * width + k * tile % width
            places.append(pl.ds(pl.multiple_of(base, tile), tile))
            held = w_held.at[pl.ds(k * tile, tile), :]
            copies.append(pltpu.make_async_copy(w_ref.at[places[k], :], held, sems.at[k]))
        inverse = None
        for k in range(steps):
            first = k * tile % width
            if k == steps // 2:
                other_copy.wait()
            streamed(copies, k)
            if k == 0:
                other_copy.start()
                inverse = inverse_rms(refs[:n_stats], features)
            piece = (own_ref if k < steps // 2 else x_held)[:, first : first + tile]
            normed = normalise(piece, inverse, gain_ref[:, places[k]])
            term = jnp.dot(
                normed, w_held[k * tile : (k + 1) * tile, :], preferred_element_type=f32
            )
            out_ref[...] = term if k == 0 else out_ref[...] + term

    return pl.pallas_call(
        body,
        out_shape=jax.ShapeDtypeStruct((rows, columns), f32),
        grid_spec=pltpu.PrefetchScalarGridSpec(
            num_scalar_prefetch=1,
            grid=(1,),
            in_specs=[VMEM] * (n_stats + 2) + [ANY, ANY],
            out_specs=VMEM,
            scratch_shapes=[
                pltpu.VMEM((rows, width), bf16),
                pltpu.VMEM((2 * width, columns), bf16),
                pltpu.SemaphoreType.DMA((steps,)),
                pltpu.SemaphoreType.DMA,
            ],
        ),
        compiler_params=params(16),
        cost_estimate=cost(4 * rows * width * columns, 4 * width * columns),
        name="query_near",
    )(scalars, *stats, gain, resident(own), in_hbm(other), in_hbm(w_query))


def query_far(half, scalars, stats, gain, near, sources, w_query, cosine, sine):
    rows = sum(piece.shape[0] for piece in sources[0])
    width = sources[0][0].shape[1]
    features, columns = gain.shape[1], w_query.shape[1]
    n_stats, n_pieces = len(stats), len(sources[0])
    held = None if half == 0 else w_query
    total = len(sources) * width
    steps = max(len(sources), STREAMS)
    tile = total // steps
    flat = [piece for source in sources for piece in source]

    def body(scalars_ref, *refs):
        x_refs = refs[n_stats + 2 : n_stats + 2 + len(flat)]
        gain_ref, near_ref = refs[n_stats : n_stats + 2]
        cos_ref, sin_ref, w_ref = refs[n_stats + 2 + len(flat) : n_stats + 5 + len(flat)]
        rest = refs[n_stats + 5 + len(flat) :]
        if held is None:
            out_ref, held_ref, acc_ref, x_held, x_sems, sems = rest
        else:
            out_ref, acc_ref, x_held, x_sems = rest
            held_ref = w_ref
        x_copies = []
        for at, x_ref in enumerate(x_refs):
            piece = x_ref.shape[0]
            first = sum(ref.shape[0] for ref in x_refs[at // n_pieces * n_pieces : at])
            part = x_held.at[at // n_pieces, pl.ds(first, piece), :]
            x_copies.append(pltpu.make_async_copy(x_ref, part, x_sems.at[at]))
            x_copies[at].start()
        places, copies = [], []
        for k in range(steps):
            base = scalars_ref[k * tile // width] * width + k * tile % width
            places.append(pl.ds(pl.multiple_of(base, tile), tile))
            if held is None:
                part = held_ref.at[pl.ds(k * tile, tile), :]
                copies.append(pltpu.make_async_copy(w_ref.at[places[k], :], part, sems.at[k]))
        inverse = inverse_rms(refs[:n_stats], features)
        acc_ref[...] = near_ref[...]
        for k in range(steps):
            first, source = k * tile % width, k * tile // width
            if first == 0:
                for copy in x_copies[source * n_pieces : (source + 1) * n_pieces]:
                    copy.wait()
            piece = x_held[source, :, first : first + tile]
            normed = normalise(piece, inverse, gain_ref[:, places[k]])
            if held is None:
                streamed(copies, k)
            acc_ref[...] += jnp.dot(
                normed, held_ref[k * tile : (k + 1) * tile, :], preferred_element_type=f32
            )
        for head in range(columns // HD):
            part = slice(head * HD, (head + 1) * HD)
            rotated = turn(acc_ref[:, part], cos_ref[...], sin_ref[...])
            out_ref[:, part] = rotated.astype(bf16)

    table = pl.BlockSpec((rows, HD), lambda k, s: (half, 0))
    query = jax.ShapeDtypeStruct((rows, columns), bf16)
    first = held is None
    return pl.pallas_call(
        body,
        out_shape=[query, placed(pltpu.VMEM, (total, columns))] if first else query,
        grid_spec=pltpu.PrefetchScalarGridSpec(
            num_scalar_prefetch=1,
            grid=(1,),
            in_specs=[pl.BlockSpec((8, rows), lambda k, s: (0, half))] * n_stats
            + [VMEM, pl.BlockSpec((rows, columns), lambda k, s: (half, 0))]
            + [ANY] * len(flat)
            + [table, table] + [ANY if first else VMEM],
            out_specs=[VMEM] * 2 if first else VMEM,
            scratch_shapes=[
                pltpu.VMEM((rows, columns), f32),
                pltpu.VMEM((len(sources), rows, width), bf16),
                pltpu.SemaphoreType.DMA((len(flat),)),
            ]
            + [pltpu.SemaphoreType.DMA((steps,))] * first,
        ),
        compiler_params=params(8),
        cost_estimate=cost(2 * rows * total * columns, 2 * total * columns * first),
        name="query_far",
    )(
        scalars, *stats, gain, near, *[in_hbm(x) for x in flat], cosine, sine,
        in_hbm(w_query) if first else resident(held),
    )


def attend_kernel(half, n_rows, pick_ref, q_ref, qdoc_ref, kdoc_ref, *refs):
    *refs, out_ref = refs
    rows, columns = q_ref.shape
    heads = columns // HD
    n_kv = kdoc_ref.shape[1] // refs[0].shape[0]
    kv_refs, mem_refs = refs[:n_kv], refs[n_kv:]
    rows_dev = kv_refs[0].shape[0]
    back = (n_kv - 1) * rows_dev
    low, high = half * rows, back + (half + 1) * rows
    keys, values = [], []
    for at, ref in enumerate(kv_refs):
        first, last = max(low, at * rows_dev), min(high, (at + 1) * rows_dev)
        if first < last:
            part = slice(first - at * rows_dev, last - at * rows_dev)
            keys.append(ref[part, :HD])
            values.append(ref[part, HD:])
    keys, values = jnp.concatenate(keys, 0), jnp.concatenate(values, 0)
    span = high - low
    scale = math.log2(math.e) / math.sqrt(HD)
    blocks = rows // BLK
    for block in range(blocks):
        tokens = slice(block * BLK, (block + 1) * BLK)
        query = jnp.concatenate(
            [q_ref[tokens, h * HD : (h + 1) * HD] for h in range(heads)], 0
        )
        row_index = pick_ref[0]
        number = row_index * (rows_dev // BLK) + half * blocks + block
        server = pick_ref[1 + n_rows + number]
        slot = lax.rem(row_index - server + n_rows, n_rows)
        alive = pick_ref[1 + server]
        mem_keys, mem_values = mem_refs[0][0], mem_refs[0][1]
        for at, ref in enumerate(mem_refs[1:]):
            mem_keys = jnp.where(slot == at + 1, ref[0], mem_keys)
            mem_values = jnp.where(slot == at + 1, ref[1], mem_values)
        column = lax.broadcasted_iota(jnp.int32, (BLK, span), 1)
        row = lax.broadcasted_iota(jnp.int32, (BLK, span), 0)
        mask = (column - back <= row + block * BLK) & (
            kdoc_ref[:, low:high] == qdoc_ref[tokens, :1]
        )
        live = lax.broadcasted_iota(jnp.int32, (1, mem_keys.shape[0]), 1) < alive
        doc = lax.dot_general(query, keys, NT, preferred_element_type=f32)
        mem = lax.dot_general(query, mem_keys, NT, preferred_element_type=f32)
        doc = jnp.where(mask[None], (doc * scale).reshape(heads, BLK, span), masked_score)
        doc = doc.reshape(heads * BLK, span)
        mem = jnp.where(live, mem * scale, masked_score)
        top = jnp.maximum(jnp.max(doc, -1, keepdims=True), jnp.max(mem, -1, keepdims=True))
        doc, mem = jnp.exp2(doc - top), jnp.exp2(mem - top)
        total = jnp.sum(doc, -1, keepdims=True) + jnp.sum(mem, -1, keepdims=True)
        share = 1.0 / total
        mixed = jnp.dot((doc * share).astype(bf16), values, preferred_element_type=f32)
        mixed = mixed + jnp.dot(
            (mem * share).astype(bf16), mem_values, preferred_element_type=f32
        )
        mixed = mixed.astype(bf16)
        for h in range(heads):
            out_ref[tokens, h * HD : (h + 1) * HD] = mixed[h * BLK : (h + 1) * BLK]


def attend_half(half, pick, query, q_doc, k_doc, kv, memories):
    rows, columns = query.shape
    slots = memories[0].shape
    span = k_doc.shape[1] + slots[1]
    return pl.pallas_call(
        functools.partial(attend_kernel, half, len(memories)),
        out_shape=jax.ShapeDtypeStruct(query.shape, bf16),
        grid_spec=pltpu.PrefetchScalarGridSpec(
            num_scalar_prefetch=1,
            grid=(1,),
            in_specs=[
                whole((rows, columns)),
                pl.BlockSpec((rows, HD), lambda i, s: (half, 0)),
                whole(k_doc.shape),
            ]
            + [whole(kv[0].shape)] * len(kv)
            + [whole(slots)] * len(memories),
            out_specs=whole((rows, columns)),
        ),
        compiler_params=params(20),
        cost_estimate=cost(
            4 * rows * columns * span, 4 * rows * columns, rows * columns // HD * span
        ),
        name="attend_half",
    )(pick, query, q_doc, k_doc, *kv, *memories)


def load_columns(scalars, w, width, count):
    parts = 4
    rows = w.shape[0] // parts

    def body(scalars_ref, w_ref, out_ref, sems):
        copies = []
        for k in range(count * parts):
            column = pl.multiple_of(scalars_ref[k // parts] * width, width)
            part = pl.ds(k % parts * rows, rows)
            copies.append(
                pltpu.make_async_copy(
                    w_ref.at[part, pl.ds(column, width)],
                    out_ref.at[part, pl.ds(k // parts * width, width)],
                    sems.at[k],
                )
            )
            copies[k].start()
        for copy in copies:
            copy.wait()

    return pl.pallas_call(
        body,
        out_shape=placed(pltpu.VMEM, (w.shape[0], count * width)),
        grid_spec=pltpu.PrefetchScalarGridSpec(
            num_scalar_prefetch=1,
            grid=(1,),
            in_specs=[ANY],
            out_specs=VMEM,
            scratch_shapes=[pltpu.SemaphoreType.DMA((count * parts,))],
        ),
        compiler_params=params(2),
        cost_estimate=cost(0, 2 * w.shape[0] * count * width),
        name="load_columns",
    )(scalars, in_hbm(w))


def project(attended, held, block, width, sizes, kind=bf16, added=None, begin=0):
    depth = attended[0].shape[1]
    tile = min(width, 512)
    rows = sum(sizes)

    def body(*refs):
        a_refs, w_ref = refs[: len(attended)], refs[len(attended)]
        out_refs = refs[-len(sizes) :]
        for k in range(width // tile):
            part = slice(k * tile, (k + 1) * tile)
            place = slice(block * width + k * tile, block * width + (k + 1) * tile)
            pieces, first = [], 0
            for a_ref in a_refs:
                low, high = max(first, begin), min(first + a_ref.shape[0], begin + rows)
                if low < high:
                    a = a_ref[low - first : high - first, :]
                    pieces.append(jnp.dot(a, w_ref[:, place], preferred_element_type=f32))
                first += a_ref.shape[0]
            total = jnp.concatenate(pieces, 0)
            if added is not None:
                total = total + refs[len(attended) + 1][:, part].astype(f32)
            first = 0
            for size, out_ref in zip(sizes, out_refs):
                out_ref[:, part] = total[first : first + size].astype(kind)
                first += size

    given = [] if added is None else [added]
    return pl.pallas_call(
        body,
        out_shape=[jax.ShapeDtypeStruct((size, width), kind) for size in sizes],
        in_specs=[VMEM] * (len(attended) + 1 + len(given)),
        out_specs=[VMEM] * len(sizes),
        compiler_params=params(8),
        cost_estimate=cost(2 * rows * depth * width, 2 * rows * (depth + width)),
        name="project",
    )(*attended, resident(held), *given)


def on_device(tokens, norm_gain, w_query, w_key, w_value, w_out, doc_ids, assign, res_len, res_mem):
    n_tensor = lax.axis_size("tensor")
    n_rows = lax.axis_size("rows")
    chips = n_tensor // 2
    tensor_index = lax.axis_index("tensor").astype(jnp.int32)
    row_index = lax.axis_index("rows").astype(jnp.int32)
    chip, core = tensor_index // 2, tensor_index % 2
    rows_dev, width = tokens.shape
    features = norm_gain.shape[0]
    kv_heads = w_key.shape[1] // HD
    sharers = n_tensor // kv_heads

    def to_core(x):
        return lax.ppermute(x, "tensor", [(i, i ^ 1) for i in range(n_tensor)])

    def to_chip(x, ahead):
        pairs = [(i, (i + 2 * ahead) % n_tensor) for i in range(n_tensor)]
        return lax.ppermute(x, "tensor", pairs)

    def up(x):
        return lax.ppermute(x, "rows", [(i, (i + 1) % n_rows) for i in range(n_rows)])

    away = range(1, chips)

    half_rows = rows_dev // HALVES
    sizes = [half_rows // 2, half_rows // 2] + [half_rows] * (HALVES - 1)
    *pieces, own_tokens, stat = prep(tokens, sizes)
    chip_stats = [to_chip(stat, ahead) for ahead in away]
    stats = [stat, to_core(stat)] + chip_stats + [to_core(s) for s in chip_stats]

    def gather(piece):
        arrived = [to_chip(piece, ahead) for ahead in away]
        return arrived + [to_core(a) for a in arrived]

    far_pieces = [gather(pieces[0])]
    core_tokens = to_core(tokens)
    near_order = jnp.stack([tensor_index, tensor_index ^ 1])
    far_order = [(tensor_index - 2 * ahead) % n_tensor for ahead in away]
    far_order += [((tensor_index ^ 1) - 2 * ahead) % n_tensor for ahead in away]
    far_order = jnp.stack(far_order)

    head_group = after(tensor_index // sharers, stat)
    memories = [lax.dynamic_slice_in_dim(res_mem[0], head_group * HD, HD, 2)]
    for _ in range(n_rows - 1):
        memories.append(up(memories[-1]))

    half_dim = HD // 2
    lane = jnp.arange(HD, dtype=jnp.int32)
    frequency = rope_base ** (-((lane % half_dim).astype(f32) / half_dim))
    positions = (row_index * rows_dev + jnp.arange(rows_dev, dtype=jnp.int32)).astype(f32)
    angles = positions[:, None] * frequency[None, :]
    cosine = jnp.cos(angles)
    sine = jnp.sin(angles) * jnp.where(lane < half_dim, -1.0, 1.0)[None, :]

    gain = norm_gain.astype(f32)[None]
    targets = jnp.arange(chips, dtype=jnp.int32) * 2
    heads = [(targets + core) // sharers, (targets + 1 - core) // sharers, tensor_index[None]]
    scalars = jnp.concatenate(heads).astype(jnp.int32)
    held = load([after(w_key, stat), w_value])
    scalars = after(scalars, memories[1])
    own, send = kv_partial(scalars, stats, gain, own_tokens, *held, chips)
    arrived = after(to_core(send), *far_pieces[0][: chips - 1])
    pairs = []
    for ahead in away:
        target = (chip + ahead) % chips
        pair = lax.dynamic_index_in_dim(own, target, 0, False).astype(f32)
        pair = pair + lax.dynamic_index_in_dim(arrived, target, 0, False).astype(f32)
        pairs.append(pair.astype(bf16))
    others = [to_chip(pair, ahead) for pair, ahead in zip(pairs, away)]
    for piece in pieces[1:-1]:
        far_pieces.append(gather(after(piece, *pairs)))
    last_piece = after(pieces[-1], *pairs)
    last_arrived = [to_chip(last_piece, ahead) for ahead in away]
    near = query_near(after(near_order, *pairs), stats, gain, own_tokens, core_tokens, w_query)
    kv = [kv_final(own, arrived, others, cosine, sine, after(chip, near, *memories[2:3]))]
    total_rows = n_rows * rows_dev
    longest = total_rows // 2
    back = -(-(longest - 1) // rows_dev)
    targets = []
    for ahead in away:
        far = ((chip + ahead) % chips) * 2
        targets += [far + 1 - core, far + core]
    far_targets = jnp.stack(targets)
    near_targets = jnp.stack([tensor_index ^ 1, tensor_index])
    w_out_far = load_columns(after(far_targets, kv[0]), w_out, width, n_tensor - 2)
    for at in range(back):
        kv.insert(0, up(after(kv[0], w_out_far) if at == 1 else kv[0]))

    padded = jnp.concatenate([jnp.full((back * rows_dev,), -1, jnp.int32), doc_ids])
    k_doc = lax.dynamic_slice_in_dim(padded, row_index * rows_dev, (back + 1) * rows_dev)[None]
    q_doc = jnp.broadcast_to(k_doc[0, back * rows_dev :, None], (rows_dev, HD))
    pick = jnp.concatenate([row_index[None], res_len, assign[:, 0]])

    cuts = [half_rows * 3 // 4, half_rows // 4], [half_rows // 2] * 2
    w_far, ready, attended, outs = w_query, [kv[-1], w_out_far], [], []
    for half in range(HALVES):
        if half == 1:
            arrived = [after(a, attended[0]) for a in last_arrived]
            far_pieces.append(last_arrived + [to_core(a) for a in arrived])
        sources = [list(x) for x in zip(*(far_pieces[:2] if half == 0 else far_pieces[2:]))]
        order = after(far_order, *ready)
        query = query_far(half, order, stats, gain, near, sources, w_far, cosine, sine)
        if half == 0:
            query, w_far = query
        one = attend_half(half, pick, query, q_doc, k_doc, kv, memories)
        attended.append(one)
        one = after(one, *(last_arrived if half == 0 else outs[0]))
        ready, sums = [], [[] for _ in cuts[half]]
        for ahead in away:
            block = 2 * (ahead - 1)
            other = [to_core(x) for x in project([one], w_out_far, block, width, cuts[half])]
            begin = 0
            for at, term in enumerate(other):
                size = cuts[half][at]
                (pair,) = project(
                    [one], w_out_far, block + 1, width, [size], added=term, begin=begin
                )
                begin += size
                ready.append(pair)
                sums[at].append(to_chip(pair, ahead))
        outs += sums
    w_near = load_columns(after(near_targets, *ready), w_out, width, 2)
    w_near = after(w_near, *outs[1], *outs[2])
    (term,) = project(attended, w_near, 0, width, [rows_dev])
    sizes = list(cuts[0]) + list(cuts[1])
    parts = list(project(attended, w_near, 1, width, sizes, f32, to_core(term)))
    for at, arrived in enumerate(outs):
        for piece in arrived:
            parts[at] = parts[at] + piece.astype(f32)
    return jnp.concatenate([part.astype(bf16) for part in parts], 0)


def solution(mesh):
    in_specs = (
        P(("groups", "rows"), "tensor"),
        P(),
        P(None, "tensor"),
        P("tensor", None),
        P("tensor", None),
        P("tensor", None),
        P("groups"),
        P("groups", None),
        P("groups"),
        P(("groups", "rows"), None, None, None),
    )
    out_specs = P(("groups", "rows"), "tensor")
    return jax.shard_map(
        on_device, mesh=mesh, in_specs=in_specs, out_specs=out_specs, check_vma=False
    )
```

time: 140 us -> 88.7 us (0.63)
  local copies, waits for them, and re-layouts: 24.9 us -> 1.73 us
  starting transfers between devices: 34.8 us -> 15 us
  waiting for transfers between devices: 31.2 us -> 23.1 us
    unnamed x36 -> x18, local copies, waits for them, and re-layouts: 23.2 us -> 1.51 us
    ppermute x8 -> x5, starting transfers between devices: 25.3 us -> 4.21 us  [up(): lax.ppermute(x, 'rows', [(i, (i + 1) % n_rows) for i in range(n_rows)])]
    ppermute x6 -> x9, waiting for transfers between devices: 28.3 us -> 11.3 us  [to_chip(): return lax.ppermute(x, 'tensor', pairs)]
    ppermute x11 -> x12, waiting for transfers between devices: 0.6 us -> 7.08 us  [to_core(): return lax.ppermute(x, 'tensor', [(i, i ^ 1) for i in range(n_tensor)])]
    ppermute x8 -> x5, waiting for transfers between devices: 2.29 us -> 4.74 us  [up(): lax.ppermute(x, 'rows', [(i, (i + 1) % n_rows) for i in range(n_rows)])]
    pallas_call x13 -> x17, Pallas kernels: 39.2 us -> 41.3 us  [the longest x2 8.82 us: query_far(): pl.pallas_call(body, out_shape=[query, placed(pltpu.VMEM, (total, columns...]
    pallas_call x1, Pallas kernels: 3.79 us -> 2.06 us  [kv_partial(): pl.pallas_call(body, out_shape=[out, out], grid_spec=pltpu.PrefetchScalar...]
    ppermute x6 -> x9, starting transfers between devices: 7.26 us -> 8.79 us  [to_chip(): return lax.ppermute(x, 'tensor', pairs)]
  transfers between devices with their start and end apart: 25 -> 26, of which waited for: 5 -> 12; matrix products, arithmetic and copies ran while one was open for 4% -> 3% of each run, Pallas kernels for 30% -> 47%
where the time goes in v2:
time: 88.7 us; the launch traced here: 88.5 us
  Pallas kernels  44.4 us (50%)
  waiting for transfers between devices  23.1 us (26%)
  starting transfers between devices  15 us (17%)
  other arithmetic  3.71 us (4%)
  local copies, waits for them, and re-layouts  1.73 us (2%)
    ppermute x9, waiting for transfers between devices, to_chip(): return lax.ppermute(x, 'tensor', pairs)  11.3 us
    pallas_call x2, Pallas kernels, query_far(): pl.pallas_call(body, out_shape=[query, placed(pltpu.VMEM, (total, columns...  8.82 us
    ppermute x9, starting transfers between devices, to_chip(): return lax.ppermute(x, 'tensor', pairs)  8.79 us
    pallas_call x2, Pallas kernels, load_columns(): pl.pallas_call(body, out_shape=placed(pltpu.VMEM, (w.shape[0], count * wi...  8.06 us
    pallas_call x8, Pallas kernels, project(): pl.pallas_call(body, out_shape=[jax.ShapeDtypeStruct((size, width), kind)...  7.61 us
    ppermute x12, waiting for transfers between devices, to_core(): return lax.ppermute(x, 'tensor', [(i, i ^ 1) for i in range(n_tensor)])  7.08 us
    pallas_call x2, Pallas kernels, attend_half(): pl.pallas_call(functools.partial(attend_kernel, half, len(memories)), out...  6.67 us
    pallas_call x1, Pallas kernels, query_near(): pl.pallas_call(body, out_shape=jax.ShapeDtypeStruct((rows, columns), f32)...  5.73 us
  transfers between devices with their start and end apart: 26, of which 12 were waited for; matrix products, arithmetic and copies ran while one was open for 3% of the time, Pallas kernels for 47%

profile of v2, /device:TPU:0, one launch (start us, length us, event | category | flops | bytes accessed | tf_op | source)
XLA Modules:
  0.0 88.5 jit_solution(7536463278841510432)
XLA Ops:
  0.5 2.2 %prep.1 = (bf16[64,2048]{1,0:T(8,128)(2,1)}, bf16[64,2048]{1,0:T(8,128)(2,1)}, bf16[128,2048]{1,0:T(8,128)(2,1)}, bf16[256,2048]{1,0:T(8,128)(2,1)S(1)}, f32[8,256]{1,0:T(8,128)S(1)}) custom-call(bf16[256,2048]{1,0:T(8,128)(2,1)} %x_ref.1), custom_call_target="tpu_custom_call" | custom-call | flops 10485 | bytes 20971 | tf_op jit(solution)/shard_map/prep/pallas_call | solution.py:105
  2.7 2.7 %collective-permute-start = (bf16[2,512,128]{2,1,0:T(8,128)(2,1)S(1)}, bf16[2,512,128]{2,1,0:T(8,128)(2,1)S(1)}, u32[]{:S(2)}, u32[]{:S(2)}) collective-permute-start(bf16[2,512,128]{2,1,0:T(8,128)(2,1)S(1)} %dynamic-slice_bitcast_fusion.refs_3_), channel_id=1, source_target_pairs={{0,1},{1,2},{2,3},{3,0},{4,5},{5,6},{6,7},{7,4},{8,9},{9,10},{10,1... | collective-permute-start | bytes 786440 | tf_op jit(solution)/shard_map/ppermute | solution.py:545
  5.5 1.5 %collective-permute-start.2 = (f32[8,256]{1,0:T(8,128)S(1)}, f32[8,256]{1,0:T(8,128)S(1)}, u32[]{:S(2)}, u32[]{:S(2)}) collective-permute-start(f32[8,256]{1,0:T(8,128)S(1)} %get-tuple-element.41.refs_0_), channel_id=1, source_target_pairs={{0,8},{4,12},{8,0},{12,4},{1,9},{5,13},{9,1},{13,5},{2,10},{6,14},... | collective-permute-start | bytes 24584 | tf_op jit(solution)/shard_map/ppermute | solution.py:542
  7.5 1.6 %collective-permute-done.2.refs_2_ = f32[8,256]{1,0:T(8,128)S(1)} collective-permute-done((f32[8,256]{1,0:T(8,128)S(1)}, f32[8,256]{1,0:T(8,128)S(1)}, u32[]{:S(2)}, u32[]{:S(2)}) %collective-permute-start.2) | collective-permute-done | bytes 8224 | tf_op jit(solution)/shard_map/ppermute | solution.py:542
  9.9 2.2 %load.1 = (bf16[2048,512]{1,0:T(8,128)(2,1)S(1)}, bf16[2048,512]{1,0:T(8,128)(2,1)S(1)}) custom-call(bf16[2048,512]{1,0:T(8,128)(2,1)} %refs_0_, bf16[2048,512]{1,0:T(8,128)(2,1)} %refs_1_.1), custom_call_target="tpu_custom_call" | custom-call | bytes 41943 | tf_op jit(solution)/shard_map/load/pallas_call | solution.py:142
  12.2 2.2 %collective-permute-done.refs_4_ = bf16[2,512,128]{2,1,0:T(8,128)(2,1)S(1)} collective-permute-done((bf16[2,512,128]{2,1,0:T(8,128)(2,1)S(1)}, bf16[2,512,128]{2,1,0:T(8,128)(2,1)S(1)}, u32[]{:S(2)}, u32[]{:S(2)}) %collective-permute-start) | collective-permute-done | bytes 262176 | tf_op jit(solution)/shard_map/ppermute | solution.py:545
  14.4 2.1 %kv_partial.1 = (bf16[2,256,256]{2,1,0:T(8,128)(2,1)S(1)}, bf16[2,256,256]{2,1,0:T(8,128)(2,1)S(1)}) custom-call(s32[5]{0:T(128)S(1)} %pad_add_fusion.3.scalars_ref, f32[8,256]{1,0:T(8,128)S(1)} %get-tuple-element.41.refs_0_, f32[8,256]{1,0:T(8,128)S(1)} %collective-permute-done.1.refs_1_, f32[8,256]{1,0:T(8,128)S(1)} %collective-permute-done.2.refs_2_, ...), custom_call_target="tpu_custom_call" | custom-call | flops 10737418 | bytes 10485 | tf_op jit(solution)/shard_map/kv_partial/pallas_call | solution.py:180
  16.7 1.4 %collective-permute-done.4.arrived_ref = bf16[2,256,256]{2,1,0:T(8,128)(2,1)S(1)} collective-permute-done((bf16[2,256,256]{2,1,0:T(8,128)(2,1)S(1)}, bf16[2,256,256]{2,1,0:T(8,128)(2,1)S(1)}, u32[]{:S(2)}, u32[]{:S(2)}) %collective-permute-start.4) | collective-permute-done | bytes 262176 | tf_op jit(solution)/shard_map/ppermute | solution.py:538
  18.8 1.5 %collective-permute-start.8 = (bf16[256,256]{1,0:T(8,128)(2,1)}, bf16[256,256]{1,0:T(8,128)(2,1)}, u32[]{:S(2)}, u32[]{:S(2)}) collective-permute-start(bf16[256,256]{1,0:T(8,128)(2,1)} %fusion.1), channel_id=1, source_target_pairs={{0,8},{4,12},{8,0},{12,4},{1,9},{5,13},{9,1},{13,5},{2,10},{6,14},... | collective-permute-start | bytes 393224 | tf_op jit(solution)/shard_map/ppermute | solution.py:542
  20.8 1.5 %collective-permute-start.15 = (bf16[128,2048]{1,0:T(8,128)(2,1)}, bf16[128,2048]{1,0:T(8,128)(2,1)}, u32[]{:S(2)}, u32[]{:S(2)}) collective-permute-start(bf16[128,2048]{1,0:T(8,128)(2,1)} %get-tuple-element.61), channel_id=1, source_target_pairs={{0,8},{4,12},{8,0},{12,4},{1,9},{5,13},{9,1},{13,5},{2,10},{6,14},... | collective-permute-start | bytes 1572872 | tf_op jit(solution)/shard_map/ppermute | solution.py:542
  23.0 5.7 %query_near.1.refs_5_ = f32[256,1024]{1,0:T(8,128)S(1)} custom-call(s32[2]{0:T(128)S(1)} %pad_add_fusion.2.scalars_ref, f32[8,256]{1,0:T(8,128)S(1)} %get-tuple-element.41.refs_0_, f32[8,256]{1,0:T(8,128)S(1)} %collective-permute-done.1.refs_1_, f32[8,256]{1,0:T(8,128)S(1)} %collective-permute-done.2.refs_2_, f32[8,256]{1,0:T(8,128)S(1)} %collective-permute-done.3.refs_3_, ...), custom_call_target="tpu_custom_call" | custom-call | flops 21474836 | bytes 83886 | tf_op jit(solution)/shard_map/query_near/pallas_call | solution.py:261
  28.8 1.0 %kv_final.1.refs_2_ = bf16[256,256]{1,0:T(8,128)(2,1)S(1)} custom-call(s32[1]{0:T(128)} %bitcast.9.chip_ref, bf16[2,256,256]{2,1,0:T(8,128)(2,1)S(1)} %get-tuple-element.48.own_ref, bf16[2,256,256]{2,1,0:T(8,128)(2,1)S(1)} %copy-done.3, bf16[256,256]{1,0:T(8,128)(2,1)} %collective-permute-done.8.refs_0_, ...), custom_call_target="tpu_custom_call" | custom-call | flops 5242 | bytes 5242 | tf_op jit(solution)/shard_map/kv_final/pallas_call | solution.py:212
  30.0 1.4 %collective-permute-start.14 = (bf16[2,512,128]{2,1,0:T(8,128)(2,1)S(1)}, bf16[2,512,128]{2,1,0:T(8,128)(2,1)S(1)}, u32[]{:S(2)}, u32[]{:S(2)}) collective-permute-start(bf16[2,512,128]{2,1,0:T(8,128)(2,1)S(1)} %collective-permute-done.7.refs_5_), channel_id=1, source_target_pairs={{0,1},{1,2},{2,3},{3,0},{4,5},{5,6},{6,7},{7,4},{8,9},{9,10},{10,1... | collective-permute-start | bytes 786440 | tf_op jit(solution)/shard_map/ppermute | solution.py:545
  31.7 4.0 %load_columns.2.refs_1_ = bf16[1024,4096]{1,0:T(8,128)(2,1)S(1)} custom-call(s32[2]{0:T(128)S(1)} %get-tuple-element.54.scalars_ref, bf16[1024,8192]{1,0:T(8,128)(2,1)} %w_ref.3), custom_call_target="tpu_custom_call" | custom-call | bytes 83886 | tf_op jit(solution)/shard_map/load_columns/pallas_call | solution.py:471
  35.7 2.3 %collective-permute-done.12.refs_1_ = bf16[256,256]{1,0:T(8,128)(2,1)S(1)} collective-permute-done((bf16[256,256]{1,0:T(8,128)(2,1)S(1)}, bf16[256,256]{1,0:T(8,128)(2,1)S(1)}, u32[]{:S(2)}, u32[]{:S(2)}) %collective-permute-start.12) | collective-permute-done | bytes 131104 | tf_op jit(solution)/shard_map/ppermute | solution.py:545
  38.9 5.7 %query_far.2 = (bf16[128,1024]{1,0:T(8,128)(2,1)S(1)}, bf16[4096,1024]{1,0:T(8,128)(2,1)S(1)}) custom-call(s32[2]{0:T(128)S(1)} %get-tuple-element.65.scalars_ref, f32[8,256]{1,0:T(8,128)S(1)} %get-tuple-element.41.refs_0_, f32[8,256]{1,0:T(8,128)S(1)} %collective-permute-done.1.refs_1_, f32[8,256]{1,0:T(8,128)S(1)} %collective-permute-done.2.refs_2_, ...), custom_call_target="tpu_custom_call" | custom-call | flops 10737418 | bytes 83886 | tf_op jit(solution)/shard_map/query_far/pallas_call | solution.py:339
  45.0 3.3 %attend_half.2.refs_0_ = bf16[128,1024]{1,0:T(8,128)(2,1)S(1)} custom-call(s32[21]{0:T(128)S(1)} %pad_add_fusion.pick_ref, bf16[128,1024]{1,0:T(8,128)(2,1)S(1)} %get-tuple-element.58.q_ref, s32[256,128]{1,0:T(8,128)S(1)} %broadcast_in_dim.42.qdoc_ref, s32[1,768]{1,0:T(1,128)S(1)} %broadcast_in_dim.40.kdoc_ref, ...), custom_call_target="tpu_custom_call" | custom-call | flops 6710886 | bytes 5242 | tf_op jit(solution)/shard_map/attend_half/pallas_call | solution.py:428
  49.6 1.2 %collective-permute-done.16.refs_2_ = bf16[96,2048]{1,0:T(8,128)(2,1)S(1)} collective-permute-done((bf16[96,2048]{1,0:T(8,128)(2,1)S(1)}, bf16[96,2048]{1,0:T(8,128)(2,1)S(1)}, u32[]{:S(2)}, u32[]{:S(2)}) %collective-permute-start.16) | collective-permute-done | bytes 393248 | tf_op jit(solution)/shard_map/ppermute | solution.py:538
  52.2 1.3 %collective-permute-done.17.refs_2_ = bf16[32,2048]{1,0:T(8,128)(2,1)S(1)} collective-permute-done((bf16[32,2048]{1,0:T(8,128)(2,1)S(1)}, bf16[32,2048]{1,0:T(8,128)(2,1)S(1)}, u32[]{:S(2)}, u32[]{:S(2)}) %collective-permute-start.17) | collective-permute-done | bytes 131104 | tf_op jit(solution)/shard_map/ppermute | solution.py:538
  55.2 3.1 %query_far.3.q_ref = bf16[128,1024]{1,0:T(8,128)(2,1)S(1)} custom-call(s32[2]{0:T(128)S(1)} %get-tuple-element.65.scalars_ref, f32[8,256]{1,0:T(8,128)S(1)} %get-tuple-element.41.refs_0_, f32[8,256]{1,0:T(8,128)S(1)} %collective-permute-done.1.refs_1_, f32[8,256]{1,0:T(8,128)S(1)} %collective-permute-done.2.refs_2_, ...), custom_call_target="tpu_custom_call" | custom-call | flops 10737418 | tf_op jit(solution)/shard_map/query_far/pallas_call | solution.py:339
  58.3 3.3 %attend_half.3.refs_0_.refs_1_ = bf16[128,1024]{1,0:T(8,128)(2,1)S(1)} custom-call(s32[21]{0:T(128)S(1)} %pad_add_fusion.pick_ref, bf16[128,1024]{1,0:T(8,128)(2,1)S(1)} %query_far.3.q_ref, s32[256,128]{1,0:T(8,128)S(1)} %broadcast_in_dim.42.qdoc_ref, s32[1,768]{1,0:T(1,128)S(1)} %broadcast_in_dim.40.kdoc_ref, ...), custom_call_target="tpu_custom_call" | custom-call | flops 6710886 | bytes 5242 | tf_op jit(solution)/shard_map/attend_half/pallas_call | solution.py:428
  61.7 1.2 %collective-permute-done.19 = bf16[96,2048]{1,0:T(8,128)(2,1)S(1)} collective-permute-done((bf16[96,2048]{1,0:T(8,128)(2,1)S(1)}, bf16[96,2048]{1,0:T(8,128)(2,1)S(1)}, u32[]{:S(2)}, u32[]{:S(2)}) %collective-permute-start.19) | collective-permute-done | bytes 393248 | tf_op jit(solution)/shard_map/ppermute | solution.py:542
  64.2 1.0 %collective-permute-done.20.refs_2_ = bf16[64,2048]{1,0:T(8,128)(2,1)S(1)} collective-permute-done((bf16[64,2048]{1,0:T(8,128)(2,1)S(1)}, bf16[64,2048]{1,0:T(8,128)(2,1)S(1)}, u32[]{:S(2)}, u32[]{:S(2)}) %collective-permute-start.20) | collective-permute-done | bytes 262176 | tf_op jit(solution)/shard_map/ppermute | solution.py:538
  66.6 1.5 %collective-permute-start.22 = (bf16[32,2048]{1,0:T(8,128)(2,1)S(1)}, bf16[32,2048]{1,0:T(8,128)(2,1)S(1)}, u32[]{:S(2)}, u32[]{:S(2)}) collective-permute-start(bf16[32,2048]{1,0:T(8,128)(2,1)S(1)} %project.10), channel_id=1, source_target_pairs={{0,8},{4,12},{8,0},{12,4},{1,9},{5,13},{9,1},{13,5},{2,10},{6,14},... | collective-permute-start | bytes 393224 | tf_op jit(solution)/shard_map/ppermute | solution.py:542
  68.2 1.1 %project.13 = bf16[64,2048]{1,0:T(8,128)(2,1)S(1)} custom-call(bf16[128,1024]{1,0:T(8,128)(2,1)S(1)} %attend_half.3.refs_0_.refs_1_, bf16[1024,4096]{1,0:T(8,128)(2,1)S(1)} %load_columns.2.refs_1_, bf16[64,2048]{1,0:T(8,128)(2,1)S(1)} %collective-permute-done.21.refs_2_), custom_call_target="tpu_custom_call" | custom-call | flops 2684354 | bytes 3932 | tf_op jit(solution)/shard_map/project/pallas_call | solution.py:514
  69.3 4.0 %load_columns.3.refs_2_ = bf16[1024,4096]{1,0:T(8,128)(2,1)S(1)} custom-call(s32[2]{0:T(128)S(1)} %pad_add_fusion.5.scalars_ref, bf16[1024,8192]{1,0:T(8,128)(2,1)} %w_ref.3), custom_call_target="tpu_custom_call" | custom-call | bytes 83886 | tf_op jit(solution)/shard_map/load_columns/pallas_call | solution.py:471
  73.4 3.9 %collective-permute-done.22 = bf16[32,2048]{1,0:T(8,128)(2,1)S(1)} collective-permute-done((bf16[32,2048]{1,0:T(8,128)(2,1)S(1)}, bf16[32,2048]{1,0:T(8,128)(2,1)S(1)}, u32[]{:S(2)}, u32[]{:S(2)}) %collective-permute-start.22) | collective-permute-done | bytes 131104 | tf_op jit(solution)/shard_map/ppermute | solution.py:542
  77.3 1.3 %project.14 = bf16[256,2048]{1,0:T(8,128)(2,1)S(1)} custom-call(bf16[128,1024]{1,0:T(8,128)(2,1)S(1)} %attend_half.2.refs_0_, bf16[128,1024]{1,0:T(8,128)(2,1)S(1)} %attend_half.3.refs_0_.refs_1_, bf16[1024,4096]{1,0:T(8,128)(2,1)S(1)} %load_columns.3.refs_2_), custom_call_target="tpu_custom_call" | custom-call | flops 10737418 | bytes 15728 | tf_op jit(solution)/shard_map/project/pallas_call | solution.py:514
  79.2 2.1 %collective-permute-done.24.refs_3_ = bf16[256,2048]{1,0:T(8,128)(2,1)S(1)} collective-permute-done((bf16[256,2048]{1,0:T(8,128)(2,1)S(1)}, bf16[256,2048]{1,0:T(8,128)(2,1)S(1)}, u32[]{:S(2)}, u32[]{:S(2)}) %collective-permute-start.24) | collective-permute-done | bytes 1048608 | tf_op jit(solution)/shard_map/ppermute | solution.py:538
  81.3 1.3 %project.15 = (f32[96,2048]{1,0:T(8,128)S(1)}, f32[32,2048]{1,0:T(8,128)S(1)}, f32[64,2048]{1,0:T(8,128)S(1)}, f32[64,2048]{1,0:T(8,128)S(1)}) custom-call(bf16[128,1024]{1,0:T(8,128)(2,1)S(1)} %attend_half.2.refs_0_, bf16[128,1024]{1,0:T(8,128)(2,1)S(1)} %attend_half.3.refs_0_.refs_1_, bf16[1024,4096]{1,0:T(8,128)(2,1)S(1)} %load_columns.3.refs_2_, ...), custom_call_target="tpu_custom_call" | custom-call | flops 10737418 | bytes 15728 | tf_op jit(solution)/shard_map/project/pallas_call | solution.py:514
  82.9 4.5 %collective-permute-done.25 = bf16[64,2048]{1,0:T(8,128)(2,1)S(1)} collective-permute-done((bf16[64,2048]{1,0:T(8,128)(2,1)S(1)}, bf16[64,2048]{1,0:T(8,128)(2,1)S(1)}, u32[]{:S(2)}, u32[]{:S(2)}) %collective-permute-start.25) | collective-permute-done | bytes 262176 | tf_op jit(solution)/shard_map/ppermute | solution.py:542
  87.4 1.0 %pad_maximum_fusion = bf16[256,2048]{1,0:T(8,128)(2,1)} fusion(bf16[64,2048]{1,0:T(8,128)(2,1)S(1)} %add_convert_fusion.1, bf16[64,2048]{1,0:T(8,128)(2,1)S(1)} %add_convert_fusion.2, bf16[32,2048]{1,0:T(8,128)(2,1)S(1)} %add_convert_fusion.3, bf16[96,2048]{1,0:T(8,128)(2,1)S(1)} %add_convert_fusion), kind=kLoop, calls=%fused_computation | loop fusion | flops 4194304 | bytes 2097152 | tf_op jit(solution)/shard_map/concatenate | solution.py:654
  (78 shorter events, 13.4 us)
Async XLA Ops:
  0.0 23.0 %collective-permute-start.6 = (bf16[256,2048]{1,0:T(8,128)(2,1)}, bf16[256,2048]{1,0:T(8,128)(2,1)}, u32[]{:S(2)}, u32[]{:S(2)}) collective-permute-start(bf16[256,2048]{1,0:T(8,128)(2,1)} %x_ref.1), channel_id=1, source_target_pairs={{0,4},{4,0},{8,12},{12,8},{1,5},{5,1},{9,13},{13,9},{2,6},{6,2},{1... | collective-permute-start | bytes 3145736 | tf_op jit(solution)/shard_map/ppermute | solution.py:538
  2.7 11.6 %collective-permute-start = (bf16[2,512,128]{2,1,0:T(8,128)(2,1)S(1)}, bf16[2,512,128]{2,1,0:T(8,128)(2,1)S(1)}, u32[]{:S(2)}, u32[]{:S(2)}) collective-permute-start(bf16[2,512,128]{2,1,0:T(8,128)(2,1)S(1)} %dynamic-slice_bitcast_fusion.refs_3_), channel_id=1, source_target_pairs={{0,1},{1,2},{2,3},{3,0},{4,5},{5,6},{6,7},{7,4},{8,9},{9,10},{10,1... | collective-permute-start | bytes 786440 | tf_op jit(solution)/shard_map/ppermute | solution.py:545
  5.5 3.7 %collective-permute-start.2 = (f32[8,256]{1,0:T(8,128)S(1)}, f32[8,256]{1,0:T(8,128)S(1)}, u32[]{:S(2)}, u32[]{:S(2)}) collective-permute-start(f32[8,256]{1,0:T(8,128)S(1)} %get-tuple-element.41.refs_0_), channel_id=1, source_target_pairs={{0,8},{4,12},{8,0},{12,4},{1,9},{5,13},{9,1},{13,5},{2,10},{6,14},... | collective-permute-start | bytes 24584 | tf_op jit(solution)/shard_map/ppermute | solution.py:542
  7.0 7.4 %collective-permute-start.1 = (f32[8,256]{1,0:T(8,128)S(1)}, f32[8,256]{1,0:T(8,128)S(1)}, u32[]{:S(2)}, u32[]{:S(2)}) collective-permute-start(f32[8,256]{1,0:T(8,128)S(1)} %get-tuple-element.41.refs_0_), channel_id=1, source_target_pairs={{0,4},{4,0},{8,12},{12,8},{1,5},{5,1},{9,13},{13,9},{2,6},{6,2},{1... | collective-permute-start | bytes 24584 | tf_op jit(solution)/shard_map/ppermute | solution.py:538
  7.0 9.7 %collective-permute-start.5 = (bf16[64,2048]{1,0:T(8,128)(2,1)}, bf16[64,2048]{1,0:T(8,128)(2,1)}, u32[]{:S(2)}, u32[]{:S(2)}) collective-permute-start(bf16[64,2048]{1,0:T(8,128)(2,1)} %get-tuple-element.50), channel_id=1, source_target_pairs={{0,8},{4,12},{8,0},{12,4},{1,9},{5,13},{9,1},{13,5},{2,10},{6,14},... | collective-permute-start | bytes 786440 | tf_op jit(solution)/shard_map/ppermute | solution.py:542
  9.1 5.3 %collective-permute-start.3 = (f32[8,256]{1,0:T(8,128)S(1)}, f32[8,256]{1,0:T(8,128)S(1)}, u32[]{:S(2)}, u32[]{:S(2)}) collective-permute-start(f32[8,256]{1,0:T(8,128)S(1)} %collective-permute-done.2.refs_2_), channel_id=1, source_target_pairs={{0,4},{4,0},{8,12},{12,8},{1,5},{5,1},{9,13},{13,9},{2,6},{6,2},{1... | collective-permute-start | bytes 24584 | tf_op jit(solution)/shard_map/ppermute | solution.py:538
  16.4 1.6 %collective-permute-start.4 = (bf16[2,256,256]{2,1,0:T(8,128)(2,1)S(1)}, bf16[2,256,256]{2,1,0:T(8,128)(2,1)S(1)}, u32[]{:S(2)}, u32[]{:S(2)}) collective-permute-start(bf16[2,256,256]{2,1,0:T(8,128)(2,1)S(1)} %get-tuple-element.49), channel_id=1, source_target_pairs={{0,4},{4,0},{8,12},{12,8},{1,5},{5,1},{9,13},{13,9},{2,6},{6,2},{1... | collective-permute-start | bytes 786440 | tf_op jit(solution)/shard_map/ppermute | solution.py:538
  16.6 12.2 %collective-permute-start.7 = (bf16[2,512,128]{2,1,0:T(8,128)(2,1)S(1)}, bf16[2,512,128]{2,1,0:T(8,128)(2,1)S(1)}, u32[]{:S(2)}, u32[]{:S(2)}) collective-permute-start(bf16[2,512,128]{2,1,0:T(8,128)(2,1)S(1)} %collective-permute-done.refs_4_), channel_id=1, source_target_pairs={{0,1},{1,2},{2,3},{3,0},{4,5},{5,6},{6,7},{7,4},{8,9},{9,10},{10,1... | collective-permute-start | bytes 786440 | tf_op jit(solution)/shard_map/ppermute | solution.py:545
  18.0 4.3 %copy-start.2 = (bf16[2,256,256]{2,1,0:T(8,128)(2,1)}, bf16[2,256,256]{2,1,0:T(8,128)(2,1)S(1)}, u32[]{:S(2)}) copy-start(bf16[2,256,256]{2,1,0:T(8,128)(2,1)S(1)} %collective-permute-done.4.arrived_ref) | copy-start | bytes 786436
  18.8 9.9 %collective-permute-start.8 = (bf16[256,256]{1,0:T(8,128)(2,1)}, bf16[256,256]{1,0:T(8,128)(2,1)}, u32[]{:S(2)}, u32[]{:S(2)}) collective-permute-start(bf16[256,256]{1,0:T(8,128)(2,1)} %fusion.1), channel_id=1, source_target_pairs={{0,8},{4,12},{8,0},{12,4},{1,9},{5,13},{9,1},{13,5},{2,10},{6,14},... | collective-permute-start | bytes 393224 | tf_op jit(solution)/shard_map/ppermute | solution.py:542
  20.3 11.0 %collective-permute-start.9 = (bf16[64,2048]{1,0:T(8,128)(2,1)}, bf16[64,2048]{1,0:T(8,128)(2,1)}, u32[]{:S(2)}, u32[]{:S(2)}) collective-permute-start(bf16[64,2048]{1,0:T(8,128)(2,1)} %get-tuple-element.57), channel_id=1, source_target_pairs={{0,8},{4,12},{8,0},{12,4},{1,9},{5,13},{9,1},{13,5},{2,10},{6,14},... | collective-permute-start | bytes 786440 | tf_op jit(solution)/shard_map/ppermute | solution.py:542
  20.8 27.5 %collective-permute-start.15 = (bf16[128,2048]{1,0:T(8,128)(2,1)}, bf16[128,2048]{1,0:T(8,128)(2,1)}, u32[]{:S(2)}, u32[]{:S(2)}) collective-permute-start(bf16[128,2048]{1,0:T(8,128)(2,1)} %get-tuple-element.61), channel_id=1, source_target_pairs={{0,8},{4,12},{8,0},{12,4},{1,9},{5,13},{9,1},{13,5},{2,10},{6,14},... | collective-permute-start | bytes 1572872 | tf_op jit(solution)/shard_map/ppermute | solution.py:542
  23.0 5.8 %copy-start.3 = (bf16[2,256,256]{2,1,0:T(8,128)(2,1)S(1)}, bf16[2,256,256]{2,1,0:T(8,128)(2,1)}, u32[]{:S(2)}) copy-start(bf16[2,256,256]{2,1,0:T(8,128)(2,1)} %copy-done.2) | copy-start | bytes 786436
  29.8 8.2 %collective-permute-start.12 = (bf16[256,256]{1,0:T(8,128)(2,1)S(1)}, bf16[256,256]{1,0:T(8,128)(2,1)S(1)}, u32[]{:S(2)}, u32[]{:S(2)}) collective-permute-start(bf16[256,256]{1,0:T(8,128)(2,1)S(1)} %kv_final.1.refs_2_), channel_id=1, source_target_pairs={{0,1},{1,2},{2,3},{3,0},{4,5},{5,6},{6,7},{7,4},{8,9},{9,10},{10,1... | collective-permute-start | bytes 393224 | tf_op jit(solution)/shard_map/ppermute | solution.py:545
  29.9 8.3 %collective-permute-start.10 = (bf16[64,2048]{1,0:T(8,128)(2,1)}, bf16[64,2048]{1,0:T(8,128)(2,1)S(1)}, u32[]{:S(2)}, u32[]{:S(2)}) collective-permute-start(bf16[64,2048]{1,0:T(8,128)(2,1)} %collective-permute-done.5.refs_6_), channel_id=1, source_target_pairs={{0,4},{4,0},{8,12},{12,8},{1,5},{5,1},{9,13},{13,9},{2,6},{6,2},{1... | collective-permute-start | bytes 786440 | tf_op jit(solution)/shard_map/ppermute | solution.py:538
  30.0 14.7 %collective-permute-start.14 = (bf16[2,512,128]{2,1,0:T(8,128)(2,1)S(1)}, bf16[2,512,128]{2,1,0:T(8,128)(2,1)S(1)}, u32[]{:S(2)}, u32[]{:S(2)}) collective-permute-start(bf16[2,512,128]{2,1,0:T(8,128)(2,1)S(1)} %collective-permute-done.7.refs_5_), channel_id=1, source_target_pairs={{0,1},{1,2},{2,3},{3,0},{4,5},{5,6},{6,7},{7,4},{8,9},{9,10},{10,1... | collective-permute-start | bytes 786440 | tf_op jit(solution)/shard_map/ppermute | solution.py:545
  31.4 6.8 %collective-permute-start.11 = (bf16[64,2048]{1,0:T(8,128)(2,1)}, bf16[64,2048]{1,0:T(8,128)(2,1)}, u32[]{:S(2)}, u32[]{:S(2)}) collective-permute-start(bf16[64,2048]{1,0:T(8,128)(2,1)} %collective-permute-done.9.refs_7_), channel_id=1, source_target_pairs={{0,4},{4,0},{8,12},{12,8},{1,5},{5,1},{9,13},{13,9},{2,6},{6,2},{1... | collective-permute-start | bytes 786440 | tf_op jit(solution)/shard_map/ppermute | solution.py:538
  31.7 6.4 %copy-start.6 = (s32[1024]{0:T(1024)S(1)}, s32[1024]{0:T(1024)}, u32[]{:S(2)}) copy-start(s32[1024]{0:T(1024)} %param.16) | copy-start | bytes 12292
  31.7 6.4 %copy-start.7 = (s32[16,1]{0,1:T(1,128)S(1)}, s32[16,1]{0,1:T(1,128)}, u32[]{:S(2)}) copy-start(s32[16,1]{0,1:T(1,128)} %param.17) | copy-start | bytes 196
  31.7 6.4 %copy-start.8 = (s32[4]{0:T(128)S(1)}, s32[4]{0:T(128)}, u32[]{:S(2)}) copy-start(s32[4]{0:T(128)} %param.18) | copy-start | bytes 52
  38.0 6.8 %collective-permute-start.13 = (bf16[256,256]{1,0:T(8,128)(2,1)S(1)}, bf16[256,256]{1,0:T(8,128)(2,1)S(1)}, u32[]{:S(2)}, u32[]{:S(2)}) collective-permute-start(bf16[256,256]{1,0:T(8,128)(2,1)S(1)} %collective-permute-done.12.refs_1_), channel_id=1, source_target_pairs={{0,1},{1,2},{2,3},{3,0},{4,5},{5,6},{6,7},{7,4},{8,9},{9,10},{10,1... | collective-permute-start | bytes 393224 | tf_op jit(solution)/shard_map/ppermute | solution.py:545
  49.1 1.8 %collective-permute-start.16 = (bf16[96,2048]{1,0:T(8,128)(2,1)S(1)}, bf16[96,2048]{1,0:T(8,128)(2,1)S(1)}, u32[]{:S(2)}, u32[]{:S(2)}) collective-permute-start(bf16[96,2048]{1,0:T(8,128)(2,1)S(1)} %get-tuple-element.63), channel_id=1, source_target_pairs={{0,4},{4,0},{8,12},{12,8},{1,5},{5,1},{9,13},{13,9},{2,6},{6,2},{1... | collective-permute-start | bytes 1179656 | tf_op jit(solution)/shard_map/ppermute | solution.py:538
  49.1 5.3 %collective-permute-start.18 = (bf16[128,2048]{1,0:T(8,128)(2,1)}, bf16[128,2048]{1,0:T(8,128)(2,1)S(1)}, u32[]{:S(2)}, u32[]{:S(2)}) collective-permute-start(bf16[128,2048]{1,0:T(8,128)(2,1)} %collective-permute-done.15.refs_6_), channel_id=1, source_target_pairs={{0,4},{4,0},{8,12},{12,8},{1,5},{5,1},{9,13},{13,9},{2,6},{6,2},{1... | collective-permute-start | bytes 1572872 | tf_op jit(solution)/shard_map/ppermute | solution.py:538
  51.7 11.2 %collective-permute-start.19 = (bf16[96,2048]{1,0:T(8,128)(2,1)S(1)}, bf16[96,2048]{1,0:T(8,128)(2,1)S(1)}, u32[]{:S(2)}, u32[]{:S(2)}) collective-permute-start(bf16[96,2048]{1,0:T(8,128)(2,1)S(1)} %project.9), channel_id=1, source_target_pairs={{0,8},{4,12},{8,0},{12,4},{1,9},{5,13},{9,1},{13,5},{2,10},{6,14},... | collective-permute-start | bytes 1179656 | tf_op jit(solution)/shard_map/ppermute | solution.py:542
  52.2 1.3 %collective-permute-start.17 = (bf16[32,2048]{1,0:T(8,128)(2,1)S(1)}, bf16[32,2048]{1,0:T(8,128)(2,1)S(1)}, u32[]{:S(2)}, u32[]{:S(2)}) collective-permute-start(bf16[32,2048]{1,0:T(8,128)(2,1)S(1)} %get-tuple-element.64), channel_id=1, source_target_pairs={{0,4},{4,0},{8,12},{12,8},{1,5},{5,1},{9,13},{13,9},{2,6},{6,2},{1... | collective-permute-start | bytes 393224 | tf_op jit(solution)/shard_map/ppermute | solution.py:538
  63.6 1.6 %collective-permute-start.20 = (bf16[64,2048]{1,0:T(8,128)(2,1)S(1)}, bf16[64,2048]{1,0:T(8,128)(2,1)S(1)}, u32[]{:S(2)}, u32[]{:S(2)}) collective-permute-start(bf16[64,2048]{1,0:T(8,128)(2,1)S(1)} %get-tuple-element.69), channel_id=1, source_target_pairs={{0,4},{4,0},{8,12},{12,8},{1,5},{5,1},{9,13},{13,9},{2,6},{6,2},{1... | collective-permute-start | bytes 786440 | tf_op jit(solution)/shard_map/ppermute | solution.py:538
  63.7 4.6 %collective-permute-start.21 = (bf16[64,2048]{1,0:T(8,128)(2,1)S(1)}, bf16[64,2048]{1,0:T(8,128)(2,1)S(1)}, u32[]{:S(2)}, u32[]{:S(2)}) collective-permute-start(bf16[64,2048]{1,0:T(8,128)(2,1)S(1)} %get-tuple-element.70), channel_id=1, source_target_pairs={{0,4},{4,0},{8,12},{12,8},{1,5},{5,1},{9,13},{13,9},{2,6},{6,2},{1... | collective-permute-start | bytes 786440 | tf_op jit(solution)/shard_map/ppermute | solution.py:538
  66.1 11.2 %collective-permute-start.23 = (bf16[64,2048]{1,0:T(8,128)(2,1)S(1)}, bf16[64,2048]{1,0:T(8,128)(2,1)S(1)}, u32[]{:S(2)}, u32[]{:S(2)}) collective-permute-start(bf16[64,2048]{1,0:T(8,128)(2,1)S(1)} %project.12), channel_id=1, source_target_pairs={{0,8},{4,12},{8,0},{12,4},{1,9},{5,13},{9,1},{13,5},{2,10},{6,14},... | collective-permute-start | bytes 786440 | tf_op jit(solution)/shard_map/ppermute | solution.py:542
  66.6 10.7 %collective-permute-start.22 = (bf16[32,2048]{1,0:T(8,128)(2,1)S(1)}, bf16[32,2048]{1,0:T(8,128)(2,1)S(1)}, u32[]{:S(2)}, u32[]{:S(2)}) collective-permute-start(bf16[32,2048]{1,0:T(8,128)(2,1)S(1)} %project.10), channel_id=1, source_target_pairs={{0,8},{4,12},{8,0},{12,4},{1,9},{5,13},{9,1},{13,5},{2,10},{6,14},... | collective-permute-start | bytes 393224 | tf_op jit(solution)/shard_map/ppermute | solution.py:542
  78.6 2.7 %collective-permute-start.24 = (bf16[256,2048]{1,0:T(8,128)(2,1)S(1)}, bf16[256,2048]{1,0:T(8,128)(2,1)S(1)}, u32[]{:S(2)}, u32[]{:S(2)}) collective-permute-start(bf16[256,2048]{1,0:T(8,128)(2,1)S(1)} %project.14), channel_id=1, source_target_pairs={{0,4},{4,0},{8,12},{12,8},{1,5},{5,1},{9,13},{13,9},{2,6},{6,2},{1... | collective-permute-start | bytes 3145736 | tf_op jit(solution)/shard_map/ppermute | solution.py:538
  78.7 8.7 %collective-permute-start.25 = (bf16[64,2048]{1,0:T(8,128)(2,1)S(1)}, bf16[64,2048]{1,0:T(8,128)(2,1)S(1)}, u32[]{:S(2)}, u32[]{:S(2)}) collective-permute-start(bf16[64,2048]{1,0:T(8,128)(2,1)S(1)} %project.13), channel_id=1, source_target_pairs={{0,8},{4,12},{8,0},{12,4},{1,9},{5,13},{9,1},{13,5},{2,10},{6,14},... | collective-permute-start | bytes 786440 | tf_op jit(solution)/shard_map/ppermute | solution.py:542
  82.7 5.8 %copy-start.1 = (bf16[1,2,512,512]{3,2,1,0:T(8,128)(2,1)S(1)}, bf16[1,2,512,512]{3,2,1,0:T(8,128)(2,1)}, u32[]{:S(2)}) copy-start(bf16[1,2,512,512]{3,2,1,0:T(8,128)(2,1)} %param.19) | copy-start | bytes 3145732
  (3 other events, 4.2 us)

commit v3 on v2

--- a/solution.py
+++ b/solution.py
@@ -14,6 +14,7 @@
 STREAMS = 8
 CHEAP = 100
 DEPTH = 6
+SCOPED = 20
 
 norm_eps = 1e-05
 rope_base = 500000.0
@@ -36,8 +37,8 @@
     return pltpu.with_memory_space_constraint(x, pltpu.VMEM)
 
 
-def placed(space, shape):
-    return space(shape, bf16)
+def placed(space, shape, kind=bf16):
+    return space(shape, kind)
 
 
 def in_hbm(x):
@@ -109,7 +110,7 @@
         in_specs=[ANY],
         out_specs=[ANY] * count + [VMEM] * 2,
         scratch_shapes=[pltpu.SemaphoreType.DMA((parts + count,))],
-        compiler_params=params(2),
+        compiler_params=params(SCOPED),
         cost_estimate=cost(2 * rows * width, 4 * rows * width),
         name="prep",
     )(in_hbm(tokens))
@@ -145,7 +146,7 @@
         in_specs=[ANY] * len(arrays),
         out_specs=[VMEM] * len(arrays),
         scratch_shapes=[pltpu.SemaphoreType.DMA((len(arrays),))],
-        compiler_params=params(2),
+        compiler_params=params(SCOPED),
         cost_estimate=cost(0, moved),
         name="load",
     )(*[in_hbm(a) for a in arrays])
@@ -187,7 +188,7 @@
             out_specs=[VMEM] * 2,
             scratch_shapes=[pltpu.VMEM((rows, kv_width), f32)] * 2,
         ),
-        compiler_params=params(8),
+        compiler_params=params(SCOPED),
         cost_estimate=cost(4 * rows * width * kv_width, 2 * rows * width),
         name="kv_partial",
     )(scalars, *stats, gain, resident(tokens), resident(w_key), resident(w_value))
@@ -220,17 +221,54 @@
             + [whole((rows, HD))] * 2,
             out_specs=whole((rows, width)),
         ),
-        compiler_params=params(16),
+        compiler_params=params(SCOPED),
         cost_estimate=cost(8 * rows * width, 8 * rows * width),
         name="kv_final",
     )(chip[None], own, arrived, *others, cosine, sine)
 
 
+def column_copies(columns, w_ref, out_ref, sems, width, parts=4):
+    rows = w_ref.shape[0] // parts
+    copies = []
+    for k in range(len(columns) * parts):
+        column = pl.multiple_of(columns[k // parts] * width, width)
+        part = pl.ds(k % parts * rows, rows)
+        source = w_ref.at[part, pl.ds(column, width)]
+        target = out_ref.at[part, pl.ds(k // parts * width, width)]
+        copies.append(pltpu.make_async_copy(source, target, sems.at[k]))
+    return copies
+
+
+def load_columns(scalars, w, width, count):
+    def body(scalars_ref, w_ref, out_ref, sems):
+        columns = [scalars_ref[k] for k in range(count)]
+        copies = column_copies(columns, w_ref, out_ref, sems, width)
+        for copy in copies:
+            copy.start()
+        for copy in copies:
+            copy.wait()
+
+    return pl.pallas_call(
+        body,
+        out_shape=placed(pltpu.VMEM, (w.shape[0], count * width)),
+        grid_spec=pltpu.PrefetchScalarGridSpec(
+            num_scalar_prefetch=1,
+            grid=(1,),
+            in_specs=[ANY],
+            out_specs=VMEM,
+            scratch_shapes=[pltpu.SemaphoreType.DMA((count * 4,))],
+        ),
+        compiler_params=params(SCOPED),
+        cost_estimate=cost(0, 2 * w.shape[0] * count * width),
+        name="load_columns",
+    )(scalars, in_hbm(w))
+
+
 def query_near(scalars, stats, gain, own, other, w_query):
     rows, width = own.shape
     features, columns = gain.shape[1], w_query.shape[1]
-    steps = max(2, STREAMS)
-    tile = 2 * width // steps
+    tile = min(width, 1024)
+    steps = 2 * width // tile
     n_stats = len(stats)
 
     def body(scalars_ref, *refs):
@@ -240,19 +278,23 @@
         for k in range(steps):
             base = scalars_ref[k * tile // width] * width + k * tile % width
             places.append(pl.ds(pl.multiple_of(base, tile), tile))
-            held = w_held.at[pl.ds(k * tile, tile), :]
-            copies.append(pltpu.make_async_copy(w_ref.at[places[k], :], held, sems.at[k]))
+            for part in range(2):
+                first = pl.multiple_of(base + part * tile // 2, tile // 2)
+                held = w_held.at[pl.ds(k * tile + part * tile // 2, tile // 2), :]
+                source = w_ref.at[pl.ds(first, tile // 2), :]
+                copies.append(pltpu.make_async_copy(source, held, sems.at[2 * k + part]))
         inverse = None
         for k in range(steps):
             first = k * tile % width
             if k == steps // 2:
                 other_copy.wait()
-            streamed(copies, k)
+            streamed(copies, 2 * k)
             if k == 0:
                 other_copy.start()
                 inverse = inverse_rms(refs[:n_stats], features)
             piece = (own_ref if k < steps // 2 else x_held)[:, first : first + tile]
             normed = normalise(piece, inverse, gain_ref[:, places[k]])
+            streamed(copies, 2 * k + 1)
             term = jnp.dot(
                 normed, w_held[k * tile : (k + 1) * tile, :], preferred_element_type=f32
             )
@@ -260,7 +302,7 @@
 
     return pl.pallas_call(
         body,
-        out_shape=jax.ShapeDtypeStruct((rows, columns), f32),
+        out_shape=placed(pltpu.VMEM, (rows, columns), f32),
         grid_spec=pltpu.PrefetchScalarGridSpec(
             num_scalar_prefetch=1,
             grid=(1,),
@@ -269,36 +311,36 @@
             scratch_shapes=[
                 pltpu.VMEM((rows, width), bf16),
                 pltpu.VMEM((2 * width, columns), bf16),
-                pltpu.SemaphoreType.DMA((steps,)),
+                pltpu.SemaphoreType.DMA((2 * steps,)),
                 pltpu.SemaphoreType.DMA,
             ],
         ),
-        compiler_params=params(16),
+        compiler_params=params(SCOPED),
         cost_estimate=cost(4 * rows * width * columns, 4 * width * columns),
         name="query_near",
-    )(scalars, *stats, gain, resident(own), in_hbm(other), in_hbm(w_query))
-
-
-def query_far(half, scalars, stats, gain, near, sources, w_query, cosine, sine):
+    )(scalars, *stats, gain, resident(own), other, in_hbm(w_query))
+
+
+def query_far(half, scalars, stats, gain, near, sources, weights, out_width, cosine, sine):
     rows = sum(piece.shape[0] for piece in sources[0])
     width = sources[0][0].shape[1]
-    features, columns = gain.shape[1], w_query.shape[1]
+    features, columns = gain.shape[1], weights[0].shape[1]
     n_stats, n_pieces = len(stats), len(sources[0])
-    held = None if half == 0 else w_query
     total = len(sources) * width
-    steps = max(len(sources), STREAMS)
-    tile = total // steps
+    tile = min(width, 1024)
+    steps = total // tile
     flat = [piece for source in sources for piece in source]
+    first_half = half == 0
 
     def body(scalars_ref, *refs):
         x_refs = refs[n_stats + 2 : n_stats + 2 + len(flat)]
         gain_ref, near_ref = refs[n_stats : n_stats + 2]
         cos_ref, sin_ref, w_ref = refs[n_stats + 2 + len(flat) : n_stats + 5 + len(flat)]
         rest = refs[n_stats + 5 + len(flat) :]
-        if held is None:
+        if first_half:
             out_ref, held_ref, acc_ref, x_held, x_sems, sems = rest
         else:
-            out_ref, acc_ref, x_held, x_sems = rest
+            wo_ref, out_ref, wo_held, acc_ref, x_held, x_sems, sems = rest
             held_ref = w_ref
         x_copies = []
         for at, x_ref in enumerate(x_refs):
@@ -311,55 +353,72 @@
         for k in range(steps):
             base = scalars_ref[k * tile // width] * width + k * tile % width
             places.append(pl.ds(pl.multiple_of(base, tile), tile))
-            if held is None:
-                part = held_ref.at[pl.ds(k * tile, tile), :]
-                copies.append(pltpu.make_async_copy(w_ref.at[places[k], :], part, sems.at[k]))
-        inverse = inverse_rms(refs[:n_stats], features)
-        acc_ref[...] = near_ref[...]
+            for part in range(2 * first_half):
+                first = pl.multiple_of(base + part * tile // 2, tile // 2)
+                held = held_ref.at[pl.ds(k * tile + part * tile // 2, tile // 2), :]
+                source = w_ref.at[pl.ds(first, tile // 2), :]
+                copies.append(pltpu.make_async_copy(source, held, sems.at[2 * k + part]))
+        if not first_half:
+            targets = [scalars_ref[len(sources) + k] for k in range(2)]
+            copies = column_copies(targets, wo_ref, wo_held, sems, out_width)
+            for copy in copies:
+                copy.start()
+        inverse = None
         for k in range(steps):
             first, source = k * tile % width, k * tile // width
+            if first_half:
+                streamed(copies, 2 * k)
+            if k == 0:
+                inverse = inverse_rms(refs[:n_stats], features)
             if first == 0:
                 for copy in x_copies[source * n_pieces : (source + 1) * n_pieces]:
                     copy.wait()
-            piece = x_held[source, :, first : first + tile]
-            normed = normalise(piece, inverse, gain_ref[:, places[k]])
-            if held is None:
-                streamed(copies, k)
-            acc_ref[...] += jnp.dot(
+            normed = normalise(
+                x_held[source, :, first : first + tile], inverse, gain_ref[:, places[k]]
+            )
+            if first_half:
+                streamed(copies, 2 * k + 1)
+            term = jnp.dot(
                 normed, held_ref[k * tile : (k + 1) * tile, :], preferred_element_type=f32
             )
+            given = near_ref[half * rows : (half + 1) * rows, :] if k == 0 else acc_ref[...]
+            acc_ref[...] = given + term
         for head in range(columns // HD):
             part = slice(head * HD, (head + 1) * HD)
             rotated = turn(acc_ref[:, part], cos_ref[...], sin_ref[...])
             out_ref[:, part] = rotated.astype(bf16)
+        if not first_half:
+            for copy in copies:
+                copy.wait()
 
     table = pl.BlockSpec((rows, HD), lambda k, s: (half, 0))
     query = jax.ShapeDtypeStruct((rows, columns), bf16)
-    first = held is None
+    held_shape = (total, columns) if first_half else (columns, 2 * out_width)
+    given = [in_hbm(weights[0])] if first_half else [resident(weights[0]), in_hbm(weights[1])]
     return pl.pallas_call(
         body,
-        out_shape=[query, placed(pltpu.VMEM, (total, columns))] if first else query,
+        out_shape=[query, placed(pltpu.VMEM, held_shape)],
         grid_spec=pltpu.PrefetchScalarGridSpec(
             num_scalar_prefetch=1,
             grid=(1,),
             in_specs=[pl.BlockSpec((8, rows), lambda k, s: (0, half))] * n_stats
-            + [VMEM, pl.BlockSpec((rows, columns), lambda k, s: (half, 0))]
+            + [VMEM, VMEM]
             + [ANY] * len(flat)
-            + [table, table] + [ANY if first else VMEM],
-            out_specs=[VMEM] * 2 if first else VMEM,
+            + [table, table]
+            + ([ANY] if first_half else [VMEM, ANY]),
+            out_specs=[VMEM, VMEM],
             scratch_shapes=[
                 pltpu.VMEM((rows, columns), f32),
                 pltpu.VMEM((len(sources), rows, width), bf16),
                 pltpu.SemaphoreType.DMA((len(flat),)),
-            ]
-            + [pltpu.SemaphoreType.DMA((steps,))] * first,
+                pltpu.SemaphoreType.DMA((2 * steps if first_half else 8,)),
+            ],
         ),
-        compiler_params=params(8),
-        cost_estimate=cost(2 * rows * total * columns, 2 * total * columns * first),
+        compiler_params=params(SCOPED),
+        cost_estimate=cost(2 * rows * total * columns, 2 * total * columns),
         name="query_far",
     )(
-        scalars, *stats, gain, near, *[in_hbm(x) for x in flat], cosine, sine,
-        in_hbm(w_query) if first else resident(held),
+        scalars, *stats, gain, resident(near), *flat, cosine, sine, *given
     )
 
 
@@ -440,7 +499,7 @@
             + [whole(slots)] * len(memories),
             out_specs=whole((rows, columns)),
         ),
-        compiler_params=params(20),
+        compiler_params=params(SCOPED),
         cost_estimate=cost(
             4 * rows * columns * span, 4 * rows * columns, rows * columns // HD * span
         ),
@@ -448,43 +507,7 @@
     )(pick, query, q_doc, k_doc, *kv, *memories)
 
 
-def load_columns(scalars, w, width, count):
-    parts = 4
-    rows = w.shape[0] // parts
-
-    def body(scalars_ref, w_ref, out_ref, sems):
-        copies = []
-        for k in range(count * parts):
-            column = pl.multiple_of(scalars_ref[k // parts] * width, width)
-            part = pl.ds(k % parts * rows, rows)
-            copies.append(
-                pltpu.make_async_copy(
-                    w_ref.at[part, pl.ds(column, width)],
-                    out_ref.at[part, pl.ds(k // parts * width, width)],
-                    sems.at[k],
-                )
-            )
-            copies[k].start()
-        for copy in copies:
-            copy.wait()
-
-    return pl.pallas_call(
-        body,
-        out_shape=placed(pltpu.VMEM, (w.shape[0], count * width)),
-        grid_spec=pltpu.PrefetchScalarGridSpec(
-            num_scalar_prefetch=1,
-            grid=(1,),
-            in_specs=[ANY],
-            out_specs=VMEM,
-            scratch_shapes=[pltpu.SemaphoreType.DMA((count * parts,))],
-        ),
-        compiler_params=params(2),
-        cost_estimate=cost(0, 2 * w.shape[0] * count * width),
-        name="load_columns",
-    )(scalars, in_hbm(w))
-
-
-def project(attended, held, block, width, sizes, kind=bf16, added=None, begin=0):
+def project(attended, held, block, width, sizes, kind=bf16, added=(), begin=0):
     depth = attended[0].shape[1]
     tile = min(width, 512)
     rows = sum(sizes)
@@ -503,23 +526,23 @@
                     pieces.append(jnp.dot(a, w_ref[:, place], preferred_element_type=f32))
                 first += a_ref.shape[0]
             total = jnp.concatenate(pieces, 0)
-            if added is not None:
-                total = total + refs[len(attended) + 1][:, part].astype(f32)
+            if added:
+                terms = [ref[:, part].astype(f32) for ref in refs[len(attended) + 1 : -len(sizes)]]
+                total = total + jnp.concatenate(terms, 0)
             first = 0
             for size, out_ref in zip(sizes, out_refs):
                 out_ref[:, part] = total[first : first + size].astype(kind)
                 first += size
 
-    given = [] if added is None else [added]
     return pl.pallas_call(
         body,
         out_shape=[jax.ShapeDtypeStruct((size, width), kind) for size in sizes],
-        in_specs=[VMEM] * (len(attended) + 1 + len(given)),
+        in_specs=[VMEM] * (len(attended) + 1 + len(added)),
         out_specs=[VMEM] * len(sizes),
-        compiler_params=params(8),
+        compiler_params=params(SCOPED),
         cost_estimate=cost(2 * rows * depth * width, 2 * rows * (depth + width)),
         name="project",
-    )(*attended, resident(held), *given)
+    )(*attended, resident(held), *added)
 
 
 def on_device(tokens, norm_gain, w_query, w_key, w_value, w_out, doc_ids, assign, res_len, res_mem):
@@ -547,7 +570,7 @@
     away = range(1, chips)
 
     half_rows = rows_dev // HALVES
-    sizes = [half_rows // 2, half_rows // 2] + [half_rows] * (HALVES - 1)
+    sizes = [half_rows] * HALVES
     *pieces, own_tokens, stat = prep(tokens, sizes)
     chip_stats = [to_chip(stat, ahead) for ahead in away]
     stats = [stat, to_core(stat)] + chip_stats + [to_core(s) for s in chip_stats]
@@ -581,9 +604,8 @@
     heads = [(targets + core) // sharers, (targets + 1 - core) // sharers, tensor_index[None]]
     scalars = jnp.concatenate(heads).astype(jnp.int32)
     held = load([after(w_key, stat), w_value])
-    scalars = after(scalars, memories[1])
     own, send = kv_partial(scalars, stats, gain, own_tokens, *held, chips)
-    arrived = after(to_core(send), *far_pieces[0][: chips - 1])
+    arrived = after(to_core(after(send, memories[1])), *far_pieces[0][: chips - 1])
     pairs = []
     for ahead in away:
         target = (chip + ahead) % chips
@@ -591,63 +613,71 @@
         pair = pair + lax.dynamic_index_in_dim(arrived, target, 0, False).astype(f32)
         pairs.append(pair.astype(bf16))
     others = [to_chip(pair, ahead) for pair, ahead in zip(pairs, away)]
-    for piece in pieces[1:-1]:
-        far_pieces.append(gather(after(piece, *pairs)))
-    last_piece = after(pieces[-1], *pairs)
-    last_arrived = [to_chip(last_piece, ahead) for ahead in away]
-    near = query_near(after(near_order, *pairs), stats, gain, own_tokens, core_tokens, w_query)
-    kv = [kv_final(own, arrived, others, cosine, sine, after(chip, near, *memories[2:3]))]
-    total_rows = n_rows * rows_dev
-    longest = total_rows // 2
-    back = -(-(longest - 1) // rows_dev)
     targets = []
     for ahead in away:
         far = ((chip + ahead) % chips) * 2
         targets += [far + 1 - core, far + core]
     far_targets = jnp.stack(targets)
     near_targets = jnp.stack([tensor_index ^ 1, tensor_index])
-    w_out_far = load_columns(after(far_targets, kv[0]), w_out, width, n_tensor - 2)
-    for at in range(back):
-        kv.insert(0, up(after(kv[0], w_out_far) if at == 1 else kv[0]))
+    total_rows = n_rows * rows_dev
+    longest = total_rows // 2
+    back = -(-(longest - 1) // rows_dev)
 
     padded = jnp.concatenate([jnp.full((back * rows_dev,), -1, jnp.int32), doc_ids])
     k_doc = lax.dynamic_slice_in_dim(padded, row_index * rows_dev, (back + 1) * rows_dev)[None]
     q_doc = jnp.broadcast_to(k_doc[0, back * rows_dev :, None], (rows_dev, HD))
     pick = jnp.concatenate([row_index[None], res_len, assign[:, 0]])
-
-    cuts = [half_rows * 3 // 4, half_rows // 4], [half_rows // 2] * 2
-    w_far, ready, attended, outs = w_query, [kv[-1], w_out_far], [], []
+    far_order = jnp.concatenate([far_order, near_targets])
+    small = (k_doc, q_doc, pick, near_order, far_order, cosine, sine)
+
+    w_out_far = load_columns(after(far_targets, *pairs, *small), w_out, width, n_tensor - 2)
+    kv = [kv_final(own, arrived, others, cosine, sine, after(chip, w_out_far, *memories[2:3]))]
+    last_piece = after(pieces[-1], kv[0])
+    last_arrived = [to_chip(last_piece, ahead) for ahead in away]
+    near_order = after(near_order, kv[0])
+    near = query_near(near_order, stats, gain, own_tokens, core_tokens, w_query)
+    for at in range(back):
+        kv.insert(0, up(after(kv[0], near) if at == 1 else kv[0]))
+
+    early = half_rows * 3 // 4 // 16 * 16
+    cuts = [early, half_rows - early], [half_rows]
+    weights, ready, attended, outs = [w_query], [near], [], []
     for half in range(HALVES):
         if half == 1:
             arrived = [after(a, attended[0]) for a in last_arrived]
             far_pieces.append(last_arrived + [to_core(a) for a in arrived])
-        sources = [list(x) for x in zip(*(far_pieces[:2] if half == 0 else far_pieces[2:]))]
+        sources = [list(x) for x in zip(*(far_pieces[half : half + 1]))]
         order = after(far_order, *ready)
-        query = query_far(half, order, stats, gain, near, sources, w_far, cosine, sine)
-        if half == 0:
-            query, w_far = query
+        query, w_held = query_far(
+            half, order, stats, gain, near, sources, weights, width, cosine, sine
+        )
+        weights = [w_held, w_out]
         one = attend_half(half, pick, query, q_doc, k_doc, kv, memories)
         attended.append(one)
         one = after(one, *(last_arrived if half == 0 else outs[0]))
-        ready, sums = [], [[] for _ in cuts[half]]
+        ready, sums, begin = [], [[] for _ in cuts[half]], 0
+        others = []
         for ahead in away:
             block = 2 * (ahead - 1)
-            other = [to_core(x) for x in project([one], w_out_far, block, width, cuts[half])]
-            begin = 0
-            for at, term in enumerate(other):
-                size = cuts[half][at]
+            sent = project([one], w_out_far, block, width, cuts[half])
+            last = after(attended[-1], *sent)
+            others.append([to_core(x) for x in sent])
+        if half == HALVES - 1:
+            terms = project(attended[:-1] + [last], w_held, 0, width, [rows_dev])
+            one = after(one, *terms)
+            terms = [to_core(x) for x in terms]
+        for at, size in enumerate(cuts[half]):
+            for ahead, other in zip(away, others):
                 (pair,) = project(
-                    [one], w_out_far, block + 1, width, [size], added=term, begin=begin
+                    [one], w_out_far, 2 * ahead - 1, width, [size], added=[other[at]], begin=begin
                 )
-                begin += size
                 ready.append(pair)
                 sums[at].append(to_chip(pair, ahead))
+            begin += size
         outs += sums
-    w_near = load_columns(after(near_targets, *ready), w_out, width, 2)
-    w_near = after(w_near, *outs[1], *outs[2])
-    (term,) = project(attended, w_near, 0, width, [rows_dev])
     sizes = list(cuts[0]) + list(cuts[1])
-    parts = list(project(attended, w_near, 1, width, sizes, f32, to_core(term)))
+    own_half = after(attended[-1], *ready)
+    parts = list(project([attended[0], own_half], w_held, 1, width, sizes, f32, terms))
     for at, arrived in enumerate(outs):
         for piece in arrived:
             parts[at] = parts[at] + piece.astype(f32)

time: 88.7 us -> 83.9 us (0.946)
  Pallas kernels: 44.4 us -> 38.7 us
  waiting for transfers between devices: 23.1 us -> 26.4 us
  starting transfers between devices: 15 us -> 14.1 us
    ppermute x9 -> x7, waiting for transfers between devices: 11.3 us -> 17 us  [to_chip(): return lax.ppermute(x, 'tensor', pairs)]
    pallas_call x2 -> x1, Pallas kernels: 8.06 us -> 4.03 us  [load_columns(): pl.pallas_call(body, out_shape=placed(pltpu.VMEM, (w.shape[0], count * wi...]
    ppermute x12 -> x10, waiting for transfers between devices: 7.08 us -> 4.65 us  [to_core(): return lax.ppermute(x, 'tensor', [(i, i ^ 1) for i in range(n_tensor)])]
    ppermute x9 -> x7, starting transfers between devices: 8.79 us -> 6.87 us  [to_chip(): return lax.ppermute(x, 'tensor', pairs)]
    unnamed x18 -> x14, local copies, waits for them, and re-layouts: 1.51 us -> 0.28 us
    ppermute x5, starting transfers between devices: 4.21 us -> 5.44 us  [up(): lax.ppermute(x, 'rows', [(i, (i + 1) % n_rows) for i in range(n_rows)])]
    pallas_call x8 -> x7, Pallas kernels: 7.61 us -> 6.48 us  [project(): pl.pallas_call(body, out_shape=[jax.ShapeDtypeStruct((size, width), kind)...]
    pallas_call x1, Pallas kernels: 1.03 us -> 0.12 us  [kv_final(): pl.pallas_call(body, out_shape=jax.ShapeDtypeStruct((rows, width), bf16),...]
  transfers between devices with their start and end apart: 26 -> 22, of which waited for: 12 -> 9; matrix products, arithmetic and copies ran while one was open for 3% -> 3% of each run, Pallas kernels for 47% -> 43%
where the time goes in v3:
time: 83.9 us; the launch traced here: 83.7 us
  Pallas kernels  38.7 us (46%)
  waiting for transfers between devices  26.4 us (31%)
  starting transfers between devices  14.1 us (17%)
  other arithmetic  2.99 us (4%)
  local copies, waits for them, and re-layouts  1.19 us (1%)
    ppermute x7, waiting for transfers between devices, to_chip(): return lax.ppermute(x, 'tensor', pairs)  17 us
    pallas_call x2, Pallas kernels, query_far(): pl.pallas_call(body, out_shape=[query, placed(pltpu.VMEM, held_shape)], g...  9.32 us
    ppermute x7, starting transfers between devices, to_chip(): return lax.ppermute(x, 'tensor', pairs)  6.87 us
    pallas_call x2, Pallas kernels, attend_half(): pl.pallas_call(functools.partial(attend_kernel, half, len(memories)), out...  6.79 us
    pallas_call x7, Pallas kernels, project(): pl.pallas_call(body, out_shape=[jax.ShapeDtypeStruct((size, width), kind)...  6.48 us
    ppermute x5, starting transfers between devices, up(): lax.ppermute(x, 'rows', [(i, (i + 1) % n_rows) for i in range(n_rows)])  5.44 us
    pallas_call x1, Pallas kernels, query_near(): pl.pallas_call(body, out_shape=placed(pltpu.VMEM, (rows, columns), f32),...  5.44 us
    ppermute x5, waiting for transfers between devices, up(): lax.ppermute(x, 'rows', [(i, (i + 1) % n_rows) for i in range(n_rows)])  4.76 us
  transfers between devices with their start and end apart: 22, of which 9 were waited for; matrix products, arithmetic and copies ran while one was open for 3% of the time, Pallas kernels for 43%

profile of v3, /device:TPU:0, one launch (start us, length us, event | category | flops | bytes accessed | tf_op | source)
XLA Modules:
  0.0 83.7 jit_solution(16777910728890518259)
XLA Ops:
  0.5 2.2 %prep.1 = (bf16[128,2048]{1,0:T(8,128)(2,1)}, bf16[128,2048]{1,0:T(8,128)(2,1)}, bf16[256,2048]{1,0:T(8,128)(2,1)S(1)}, f32[8,256]{1,0:T(8,128)S(1)}) custom-call(bf16[256,2048]{1,0:T(8,128)(2,1)} %x_ref.1), custom_call_target="tpu_custom_call" | custom-call | flops 10485 | bytes 20971 | tf_op jit(solution)/shard_map/prep/pallas_call | solution.py:106
  2.7 2.7 %collective-permute-start.1 = (f32[8,256]{1,0:T(8,128)S(1)}, f32[8,256]{1,0:T(8,128)S(1)}, u32[]{:S(2)}, u32[]{:S(2)}) collective-permute-start(f32[8,256]{1,0:T(8,128)S(1)} %get-tuple-element.39.refs_0_), channel_id=1, source_target_pairs={{0,8},{4,12},{8,0},{12,4},{1,9},{5,13},{9,1},{13,5},{2,10},{6,14},... | collective-permute-start | bytes 24584 | tf_op jit(solution)/shard_map/ppermute | solution.py:565
  5.5 1.6 %collective-permute-start.3 = (bf16[2,512,128]{2,1,0:T(8,128)(2,1)S(1)}, bf16[2,512,128]{2,1,0:T(8,128)(2,1)S(1)}, u32[]{:S(2)}, u32[]{:S(2)}) collective-permute-start(bf16[2,512,128]{2,1,0:T(8,128)(2,1)S(1)} %dynamic-slice_bitcast_fusion.refs_3_), channel_id=1, source_target_pairs={{0,1},{1,2},{2,3},{3,0},{4,5},{5,6},{6,7},{7,4},{8,9},{9,10},{10,1... | collective-permute-start | bytes 786440 | tf_op jit(solution)/shard_map/ppermute | solution.py:568
  7.7 0.8 pad_dynamic-slice_fusion
  9.4 2.2 %load.1 = (bf16[2048,512]{1,0:T(8,128)(2,1)S(1)}, bf16[2048,512]{1,0:T(8,128)(2,1)S(1)}) custom-call(bf16[2048,512]{1,0:T(8,128)(2,1)} %refs_0_, bf16[2048,512]{1,0:T(8,128)(2,1)} %refs_1_.1), custom_call_target="tpu_custom_call" | custom-call | bytes 41943 | tf_op jit(solution)/shard_map/load/pallas_call | solution.py:143
  11.7 2.1 %kv_partial.1 = (bf16[2,256,256]{2,1,0:T(8,128)(2,1)S(1)}, bf16[2,256,256]{2,1,0:T(8,128)(2,1)S(1)}) custom-call(s32[5]{0:T(128)S(1)} %pad_add_fusion.4.scalars_ref, f32[8,256]{1,0:T(8,128)S(1)} %get-tuple-element.39.refs_0_, f32[8,256]{1,0:T(8,128)S(1)} %collective-permute-done.refs_1_, f32[8,256]{1,0:T(8,128)S(1)} %collective-permute-done.1.refs_2_, ...), custom_call_target="tpu_custom_call" | custom-call | flops 10737418 | bytes 10485 | tf_op jit(solution)/shard_map/kv_partial/pallas_call | solution.py:181
  13.7 2.3 %collective-permute-done.3.refs_4_ = bf16[2,512,128]{2,1,0:T(8,128)(2,1)S(1)} collective-permute-done((bf16[2,512,128]{2,1,0:T(8,128)(2,1)S(1)}, bf16[2,512,128]{2,1,0:T(8,128)(2,1)S(1)}, u32[]{:S(2)}, u32[]{:S(2)}) %collective-permute-start.3) | collective-permute-done | bytes 262176 | tf_op jit(solution)/shard_map/ppermute | solution.py:568
  16.7 4.7 %collective-permute-done.5.refs_6_ = bf16[128,2048]{1,0:T(8,128)(2,1)} collective-permute-done((bf16[128,2048]{1,0:T(8,128)(2,1)}, bf16[128,2048]{1,0:T(8,128)(2,1)}, u32[]{:S(2)}, u32[]{:S(2)}) %collective-permute-start.5) | collective-permute-done | bytes 524320 | tf_op jit(solution)/shard_map/ppermute | solution.py:565
  22.3 4.0 %load_columns.1.refs_1_ = bf16[1024,4096]{1,0:T(8,128)(2,1)S(1)} custom-call(s32[2]{0:T(128)S(1)} %pad_add_fusion.3.scalars_ref, bf16[1024,8192]{1,0:T(8,128)(2,1)} %refs_11_.1), custom_call_target="tpu_custom_call" | custom-call | bytes 83886 | tf_op jit(solution)/shard_map/load_columns/pallas_call | solution.py:251
  26.3 0.9 %collective-permute-done.6.refs_5_ = bf16[2,512,128]{2,1,0:T(8,128)(2,1)S(1)} collective-permute-done((bf16[2,512,128]{2,1,0:T(8,128)(2,1)S(1)}, bf16[2,512,128]{2,1,0:T(8,128)(2,1)S(1)}, u32[]{:S(2)}, u32[]{:S(2)}) %collective-permute-start.6) | collective-permute-done | bytes 262176 | tf_op jit(solution)/shard_map/ppermute | solution.py:568
  27.3 0.7 collective-permute-start.13
  28.1 1.6 %collective-permute-start.10 = (bf16[256,256]{1,0:T(8,128)(2,1)S(1)}, bf16[256,256]{1,0:T(8,128)(2,1)S(1)}, u32[]{:S(2)}, u32[]{:S(2)}) collective-permute-start(bf16[256,256]{1,0:T(8,128)(2,1)S(1)} %kv_final.1.refs_2_), channel_id=1, source_target_pairs={{0,1},{1,2},{2,3},{3,0},{4,5},{5,6},{6,7},{7,4},{8,9},{9,10},{10,1... | collective-permute-start | bytes 393224 | tf_op jit(solution)/shard_map/ppermute | solution.py:568
  29.7 1.6 %collective-permute-start.12 = (bf16[2,512,128]{2,1,0:T(8,128)(2,1)S(1)}, bf16[2,512,128]{2,1,0:T(8,128)(2,1)S(1)}, u32[]{:S(2)}, u32[]{:S(2)}) collective-permute-start(bf16[2,512,128]{2,1,0:T(8,128)(2,1)S(1)} %collective-permute-done.6.refs_5_), channel_id=1, source_target_pairs={{0,1},{1,2},{2,3},{3,0},{4,5},{5,6},{6,7},{7,4},{8,9},{9,10},{10,1... | collective-permute-start | bytes 786440 | tf_op jit(solution)/shard_map/ppermute | solution.py:568
  31.2 5.4 %query_near.1.refs_5_ = f32[256,1024]{1,0:T(8,128)S(1)} custom-call(s32[2]{0:T(128)S(1)} %pad_add_fusion.2.scalars_ref, f32[8,256]{1,0:T(8,128)S(1)} %get-tuple-element.39.refs_0_, f32[8,256]{1,0:T(8,128)S(1)} %collective-permute-done.refs_1_, f32[8,256]{1,0:T(8,128)S(1)} %collective-permute-done.1.refs_2_, f32[8,256]{1,0:T(8,128)S(1)} %collective-permute-done.2.refs_3_, ...), custom_call_target="tpu_custom_call" | custom-call | flops 21474836 | bytes 83886 | tf_op jit(solution)/shard_map/query_near/pallas_call | solution.py:303
  37.3 5.0 %query_far.2 = (bf16[128,1024]{1,0:T(8,128)(2,1)S(1)}, bf16[4096,1024]{1,0:T(8,128)(2,1)S(1)}) custom-call(s32[4]{0:T(128)S(1)} %pad_add_fusion.1.scalars_ref, f32[8,256]{1,0:T(8,128)S(1)} %get-tuple-element.39.refs_0_, f32[8,256]{1,0:T(8,128)S(1)} %collective-permute-done.refs_1_, f32[8,256]{1,0:T(8,128)S(1)} %collective-permute-done.1.refs_2_, ...), custom_call_target="tpu_custom_call" | custom-call | flops 10737418 | bytes 83886 | tf_op jit(solution)/shard_map/query_far/pallas_call | solution.py:398
  42.3 1.6 %collective-permute-done.11.refs_0_ = bf16[256,256]{1,0:T(8,128)(2,1)S(1)} collective-permute-done((bf16[256,256]{1,0:T(8,128)(2,1)S(1)}, bf16[256,256]{1,0:T(8,128)(2,1)S(1)}, u32[]{:S(2)}, u32[]{:S(2)}) %collective-permute-start.11) | collective-permute-done | bytes 131104 | tf_op jit(solution)/shard_map/ppermute | solution.py:568
  43.9 3.4 %attend_half.2.refs_0_ = bf16[128,1024]{1,0:T(8,128)(2,1)S(1)} custom-call(s32[21]{0:T(128)S(1)} %pad_add_fusion.pick_ref, bf16[128,1024]{1,0:T(8,128)(2,1)S(1)} %get-tuple-element.54.q_ref, s32[256,128]{1,0:T(8,128)S(1)} %broadcast_in_dim.39.qdoc_ref, s32[1,768]{1,0:T(1,128)S(1)} %broadcast_in_dim.37.kdoc_ref, ...), custom_call_target="tpu_custom_call" | custom-call | flops 6710886 | bytes 5242 | tf_op jit(solution)/shard_map/attend_half/pallas_call | solution.py:487
  48.7 1.2 %collective-permute-done.14.refs_2_ = bf16[96,2048]{1,0:T(8,128)(2,1)S(1)} collective-permute-done((bf16[96,2048]{1,0:T(8,128)(2,1)S(1)}, bf16[96,2048]{1,0:T(8,128)(2,1)S(1)}, u32[]{:S(2)}, u32[]{:S(2)}) %collective-permute-start.14) | collective-permute-done | bytes 393248 | tf_op jit(solution)/shard_map/ppermute | solution.py:561
  49.9 0.8 project.8
  51.3 1.3 %collective-permute-done.15.refs_2_ = bf16[32,2048]{1,0:T(8,128)(2,1)S(1)} collective-permute-done((bf16[32,2048]{1,0:T(8,128)(2,1)S(1)}, bf16[32,2048]{1,0:T(8,128)(2,1)S(1)}, u32[]{:S(2)}, u32[]{:S(2)}) %collective-permute-start.15) | collective-permute-done | bytes 131104 | tf_op jit(solution)/shard_map/ppermute | solution.py:561
  52.7 0.8 project.9
  53.5 4.3 %query_far.3 = (bf16[128,1024]{1,0:T(8,128)(2,1)S(1)}, bf16[1024,4096]{1,0:T(8,128)(2,1)S(1)}) custom-call(s32[4]{0:T(128)S(1)} %pad_add_fusion.1.scalars_ref, f32[8,256]{1,0:T(8,128)S(1)} %get-tuple-element.39.refs_0_, f32[8,256]{1,0:T(8,128)S(1)} %collective-permute-done.refs_1_, f32[8,256]{1,0:T(8,128)S(1)} %collective-permute-done.1.refs_2_, ...), custom_call_target="tpu_custom_call" | custom-call | flops 10737418 | bytes 83886 | tf_op jit(solution)/shard_map/query_far/pallas_call | solution.py:398
  57.9 3.4 %attend_half.3.refs_0_.refs_1_ = bf16[128,1024]{1,0:T(8,128)(2,1)S(1)} custom-call(s32[21]{0:T(128)S(1)} %pad_add_fusion.pick_ref, bf16[128,1024]{1,0:T(8,128)(2,1)S(1)} %get-tuple-element.64.q_ref, s32[256,128]{1,0:T(8,128)S(1)} %broadcast_in_dim.39.qdoc_ref, s32[1,768]{1,0:T(1,128)S(1)} %broadcast_in_dim.37.kdoc_ref, ...), custom_call_target="tpu_custom_call" | custom-call | flops 6710886 | bytes 5242 | tf_op jit(solution)/shard_map/attend_half/pallas_call | solution.py:487
  61.9 0.8 project.10
  62.7 1.3 %project.11 = bf16[256,2048]{1,0:T(8,128)(2,1)S(1)} custom-call(bf16[128,1024]{1,0:T(8,128)(2,1)S(1)} %attend_half.2.refs_0_, bf16[128,1024]{1,0:T(8,128)(2,1)S(1)} %attend_half.3.refs_0_.refs_1_, bf16[1024,4096]{1,0:T(8,128)(2,1)S(1)} %get-tuple-element.67.refs_2_), custom_call_target="tpu_custom_call" | custom-call | flops 10737418 | bytes 15728 | tf_op jit(solution)/shard_map/project/pallas_call | solution.py:537
  64.5 0.8 collective-permute-start.20
  65.4 2.1 %collective-permute-done.18.refs_2_ = bf16[128,2048]{1,0:T(8,128)(2,1)S(1)} collective-permute-done((bf16[128,2048]{1,0:T(8,128)(2,1)S(1)}, bf16[128,2048]{1,0:T(8,128)(2,1)S(1)}, u32[]{:S(2)}, u32[]{:S(2)}) %collective-permute-start.18) | collective-permute-done | bytes 524320 | tf_op jit(solution)/shard_map/ppermute | solution.py:561
  67.4 0.8 project.12
  68.2 0.9 %collective-permute-start.21 = (bf16[128,2048]{1,0:T(8,128)(2,1)S(1)}, bf16[128,2048]{1,0:T(8,128)(2,1)S(1)}, u32[]{:S(2)}, u32[]{:S(2)}) collective-permute-start(bf16[128,2048]{1,0:T(8,128)(2,1)S(1)} %project.12), channel_id=1, source_target_pairs={{0,8},{4,12},{8,0},{12,4},{1,9},{5,13},{9,1},{13,5},{2,10},{6,14},... | collective-permute-start | bytes 1572872 | tf_op jit(solution)/shard_map/ppermute | solution.py:565
  69.1 1.3 %project.13 = (f32[96,2048]{1,0:T(8,128)S(1)}, f32[32,2048]{1,0:T(8,128)S(1)}, f32[128,2048]{1,0:T(8,128)S(1)}) custom-call(bf16[128,1024]{1,0:T(8,128)(2,1)S(1)} %attend_half.2.refs_0_, bf16[128,1024]{1,0:T(8,128)(2,1)S(1)} %attend_half.3.refs_0_.refs_1_, bf16[1024,4096]{1,0:T(8,128)(2,1)S(1)} %get-tuple-element.67.refs_2_, ...), custom_call_target="tpu_custom_call" | custom-call | flops 10737418 | bytes 15728 | tf_op jit(solution)/shard_map/project/pallas_call | solution.py:537
  70.6 11.7 %collective-permute-done.21 = bf16[128,2048]{1,0:T(8,128)(2,1)S(1)} collective-permute-done((bf16[128,2048]{1,0:T(8,128)(2,1)S(1)}, bf16[128,2048]{1,0:T(8,128)(2,1)S(1)}, u32[]{:S(2)}, u32[]{:S(2)}) %collective-permute-start.21) | collective-permute-done | bytes 524320 | tf_op jit(solution)/shard_map/ppermute | solution.py:565
  82.4 1.1 %pad_maximum_fusion = bf16[256,2048]{1,0:T(8,128)(2,1)} fusion(bf16[128,2048]{1,0:T(8,128)(2,1)S(1)} %add_convert_fusion, bf16[32,2048]{1,0:T(8,128)(2,1)S(1)} %add_convert_fusion.2, bf16[96,2048]{1,0:T(8,128)(2,1)S(1)} %add_convert_fusion.1), kind=kLoop, calls=%fused_computation | loop fusion | flops 3145728 | bytes 2097152 | tf_op jit(solution)/shard_map/concatenate | solution.py:684
  (63 shorter events, 8.0 us)
Async XLA Ops:
  0.0 5.5 %copy-start = (bf16[1,2,512,512]{3,2,1,0:T(8,128)(2,1)S(1)}, bf16[1,2,512,512]{3,2,1,0:T(8,128)(2,1)}, u32[]{:S(2)}) copy-start(bf16[1,2,512,512]{3,2,1,0:T(8,128)(2,1)} %param.19) | copy-start | bytes 3145732
  0.0 31.2 %collective-permute-start.8 = (bf16[256,2048]{1,0:T(8,128)(2,1)}, bf16[256,2048]{1,0:T(8,128)(2,1)S(1)}, u32[]{:S(2)}, u32[]{:S(2)}) collective-permute-start(bf16[256,2048]{1,0:T(8,128)(2,1)} %x_ref.1), channel_id=1, source_target_pairs={{0,4},{4,0},{8,12},{12,8},{1,5},{5,1},{9,13},{13,9},{2,6},{6,2},{1... | collective-permute-start | bytes 3145736 | tf_op jit(solution)/shard_map/ppermute | solution.py:561
  2.7 5.9 %collective-permute-start.1 = (f32[8,256]{1,0:T(8,128)S(1)}, f32[8,256]{1,0:T(8,128)S(1)}, u32[]{:S(2)}, u32[]{:S(2)}) collective-permute-start(f32[8,256]{1,0:T(8,128)S(1)} %get-tuple-element.39.refs_0_), channel_id=1, source_target_pairs={{0,8},{4,12},{8,0},{12,4},{1,9},{5,13},{9,1},{13,5},{2,10},{6,14},... | collective-permute-start | bytes 24584 | tf_op jit(solution)/shard_map/ppermute | solution.py:565
  5.3 6.3 %collective-permute-start = (f32[8,256]{1,0:T(8,128)S(1)}, f32[8,256]{1,0:T(8,128)S(1)}, u32[]{:S(2)}, u32[]{:S(2)}) collective-permute-start(f32[8,256]{1,0:T(8,128)S(1)} %get-tuple-element.39.refs_0_), channel_id=1, source_target_pairs={{0,4},{4,0},{8,12},{12,8},{1,5},{5,1},{9,13},{13,9},{2,6},{6,2},{1... | collective-permute-start | bytes 24584 | tf_op jit(solution)/shard_map/ppermute | solution.py:561
  5.5 10.5 %collective-permute-start.3 = (bf16[2,512,128]{2,1,0:T(8,128)(2,1)S(1)}, bf16[2,512,128]{2,1,0:T(8,128)(2,1)S(1)}, u32[]{:S(2)}, u32[]{:S(2)}) collective-permute-start(bf16[2,512,128]{2,1,0:T(8,128)(2,1)S(1)} %dynamic-slice_bitcast_fusion.refs_3_), channel_id=1, source_target_pairs={{0,1},{1,2},{2,3},{3,0},{4,5},{5,6},{6,7},{7,4},{8,9},{9,10},{10,1... | collective-permute-start | bytes 786440 | tf_op jit(solution)/shard_map/ppermute | solution.py:568
  7.2 14.2 %collective-permute-start.5 = (bf16[128,2048]{1,0:T(8,128)(2,1)}, bf16[128,2048]{1,0:T(8,128)(2,1)}, u32[]{:S(2)}, u32[]{:S(2)}) collective-permute-start(bf16[128,2048]{1,0:T(8,128)(2,1)} %get-tuple-element.48), channel_id=1, source_target_pairs={{0,8},{4,12},{8,0},{12,4},{1,9},{5,13},{9,1},{13,5},{2,10},{6,14},... | collective-permute-start | bytes 1572872 | tf_op jit(solution)/shard_map/ppermute | solution.py:565
  8.6 3.1 %collective-permute-start.2 = (f32[8,256]{1,0:T(8,128)S(1)}, f32[8,256]{1,0:T(8,128)S(1)}, u32[]{:S(2)}, u32[]{:S(2)}) collective-permute-start(f32[8,256]{1,0:T(8,128)S(1)} %collective-permute-done.1.refs_2_), channel_id=1, source_target_pairs={{0,4},{4,0},{8,12},{12,8},{1,5},{5,1},{9,13},{13,9},{2,6},{6,2},{1... | collective-permute-start | bytes 24584 | tf_op jit(solution)/shard_map/ppermute | solution.py:561
  11.6 10.4 %copy-start.4 = (s32[16,1]{0,1:T(1,128)S(1)}, s32[16,1]{0,1:T(1,128)}, u32[]{:S(2)}) copy-start(s32[16,1]{0,1:T(1,128)} %param.17) | copy-start | bytes 196
  11.7 10.4 %copy-start.5 = (s32[4]{0:T(128)S(1)}, s32[4]{0:T(128)}, u32[]{:S(2)}) copy-start(s32[4]{0:T(128)} %param.18) | copy-start | bytes 52
  16.0 10.3 %copy-start.2 = (bf16[2,512,128]{2,1,0:T(8,128)(2,1)}, bf16[2,512,128]{2,1,0:T(8,128)(2,1)S(1)}, u32[]{:S(2)}) copy-start(bf16[2,512,128]{2,1,0:T(8,128)(2,1)S(1)} %collective-permute-done.3.refs_4_) | copy-start | bytes 786436
  16.0 5.4 %collective-permute-start.4 = (bf16[2,256,256]{2,1,0:T(8,128)(2,1)S(1)}, bf16[2,256,256]{2,1,0:T(8,128)(2,1)S(1)}, u32[]{:S(2)}, u32[]{:S(2)}) collective-permute-start(bf16[2,256,256]{2,1,0:T(8,128)(2,1)S(1)} %get-tuple-element.47), channel_id=1, source_target_pairs={{0,4},{4,0},{8,12},{12,8},{1,5},{5,1},{9,13},{13,9},{2,6},{6,2},{1... | collective-permute-start | bytes 786440 | tf_op jit(solution)/shard_map/ppermute | solution.py:561
  16.6 10.6 %collective-permute-start.6 = (bf16[2,512,128]{2,1,0:T(8,128)(2,1)S(1)}, bf16[2,512,128]{2,1,0:T(8,128)(2,1)S(1)}, u32[]{:S(2)}, u32[]{:S(2)}) collective-permute-start(bf16[2,512,128]{2,1,0:T(8,128)(2,1)S(1)} %collective-permute-done.3.refs_4_), channel_id=1, source_target_pairs={{0,1},{1,2},{2,3},{3,0},{4,5},{5,6},{6,7},{7,4},{8,9},{9,10},{10,1... | collective-permute-start | bytes 786440 | tf_op jit(solution)/shard_map/ppermute | solution.py:568
  21.4 5.8 %collective-permute-start.7 = (bf16[256,256]{1,0:T(8,128)(2,1)S(1)}, bf16[256,256]{1,0:T(8,128)(2,1)S(1)}, u32[]{:S(2)}, u32[]{:S(2)}) collective-permute-start(bf16[256,256]{1,0:T(8,128)(2,1)S(1)} %fusion.1), channel_id=1, source_target_pairs={{0,8},{4,12},{8,0},{12,4},{1,9},{5,13},{9,1},{13,5},{2,10},{6,14},... | collective-permute-start | bytes 393224 | tf_op jit(solution)/shard_map/ppermute | solution.py:565
  22.1 15.2 %collective-permute-start.9 = (bf16[128,2048]{1,0:T(8,128)(2,1)}, bf16[128,2048]{1,0:T(8,128)(2,1)S(1)}, u32[]{:S(2)}, u32[]{:S(2)}) collective-permute-start(bf16[128,2048]{1,0:T(8,128)(2,1)} %collective-permute-done.5.refs_6_), channel_id=1, source_target_pairs={{0,4},{4,0},{8,12},{12,8},{1,5},{5,1},{9,13},{13,9},{2,6},{6,2},{1... | collective-permute-start | bytes 1572872 | tf_op jit(solution)/shard_map/ppermute | solution.py:561
  22.3 5.1 %copy-start.6 = (bf16[128,2048]{1,0:T(8,128)(2,1)S(1)}, bf16[128,2048]{1,0:T(8,128)(2,1)}, u32[]{:S(2)}) copy-start(bf16[128,2048]{1,0:T(8,128)(2,1)} %get-tuple-element.57) | copy-start | bytes 1572868
  27.3 20.0 %collective-permute-start.13 = (bf16[128,2048]{1,0:T(8,128)(2,1)S(1)}, bf16[128,2048]{1,0:T(8,128)(2,1)S(1)}, u32[]{:S(2)}, u32[]{:S(2)}) collective-permute-start(bf16[128,2048]{1,0:T(8,128)(2,1)S(1)} %copy-done.6), channel_id=1, source_target_pairs={{0,8},{4,12},{8,0},{12,4},{1,9},{5,13},{9,1},{13,5},{2,10},{6,14},... | collective-permute-start | bytes 1572872 | tf_op jit(solution)/shard_map/ppermute | solution.py:565
  28.1 8.6 %collective-permute-start.10 = (bf16[256,256]{1,0:T(8,128)(2,1)S(1)}, bf16[256,256]{1,0:T(8,128)(2,1)S(1)}, u32[]{:S(2)}, u32[]{:S(2)}) collective-permute-start(bf16[256,256]{1,0:T(8,128)(2,1)S(1)} %kv_final.1.refs_2_), channel_id=1, source_target_pairs={{0,1},{1,2},{2,3},{3,0},{4,5},{5,6},{6,7},{7,4},{8,9},{9,10},{10,1... | collective-permute-start | bytes 393224 | tf_op jit(solution)/shard_map/ppermute | solution.py:568
  29.7 12.6 %collective-permute-start.12 = (bf16[2,512,128]{2,1,0:T(8,128)(2,1)S(1)}, bf16[2,512,128]{2,1,0:T(8,128)(2,1)S(1)}, u32[]{:S(2)}, u32[]{:S(2)}) collective-permute-start(bf16[2,512,128]{2,1,0:T(8,128)(2,1)S(1)} %collective-permute-done.6.refs_5_), channel_id=1, source_target_pairs={{0,1},{1,2},{2,3},{3,0},{4,5},{5,6},{6,7},{7,4},{8,9},{9,10},{10,1... | collective-permute-start | bytes 786440 | tf_op jit(solution)/shard_map/ppermute | solution.py:568
  36.7 7.2 %copy-start.3 = (bf16[2,512,128]{2,1,0:T(8,128)(2,1)S(1)}, bf16[2,512,128]{2,1,0:T(8,128)(2,1)}, u32[]{:S(2)}) copy-start(bf16[2,512,128]{2,1,0:T(8,128)(2,1)} %copy-done.2) | copy-start | bytes 786436
  36.7 7.2 %collective-permute-start.11 = (bf16[256,256]{1,0:T(8,128)(2,1)S(1)}, bf16[256,256]{1,0:T(8,128)(2,1)S(1)}, u32[]{:S(2)}, u32[]{:S(2)}) collective-permute-start(bf16[256,256]{1,0:T(8,128)(2,1)S(1)} %collective-permute-done.10.refs_1_), channel_id=1, source_target_pairs={{0,1},{1,2},{2,3},{3,0},{4,5},{5,6},{6,7},{7,4},{8,9},{9,10},{10,1... | collective-permute-start | bytes 393224 | tf_op jit(solution)/shard_map/ppermute | solution.py:568
  48.1 1.8 %collective-permute-start.14 = (bf16[96,2048]{1,0:T(8,128)(2,1)S(1)}, bf16[96,2048]{1,0:T(8,128)(2,1)S(1)}, u32[]{:S(2)}, u32[]{:S(2)}) collective-permute-start(bf16[96,2048]{1,0:T(8,128)(2,1)S(1)} %get-tuple-element.59), channel_id=1, source_target_pairs={{0,4},{4,0},{8,12},{12,8},{1,5},{5,1},{9,13},{13,9},{2,6},{6,2},{1... | collective-permute-start | bytes 1179656 | tf_op jit(solution)/shard_map/ppermute | solution.py:561
  48.2 5.4 %collective-permute-start.16 = (bf16[128,2048]{1,0:T(8,128)(2,1)S(1)}, bf16[128,2048]{1,0:T(8,128)(2,1)S(1)}, u32[]{:S(2)}, u32[]{:S(2)}) collective-permute-start(bf16[128,2048]{1,0:T(8,128)(2,1)S(1)} %collective-permute-done.13.refs_6_), channel_id=1, source_target_pairs={{0,4},{4,0},{8,12},{12,8},{1,5},{5,1},{9,13},{13,9},{2,6},{6,2},{1... | collective-permute-start | bytes 1572872 | tf_op jit(solution)/shard_map/ppermute | solution.py:561
  50.7 11.2 %collective-permute-start.17 = (bf16[96,2048]{1,0:T(8,128)(2,1)S(1)}, bf16[96,2048]{1,0:T(8,128)(2,1)S(1)}, u32[]{:S(2)}, u32[]{:S(2)}) collective-permute-start(bf16[96,2048]{1,0:T(8,128)(2,1)S(1)} %project.8), channel_id=1, source_target_pairs={{0,8},{4,12},{8,0},{12,4},{1,9},{5,13},{9,1},{13,5},{2,10},{6,14},... | collective-permute-start | bytes 1179656 | tf_op jit(solution)/shard_map/ppermute | solution.py:565
  51.3 1.3 %collective-permute-start.15 = (bf16[32,2048]{1,0:T(8,128)(2,1)S(1)}, bf16[32,2048]{1,0:T(8,128)(2,1)S(1)}, u32[]{:S(2)}, u32[]{:S(2)}) collective-permute-start(bf16[32,2048]{1,0:T(8,128)(2,1)S(1)} %get-tuple-element.60), channel_id=1, source_target_pairs={{0,4},{4,0},{8,12},{12,8},{1,5},{5,1},{9,13},{13,9},{2,6},{6,2},{1... | collective-permute-start | bytes 393224 | tf_op jit(solution)/shard_map/ppermute | solution.py:561
  63.9 5.1 %collective-permute-start.19 = (bf16[256,2048]{1,0:T(8,128)(2,1)S(1)}, bf16[256,2048]{1,0:T(8,128)(2,1)S(1)}, u32[]{:S(2)}, u32[]{:S(2)}) collective-permute-start(bf16[256,2048]{1,0:T(8,128)(2,1)S(1)} %project.11), channel_id=1, source_target_pairs={{0,4},{4,0},{8,12},{12,8},{1,5},{5,1},{9,13},{13,9},{2,6},{6,2},{1... | collective-permute-start | bytes 3145736 | tf_op jit(solution)/shard_map/ppermute | solution.py:561
  64.0 3.4 %collective-permute-start.18 = (bf16[128,2048]{1,0:T(8,128)(2,1)S(1)}, bf16[128,2048]{1,0:T(8,128)(2,1)S(1)}, u32[]{:S(2)}, u32[]{:S(2)}) collective-permute-start(bf16[128,2048]{1,0:T(8,128)(2,1)S(1)} %project.10), channel_id=1, source_target_pairs={{0,4},{4,0},{8,12},{12,8},{1,5},{5,1},{9,13},{13,9},{2,6},{6,2},{1... | collective-permute-start | bytes 1572872 | tf_op jit(solution)/shard_map/ppermute | solution.py:561
  64.5 5.9 %collective-permute-start.20 = (bf16[32,2048]{1,0:T(8,128)(2,1)S(1)}, bf16[32,2048]{1,0:T(8,128)(2,1)S(1)}, u32[]{:S(2)}, u32[]{:S(2)}) collective-permute-start(bf16[32,2048]{1,0:T(8,128)(2,1)S(1)} %project.9), channel_id=1, source_target_pairs={{0,8},{4,12},{8,0},{12,4},{1,9},{5,13},{9,1},{13,5},{2,10},{6,14},... | collective-permute-start | bytes 393224 | tf_op jit(solution)/shard_map/ppermute | solution.py:565
  68.2 14.0 %collective-permute-start.21 = (bf16[128,2048]{1,0:T(8,128)(2,1)S(1)}, bf16[128,2048]{1,0:T(8,128)(2,1)S(1)}, u32[]{:S(2)}, u32[]{:S(2)}) collective-permute-start(bf16[128,2048]{1,0:T(8,128)(2,1)S(1)} %project.12), channel_id=1, source_target_pairs={{0,8},{4,12},{8,0},{12,4},{1,9},{5,13},{9,1},{13,5},{2,10},{6,14},... | collective-permute-start | bytes 1572872 | tf_op jit(solution)/shard_map/ppermute | solution.py:565
  82.2 1.4 %copy-start.1 = (bf16[1,2,512,512]{3,2,1,0:T(8,128)(2,1)S(1)}, bf16[1,2,512,512]{3,2,1,0:T(8,128)(2,1)}, u32[]{:S(2)}) copy-start(bf16[1,2,512,512]{3,2,1,0:T(8,128)(2,1)} %param.19) | copy-start | bytes 3145732

commit v4 on v3

--- a/solution.py
+++ b/solution.py
@@ -507,7 +507,7 @@
     )(pick, query, q_doc, k_doc, *kv, *memories)
 
 
-def project(attended, held, block, width, sizes, kind=bf16, added=(), begin=0):
+def project(attended, held, block, width, sizes, kind=bf16, added=(), begin=0, spacer=()):
     depth = attended[0].shape[1]
     tile = min(width, 512)
     rows = sum(sizes)
@@ -527,7 +527,7 @@
                 first += a_ref.shape[0]
             total = jnp.concatenate(pieces, 0)
             if added:
-                terms = [ref[:, part].astype(f32) for ref in refs[len(attended) + 1 : -len(sizes)]]
+                terms = [ref[:, part].astype(f32) for ref in refs[len(attended) + 1 :][: len(added)]]
                 total = total + jnp.concatenate(terms, 0)
             first = 0
             for size, out_ref in zip(sizes, out_refs):
@@ -537,12 +537,12 @@
     return pl.pallas_call(
         body,
         out_shape=[jax.ShapeDtypeStruct((size, width), kind) for size in sizes],
-        in_specs=[VMEM] * (len(attended) + 1 + len(added)),
+        in_specs=[VMEM] * (len(attended) + 1 + len(added)) + [ANY] * len(spacer),
         out_specs=[VMEM] * len(sizes),
         compiler_params=params(SCOPED),
         cost_estimate=cost(2 * rows * depth * width, 2 * rows * (depth + width)),
         name="project",
-    )(*attended, resident(held), *added)
+    )(*attended, resident(held), *added, *spacer)
 
 
 def on_device(tokens, norm_gain, w_query, w_key, w_value, w_out, doc_ids, assign, res_len, res_mem):
@@ -639,8 +639,7 @@
     for at in range(back):
         kv.insert(0, up(after(kv[0], near) if at == 1 else kv[0]))
 
-    early = half_rows * 3 // 4 // 16 * 16
-    cuts = [early, half_rows - early], [half_rows]
+    cuts = [half_rows], [half_rows]
     weights, ready, attended, outs = [w_query], [near], [], []
     for half in range(HALVES):
         if half == 1:
@@ -654,22 +653,24 @@
         weights = [w_held, w_out]
         one = attend_half(half, pick, query, q_doc, k_doc, kv, memories)
         attended.append(one)
-        one = after(one, *(last_arrived if half == 0 else outs[0]))
+        one = after(one, *(last_arrived if half == 0 else ()))
         ready, sums, begin = [], [[] for _ in cuts[half]], 0
-        others = []
+        others, spacer = [], []
         for ahead in away:
             block = 2 * (ahead - 1)
             sent = project([one], w_out_far, block, width, cuts[half])
             last = after(attended[-1], *sent)
             others.append([to_core(x) for x in sent])
         if half == HALVES - 1:
-            terms = project(attended[:-1] + [last], w_held, 0, width, [rows_dev])
+            terms = project(attended[:-1] + [last], w_held, 0, width, [half_rows // 2] * (2 * HALVES))
             one = after(one, *terms)
+            spacer = [to_core(after(memories[0], *outs[0], *terms))]
             terms = [to_core(x) for x in terms]
         for at, size in enumerate(cuts[half]):
             for ahead, other in zip(away, others):
                 (pair,) = project(
-                    [one], w_out_far, 2 * ahead - 1, width, [size], added=[other[at]], begin=begin
+                    [one], w_out_far, 2 * ahead - 1, width, [size], added=[other[at]], begin=begin,
+                    spacer=spacer,
                 )
                 ready.append(pair)
                 sums[at].append(to_chip(pair, ahead))

time: 83.9 us -> 82.8 us (0.987)
  Pallas kernels: 38.7 us -> 37.8 us
    ppermute x7 -> x6, waiting for transfers between devices: 17 us -> 20 us  [to_chip(): return lax.ppermute(x, 'tensor', pairs)]
    ppermute x10 -> x13, waiting for transfers between devices: 4.65 us -> 2 us  [to_core(): return lax.ppermute(x, 'tensor', [(i, i ^ 1) for i in range(n_tensor)])]
    ppermute x7 -> x6, starting transfers between devices: 6.87 us -> 5.8 us  [to_chip(): return lax.ppermute(x, 'tensor', pairs)]
    pallas_call x7 -> x6, Pallas kernels: 6.48 us -> 5.65 us  [project(): pl.pallas_call(body, out_shape=[jax.ShapeDtypeStruct((size, width), kind)...]
    ppermute x10 -> x13, starting transfers between devices: 1.76 us -> 2.28 us  [to_core(): return lax.ppermute(x, 'tensor', [(i, i ^ 1) for i in range(n_tensor)])]
  transfers between devices with their start and end apart: 22 -> 24, of which waited for: 9 -> 9; matrix products, arithmetic and copies ran while one was open for 3% -> 3% of each run, Pallas kernels for 43% -> 45%
where the time goes in v4:
time: 82.8 us; the launch traced here: 82.6 us
  Pallas kernels  37.8 us (46%)
  waiting for transfers between devices  26.8 us (32%)
  starting transfers between devices  13.5 us (16%)
  other arithmetic  3.03 us (4%)
  local copies, waits for them, and re-layouts  1.06 us (1%)
    ppermute x6, waiting for transfers between devices, to_chip(): return lax.ppermute(x, 'tensor', pairs)  20 us
    pallas_call x2, Pallas kernels, query_far(): pl.pallas_call(body, out_shape=[query, placed(pltpu.VMEM, held_shape)], g...  9.31 us
    pallas_call x2, Pallas kernels, attend_half(): pl.pallas_call(functools.partial(attend_kernel, half, len(memories)), out...  6.78 us
    ppermute x6, starting transfers between devices, to_chip(): return lax.ppermute(x, 'tensor', pairs)  5.8 us
    pallas_call x6, Pallas kernels, project(): pl.pallas_call(body, out_shape=[jax.ShapeDtypeStruct((size, width), kind)...  5.65 us
    ppermute x5, starting transfers between devices, up(): lax.ppermute(x, 'rows', [(i, (i + 1) % n_rows) for i in range(n_rows)])  5.45 us
    pallas_call x1, Pallas kernels, query_near(): pl.pallas_call(body, out_shape=placed(pltpu.VMEM, (rows, columns), f32),...  5.43 us
    ppermute x5, waiting for transfers between devices, up(): lax.ppermute(x, 'rows', [(i, (i + 1) % n_rows) for i in range(n_rows)])  4.76 us
  transfers between devices with their start and end apart: 24, of which 9 were waited for; matrix products, arithmetic and copies ran while one was open for 3% of the time, Pallas kernels for 45%

profile of v4, /device:TPU:0, one launch (start us, length us, event | category | flops | bytes accessed | tf_op | source)
XLA Modules:
  0.0 82.6 jit_solution(3384628119300836919)
XLA Ops:
  0.5 2.2 %prep.1 = (bf16[128,2048]{1,0:T(8,128)(2,1)}, bf16[128,2048]{1,0:T(8,128)(2,1)}, bf16[256,2048]{1,0:T(8,128)(2,1)S(1)}, f32[8,256]{1,0:T(8,128)S(1)}) custom-call(bf16[256,2048]{1,0:T(8,128)(2,1)} %x_ref.1), custom_call_target="tpu_custom_call" | custom-call | flops 10485 | bytes 20971 | tf_op jit(solution)/shard_map/prep/pallas_call | solution.py:106
  2.7 2.7 %collective-permute-start.1 = (f32[8,256]{1,0:T(8,128)S(1)}, f32[8,256]{1,0:T(8,128)S(1)}, u32[]{:S(2)}, u32[]{:S(2)}) collective-permute-start(f32[8,256]{1,0:T(8,128)S(1)} %get-tuple-element.40.refs_0_), channel_id=1, source_target_pairs={{0,8},{4,12},{8,0},{12,4},{1,9},{5,13},{9,1},{13,5},{2,10},{6,14},... | collective-permute-start | bytes 24584 | tf_op jit(solution)/shard_map/ppermute | solution.py:565
  5.5 1.6 %collective-permute-start.3 = (bf16[2,512,128]{2,1,0:T(8,128)(2,1)S(1)}, bf16[2,512,128]{2,1,0:T(8,128)(2,1)S(1)}, u32[]{:S(2)}, u32[]{:S(2)}) collective-permute-start(bf16[2,512,128]{2,1,0:T(8,128)(2,1)S(1)} %dynamic-slice_bitcast_fusion.refs_3_), channel_id=1, source_target_pairs={{0,1},{1,2},{2,3},{3,0},{4,5},{5,6},{6,7},{7,4},{8,9},{9,10},{10,1... | collective-permute-start | bytes 786440 | tf_op jit(solution)/shard_map/ppermute | solution.py:568
  7.7 0.8 pad_dynamic-slice_fusion
  8.7 0.7 broadcast_in_dim.43
  9.4 2.2 %load.1 = (bf16[2048,512]{1,0:T(8,128)(2,1)S(1)}, bf16[2048,512]{1,0:T(8,128)(2,1)S(1)}) custom-call(bf16[2048,512]{1,0:T(8,128)(2,1)} %refs_0_, bf16[2048,512]{1,0:T(8,128)(2,1)} %refs_1_.1), custom_call_target="tpu_custom_call" | custom-call | bytes 41943 | tf_op jit(solution)/shard_map/load/pallas_call | solution.py:143
  11.7 2.1 %kv_partial.1 = (bf16[2,256,256]{2,1,0:T(8,128)(2,1)S(1)}, bf16[2,256,256]{2,1,0:T(8,128)(2,1)S(1)}) custom-call(s32[5]{0:T(128)S(1)} %pad_add_fusion.4.scalars_ref, f32[8,256]{1,0:T(8,128)S(1)} %get-tuple-element.40.refs_0_, f32[8,256]{1,0:T(8,128)S(1)} %collective-permute-done.refs_1_, f32[8,256]{1,0:T(8,128)S(1)} %collective-permute-done.1.refs_2_, ...), custom_call_target="tpu_custom_call" | custom-call | flops 10737418 | bytes 10485 | tf_op jit(solution)/shard_map/kv_partial/pallas_call | solution.py:181
  13.7 2.3 %collective-permute-done.3.refs_4_ = bf16[2,512,128]{2,1,0:T(8,128)(2,1)S(1)} collective-permute-done((bf16[2,512,128]{2,1,0:T(8,128)(2,1)S(1)}, bf16[2,512,128]{2,1,0:T(8,128)(2,1)S(1)}, u32[]{:S(2)}, u32[]{:S(2)}) %collective-permute-start.3) | collective-permute-done | bytes 262176 | tf_op jit(solution)/shard_map/ppermute | solution.py:568
  16.7 4.7 %collective-permute-done.5.refs_6_ = bf16[128,2048]{1,0:T(8,128)(2,1)} collective-permute-done((bf16[128,2048]{1,0:T(8,128)(2,1)}, bf16[128,2048]{1,0:T(8,128)(2,1)}, u32[]{:S(2)}, u32[]{:S(2)}) %collective-permute-start.5) | collective-permute-done | bytes 524320 | tf_op jit(solution)/shard_map/ppermute | solution.py:565
  22.3 4.0 %load_columns.1.refs_1_ = bf16[1024,4096]{1,0:T(8,128)(2,1)S(1)} custom-call(s32[2]{0:T(128)S(1)} %pad_add_fusion.3.scalars_ref, bf16[1024,8192]{1,0:T(8,128)(2,1)} %refs_11_.1), custom_call_target="tpu_custom_call" | custom-call | bytes 83886 | tf_op jit(solution)/shard_map/load_columns/pallas_call | solution.py:251
  26.4 0.9 %collective-permute-done.6.refs_5_ = bf16[2,512,128]{2,1,0:T(8,128)(2,1)S(1)} collective-permute-done((bf16[2,512,128]{2,1,0:T(8,128)(2,1)S(1)}, bf16[2,512,128]{2,1,0:T(8,128)(2,1)S(1)}, u32[]{:S(2)}, u32[]{:S(2)}) %collective-permute-start.6) | collective-permute-done | bytes 262176 | tf_op jit(solution)/shard_map/ppermute | solution.py:568
  27.3 0.7 collective-permute-start.13
  28.1 1.6 %collective-permute-start.10 = (bf16[256,256]{1,0:T(8,128)(2,1)S(1)}, bf16[256,256]{1,0:T(8,128)(2,1)S(1)}, u32[]{:S(2)}, u32[]{:S(2)}) collective-permute-start(bf16[256,256]{1,0:T(8,128)(2,1)S(1)} %kv_final.1.refs_2_), channel_id=1, source_target_pairs={{0,1},{1,2},{2,3},{3,0},{4,5},{5,6},{6,7},{7,4},{8,9},{9,10},{10,1... | collective-permute-start | bytes 393224 | tf_op jit(solution)/shard_map/ppermute | solution.py:568
  29.7 1.6 %collective-permute-start.12 = (bf16[2,512,128]{2,1,0:T(8,128)(2,1)S(1)}, bf16[2,512,128]{2,1,0:T(8,128)(2,1)S(1)}, u32[]{:S(2)}, u32[]{:S(2)}) collective-permute-start(bf16[2,512,128]{2,1,0:T(8,128)(2,1)S(1)} %collective-permute-done.6.refs_5_), channel_id=1, source_target_pairs={{0,1},{1,2},{2,3},{3,0},{4,5},{5,6},{6,7},{7,4},{8,9},{9,10},{10,1... | collective-permute-start | bytes 786440 | tf_op jit(solution)/shard_map/ppermute | solution.py:568
  31.2 5.4 %query_near.1.refs_5_ = f32[256,1024]{1,0:T(8,128)S(1)} custom-call(s32[2]{0:T(128)S(1)} %pad_add_fusion.2.scalars_ref, f32[8,256]{1,0:T(8,128)S(1)} %get-tuple-element.40.refs_0_, f32[8,256]{1,0:T(8,128)S(1)} %collective-permute-done.refs_1_, f32[8,256]{1,0:T(8,128)S(1)} %collective-permute-done.1.refs_2_, f32[8,256]{1,0:T(8,128)S(1)} %collective-permute-done.2.refs_3_, ...), custom_call_target="tpu_custom_call" | custom-call | flops 21474836 | bytes 83886 | tf_op jit(solution)/shard_map/query_near/pallas_call | solution.py:303
  37.3 5.0 %query_far.2 = (bf16[128,1024]{1,0:T(8,128)(2,1)S(1)}, bf16[4096,1024]{1,0:T(8,128)(2,1)S(1)}) custom-call(s32[4]{0:T(128)S(1)} %pad_add_fusion.1.scalars_ref, f32[8,256]{1,0:T(8,128)S(1)} %get-tuple-element.40.refs_0_, f32[8,256]{1,0:T(8,128)S(1)} %collective-permute-done.refs_1_, f32[8,256]{1,0:T(8,128)S(1)} %collective-permute-done.1.refs_2_, ...), custom_call_target="tpu_custom_call" | custom-call | flops 10737418 | bytes 83886 | tf_op jit(solution)/shard_map/query_far/pallas_call | solution.py:398
  42.3 1.6 %collective-permute-done.11.refs_0_ = bf16[256,256]{1,0:T(8,128)(2,1)S(1)} collective-permute-done((bf16[256,256]{1,0:T(8,128)(2,1)S(1)}, bf16[256,256]{1,0:T(8,128)(2,1)S(1)}, u32[]{:S(2)}, u32[]{:S(2)}) %collective-permute-start.11) | collective-permute-done | bytes 131104 | tf_op jit(solution)/shard_map/ppermute | solution.py:568
  43.9 3.4 %attend_half.2.refs_0_ = bf16[128,1024]{1,0:T(8,128)(2,1)S(1)} custom-call(s32[21]{0:T(128)S(1)} %pad_add_fusion.pick_ref, bf16[128,1024]{1,0:T(8,128)(2,1)S(1)} %get-tuple-element.55.q_ref, s32[256,128]{1,0:T(8,128)S(1)} %broadcast_in_dim.39.qdoc_ref, s32[1,768]{1,0:T(1,128)S(1)} %broadcast_in_dim.37.kdoc_ref, ...), custom_call_target="tpu_custom_call" | custom-call | flops 6710886 | bytes 5242 | tf_op jit(solution)/shard_map/attend_half/pallas_call | solution.py:487
  47.3 0.7 project.6
  48.7 1.4 %collective-permute-done.14.refs_2_ = bf16[128,2048]{1,0:T(8,128)(2,1)S(1)} collective-permute-done((bf16[128,2048]{1,0:T(8,128)(2,1)S(1)}, bf16[128,2048]{1,0:T(8,128)(2,1)S(1)}, u32[]{:S(2)}, u32[]{:S(2)}) %collective-permute-start.14) | collective-permute-done | bytes 524320 | tf_op jit(solution)/shard_map/ppermute | solution.py:561
  50.1 0.8 project.7
  50.8 0.6 collective-permute-start.17
  51.5 4.3 %query_far.3 = (bf16[128,1024]{1,0:T(8,128)(2,1)S(1)}, bf16[1024,4096]{1,0:T(8,128)(2,1)S(1)}) custom-call(s32[4]{0:T(128)S(1)} %pad_add_fusion.1.scalars_ref, f32[8,256]{1,0:T(8,128)S(1)} %get-tuple-element.40.refs_0_, f32[8,256]{1,0:T(8,128)S(1)} %collective-permute-done.refs_1_, f32[8,256]{1,0:T(8,128)S(1)} %collective-permute-done.1.refs_2_, ...), custom_call_target="tpu_custom_call" | custom-call | flops 10737418 | bytes 83886 | tf_op jit(solution)/shard_map/query_far/pallas_call | solution.py:398
  55.8 3.4 %attend_half.3.refs_0_.refs_1_ = bf16[128,1024]{1,0:T(8,128)(2,1)S(1)} custom-call(s32[21]{0:T(128)S(1)} %pad_add_fusion.pick_ref, bf16[128,1024]{1,0:T(8,128)(2,1)S(1)} %get-tuple-element.63.q_ref, s32[256,128]{1,0:T(8,128)S(1)} %broadcast_in_dim.39.qdoc_ref, s32[1,768]{1,0:T(1,128)S(1)} %broadcast_in_dim.37.kdoc_ref, ...), custom_call_target="tpu_custom_call" | custom-call | flops 6710886 | bytes 5242 | tf_op jit(solution)/shard_map/attend_half/pallas_call | solution.py:487
  59.2 0.8 project.8
  60.1 1.3 %project.9 = (bf16[64,2048]{1,0:T(8,128)(2,1)S(1)}, bf16[64,2048]{1,0:T(8,128)(2,1)S(1)}, bf16[64,2048]{1,0:T(8,128)(2,1)S(1)}, bf16[64,2048]{1,0:T(8,128)(2,1)S(1)}) custom-call(bf16[128,1024]{1,0:T(8,128)(2,1)S(1)} %attend_half.2.refs_0_, bf16[128,1024]{1,0:T(8,128)(2,1)S(1)} %attend_half.3.refs_0_.refs_1_, bf16[1024,4096]{1,0:T(8,128)(2,1)S(1)} %get-tuple-element.65.refs_2_), custom_call_target="tpu_custom_call" | custom-call | flops 10737418 | bytes 15728 | tf_op jit(solution)/shard_map/project/pallas_call | solution.py:537
  61.4 3.5 %collective-permute-done.17 = bf16[128,2048]{1,0:T(8,128)(2,1)S(1)} collective-permute-done((bf16[128,2048]{1,0:T(8,128)(2,1)S(1)}, bf16[128,2048]{1,0:T(8,128)(2,1)S(1)}, u32[]{:S(2)}, u32[]{:S(2)}) %collective-permute-start.17) | collective-permute-done | bytes 524320 | tf_op jit(solution)/shard_map/ppermute | solution.py:565
  66.4 0.8 project.10
  67.2 0.6 collective-permute-start.23
  67.9 1.3 %project.11 = (f32[128,2048]{1,0:T(8,128)S(1)}, f32[128,2048]{1,0:T(8,128)S(1)}) custom-call(bf16[128,1024]{1,0:T(8,128)(2,1)S(1)} %attend_half.2.refs_0_, bf16[128,1024]{1,0:T(8,128)(2,1)S(1)} %attend_half.3.refs_0_.refs_1_, bf16[1024,4096]{1,0:T(8,128)(2,1)S(1)} %get-tuple-element.65.refs_2_, bf16[64,2048]{1,0:T(8,128)(2,1)S(1)} %collective-permute-done.19.refs_3_, ...), custom_call_target="tpu_custom_call" | custom-call | flops 10737418 | bytes 15728 | tf_op jit(solution)/shard_map/project/pallas_call | solution.py:537
  69.4 11.8 %collective-permute-done.23 = bf16[128,2048]{1,0:T(8,128)(2,1)S(1)} collective-permute-done((bf16[128,2048]{1,0:T(8,128)(2,1)S(1)}, bf16[128,2048]{1,0:T(8,128)(2,1)S(1)}, u32[]{:S(2)}, u32[]{:S(2)}) %collective-permute-start.23) | collective-permute-done | bytes 524320 | tf_op jit(solution)/shard_map/ppermute | solution.py:565
  81.4 1.1 %pad_maximum_fusion = bf16[256,2048]{1,0:T(8,128)(2,1)} fusion(bf16[128,2048]{1,0:T(8,128)(2,1)S(1)} %add_convert_fusion, bf16[128,2048]{1,0:T(8,128)(2,1)S(1)} %add_convert_fusion.1), kind=kLoop, calls=%fused_computation | loop fusion | flops 2097152 | bytes 2097152 | tf_op jit(solution)/shard_map/concatenate | solution.py:685
  (65 shorter events, 6.3 us)
Async XLA Ops:
  0.0 5.5 %copy-start = (bf16[1,2,512,512]{3,2,1,0:T(8,128)(2,1)S(1)}, bf16[1,2,512,512]{3,2,1,0:T(8,128)(2,1)}, u32[]{:S(2)}) copy-start(bf16[1,2,512,512]{3,2,1,0:T(8,128)(2,1)} %param.19) | copy-start | bytes 3145732
  0.0 31.2 %collective-permute-start.8 = (bf16[256,2048]{1,0:T(8,128)(2,1)}, bf16[256,2048]{1,0:T(8,128)(2,1)S(1)}, u32[]{:S(2)}, u32[]{:S(2)}) collective-permute-start(bf16[256,2048]{1,0:T(8,128)(2,1)} %x_ref.1), channel_id=1, source_target_pairs={{0,4},{4,0},{8,12},{12,8},{1,5},{5,1},{9,13},{13,9},{2,6},{6,2},{1... | collective-permute-start | bytes 3145736 | tf_op jit(solution)/shard_map/ppermute | solution.py:561
  2.7 5.9 %collective-permute-start.1 = (f32[8,256]{1,0:T(8,128)S(1)}, f32[8,256]{1,0:T(8,128)S(1)}, u32[]{:S(2)}, u32[]{:S(2)}) collective-permute-start(f32[8,256]{1,0:T(8,128)S(1)} %get-tuple-element.40.refs_0_), channel_id=1, source_target_pairs={{0,8},{4,12},{8,0},{12,4},{1,9},{5,13},{9,1},{13,5},{2,10},{6,14},... | collective-permute-start | bytes 24584 | tf_op jit(solution)/shard_map/ppermute | solution.py:565
  5.3 6.3 %collective-permute-start = (f32[8,256]{1,0:T(8,128)S(1)}, f32[8,256]{1,0:T(8,128)S(1)}, u32[]{:S(2)}, u32[]{:S(2)}) collective-permute-start(f32[8,256]{1,0:T(8,128)S(1)} %get-tuple-element.40.refs_0_), channel_id=1, source_target_pairs={{0,4},{4,0},{8,12},{12,8},{1,5},{5,1},{9,13},{13,9},{2,6},{6,2},{1... | collective-permute-start | bytes 24584 | tf_op jit(solution)/shard_map/ppermute | solution.py:561
  5.5 10.5 %collective-permute-start.3 = (bf16[2,512,128]{2,1,0:T(8,128)(2,1)S(1)}, bf16[2,512,128]{2,1,0:T(8,128)(2,1)S(1)}, u32[]{:S(2)}, u32[]{:S(2)}) collective-permute-start(bf16[2,512,128]{2,1,0:T(8,128)(2,1)S(1)} %dynamic-slice_bitcast_fusion.refs_3_), channel_id=1, source_target_pairs={{0,1},{1,2},{2,3},{3,0},{4,5},{5,6},{6,7},{7,4},{8,9},{9,10},{10,1... | collective-permute-start | bytes 786440 | tf_op jit(solution)/shard_map/ppermute | solution.py:568
  7.2 14.2 %collective-permute-start.5 = (bf16[128,2048]{1,0:T(8,128)(2,1)}, bf16[128,2048]{1,0:T(8,128)(2,1)}, u32[]{:S(2)}, u32[]{:S(2)}) collective-permute-start(bf16[128,2048]{1,0:T(8,128)(2,1)} %get-tuple-element.49), channel_id=1, source_target_pairs={{0,8},{4,12},{8,0},{12,4},{1,9},{5,13},{9,1},{13,5},{2,10},{6,14},... | collective-permute-start | bytes 1572872 | tf_op jit(solution)/shard_map/ppermute | solution.py:565
  8.6 3.1 %collective-permute-start.2 = (f32[8,256]{1,0:T(8,128)S(1)}, f32[8,256]{1,0:T(8,128)S(1)}, u32[]{:S(2)}, u32[]{:S(2)}) collective-permute-start(f32[8,256]{1,0:T(8,128)S(1)} %collective-permute-done.1.refs_2_), channel_id=1, source_target_pairs={{0,4},{4,0},{8,12},{12,8},{1,5},{5,1},{9,13},{13,9},{2,6},{6,2},{1... | collective-permute-start | bytes 24584 | tf_op jit(solution)/shard_map/ppermute | solution.py:561
  11.6 10.4 %copy-start.4 = (s32[16,1]{0,1:T(1,128)S(1)}, s32[16,1]{0,1:T(1,128)}, u32[]{:S(2)}) copy-start(s32[16,1]{0,1:T(1,128)} %param.17) | copy-start | bytes 196
  11.7 10.4 %copy-start.5 = (s32[4]{0:T(128)S(1)}, s32[4]{0:T(128)}, u32[]{:S(2)}) copy-start(s32[4]{0:T(128)} %param.18) | copy-start | bytes 52
  16.0 10.3 %copy-start.2 = (bf16[2,512,128]{2,1,0:T(8,128)(2,1)}, bf16[2,512,128]{2,1,0:T(8,128)(2,1)S(1)}, u32[]{:S(2)}) copy-start(bf16[2,512,128]{2,1,0:T(8,128)(2,1)S(1)} %collective-permute-done.3.refs_4_) | copy-start | bytes 786436
  16.0 5.4 %collective-permute-start.4 = (bf16[2,256,256]{2,1,0:T(8,128)(2,1)S(1)}, bf16[2,256,256]{2,1,0:T(8,128)(2,1)S(1)}, u32[]{:S(2)}, u32[]{:S(2)}) collective-permute-start(bf16[2,256,256]{2,1,0:T(8,128)(2,1)S(1)} %get-tuple-element.48), channel_id=1, source_target_pairs={{0,4},{4,0},{8,12},{12,8},{1,5},{5,1},{9,13},{13,9},{2,6},{6,2},{1... | collective-permute-start | bytes 786440 | tf_op jit(solution)/shard_map/ppermute | solution.py:561
  16.6 10.6 %collective-permute-start.6 = (bf16[2,512,128]{2,1,0:T(8,128)(2,1)S(1)}, bf16[2,512,128]{2,1,0:T(8,128)(2,1)S(1)}, u32[]{:S(2)}, u32[]{:S(2)}) collective-permute-start(bf16[2,512,128]{2,1,0:T(8,128)(2,1)S(1)} %collective-permute-done.3.refs_4_), channel_id=1, source_target_pairs={{0,1},{1,2},{2,3},{3,0},{4,5},{5,6},{6,7},{7,4},{8,9},{9,10},{10,1... | collective-permute-start | bytes 786440 | tf_op jit(solution)/shard_map/ppermute | solution.py:568
  21.4 5.8 %collective-permute-start.7 = (bf16[256,256]{1,0:T(8,128)(2,1)S(1)}, bf16[256,256]{1,0:T(8,128)(2,1)S(1)}, u32[]{:S(2)}, u32[]{:S(2)}) collective-permute-start(bf16[256,256]{1,0:T(8,128)(2,1)S(1)} %fusion.1), channel_id=1, source_target_pairs={{0,8},{4,12},{8,0},{12,4},{1,9},{5,13},{9,1},{13,5},{2,10},{6,14},... | collective-permute-start | bytes 393224 | tf_op jit(solution)/shard_map/ppermute | solution.py:565
  22.1 15.2 %collective-permute-start.9 = (bf16[128,2048]{1,0:T(8,128)(2,1)}, bf16[128,2048]{1,0:T(8,128)(2,1)S(1)}, u32[]{:S(2)}, u32[]{:S(2)}) collective-permute-start(bf16[128,2048]{1,0:T(8,128)(2,1)} %collective-permute-done.5.refs_6_), channel_id=1, source_target_pairs={{0,4},{4,0},{8,12},{12,8},{1,5},{5,1},{9,13},{13,9},{2,6},{6,2},{1... | collective-permute-start | bytes 1572872 | tf_op jit(solution)/shard_map/ppermute | solution.py:561
  22.3 5.0 %copy-start.6 = (bf16[128,2048]{1,0:T(8,128)(2,1)S(1)}, bf16[128,2048]{1,0:T(8,128)(2,1)}, u32[]{:S(2)}) copy-start(bf16[128,2048]{1,0:T(8,128)(2,1)} %get-tuple-element.58) | copy-start | bytes 1572868
  27.3 20.0 %collective-permute-start.13 = (bf16[128,2048]{1,0:T(8,128)(2,1)S(1)}, bf16[128,2048]{1,0:T(8,128)(2,1)S(1)}, u32[]{:S(2)}, u32[]{:S(2)}) collective-permute-start(bf16[128,2048]{1,0:T(8,128)(2,1)S(1)} %copy-done.6), channel_id=1, source_target_pairs={{0,8},{4,12},{8,0},{12,4},{1,9},{5,13},{9,1},{13,5},{2,10},{6,14},... | collective-permute-start | bytes 1572872 | tf_op jit(solution)/shard_map/ppermute | solution.py:565
  28.1 8.6 %collective-permute-start.10 = (bf16[256,256]{1,0:T(8,128)(2,1)S(1)}, bf16[256,256]{1,0:T(8,128)(2,1)S(1)}, u32[]{:S(2)}, u32[]{:S(2)}) collective-permute-start(bf16[256,256]{1,0:T(8,128)(2,1)S(1)} %kv_final.1.refs_2_), channel_id=1, source_target_pairs={{0,1},{1,2},{2,3},{3,0},{4,5},{5,6},{6,7},{7,4},{8,9},{9,10},{10,1... | collective-permute-start | bytes 393224 | tf_op jit(solution)/shard_map/ppermute | solution.py:568
  29.7 12.6 %collective-permute-start.12 = (bf16[2,512,128]{2,1,0:T(8,128)(2,1)S(1)}, bf16[2,512,128]{2,1,0:T(8,128)(2,1)S(1)}, u32[]{:S(2)}, u32[]{:S(2)}) collective-permute-start(bf16[2,512,128]{2,1,0:T(8,128)(2,1)S(1)} %collective-permute-done.6.refs_5_), channel_id=1, source_target_pairs={{0,1},{1,2},{2,3},{3,0},{4,5},{5,6},{6,7},{7,4},{8,9},{9,10},{10,1... | collective-permute-start | bytes 786440 | tf_op jit(solution)/shard_map/ppermute | solution.py:568
  36.7 7.2 %copy-start.3 = (bf16[2,512,128]{2,1,0:T(8,128)(2,1)S(1)}, bf16[2,512,128]{2,1,0:T(8,128)(2,1)}, u32[]{:S(2)}) copy-start(bf16[2,512,128]{2,1,0:T(8,128)(2,1)} %copy-done.2) | copy-start | bytes 786436
  36.7 7.2 %collective-permute-start.11 = (bf16[256,256]{1,0:T(8,128)(2,1)S(1)}, bf16[256,256]{1,0:T(8,128)(2,1)S(1)}, u32[]{:S(2)}, u32[]{:S(2)}) collective-permute-start(bf16[256,256]{1,0:T(8,128)(2,1)S(1)} %collective-permute-done.10.refs_1_), channel_id=1, source_target_pairs={{0,1},{1,2},{2,3},{3,0},{4,5},{5,6},{6,7},{7,4},{8,9},{9,10},{10,1... | collective-permute-start | bytes 393224 | tf_op jit(solution)/shard_map/ppermute | solution.py:568
  48.1 2.0 %collective-permute-start.14 = (bf16[128,2048]{1,0:T(8,128)(2,1)S(1)}, bf16[128,2048]{1,0:T(8,128)(2,1)S(1)}, u32[]{:S(2)}, u32[]{:S(2)}) collective-permute-start(bf16[128,2048]{1,0:T(8,128)(2,1)S(1)} %project.6), channel_id=1, source_target_pairs={{0,4},{4,0},{8,12},{12,8},{1,5},{5,1},{9,13},{13,9},{2,6},{6,2},{1... | collective-permute-start | bytes 1572872 | tf_op jit(solution)/shard_map/ppermute | solution.py:561
  48.2 3.3 %collective-permute-start.15 = (bf16[128,2048]{1,0:T(8,128)(2,1)S(1)}, bf16[128,2048]{1,0:T(8,128)(2,1)S(1)}, u32[]{:S(2)}, u32[]{:S(2)}) collective-permute-start(bf16[128,2048]{1,0:T(8,128)(2,1)S(1)} %collective-permute-done.13.refs_6_), channel_id=1, source_target_pairs={{0,4},{4,0},{8,12},{12,8},{1,5},{5,1},{9,13},{13,9},{2,6},{6,2},{1... | collective-permute-start | bytes 1572872 | tf_op jit(solution)/shard_map/ppermute | solution.py:561
  50.8 14.0 %collective-permute-start.17 = (bf16[128,2048]{1,0:T(8,128)(2,1)S(1)}, bf16[128,2048]{1,0:T(8,128)(2,1)S(1)}, u32[]{:S(2)}, u32[]{:S(2)}) collective-permute-start(bf16[128,2048]{1,0:T(8,128)(2,1)S(1)} %project.7), channel_id=1, source_target_pairs={{0,8},{4,12},{8,0},{12,4},{1,9},{5,13},{9,1},{13,5},{2,10},{6,14},... | collective-permute-start | bytes 1572872 | tf_op jit(solution)/shard_map/ppermute | solution.py:565
  60.0 5.9 %collective-permute-start.16 = (bf16[128,2048]{1,0:T(8,128)(2,1)S(1)}, bf16[128,2048]{1,0:T(8,128)(2,1)S(1)}, u32[]{:S(2)}, u32[]{:S(2)}) collective-permute-start(bf16[128,2048]{1,0:T(8,128)(2,1)S(1)} %project.8), channel_id=1, source_target_pairs={{0,4},{4,0},{8,12},{12,8},{1,5},{5,1},{9,13},{13,9},{2,6},{6,2},{1... | collective-permute-start | bytes 1572872 | tf_op jit(solution)/shard_map/ppermute | solution.py:561
  64.9 1.5 %collective-permute-start.18 = (bf16[2,512,128]{2,1,0:T(8,128)(2,1)S(1)}, bf16[2,512,128]{2,1,0:T(8,128)(2,1)S(1)}, u32[]{:S(2)}, u32[]{:S(2)}) collective-permute-start(bf16[2,512,128]{2,1,0:T(8,128)(2,1)S(1)} %dynamic-slice_bitcast_fusion.refs_3_), channel_id=1, source_target_pairs={{0,4},{4,0},{8,12},{12,8},{1,5},{5,1},{9,13},{13,9},{2,6},{6,2},{1... | collective-permute-start | bytes 786440 | tf_op jit(solution)/shard_map/ppermute | solution.py:561
  64.9 3.0 %collective-permute-start.19 = (bf16[64,2048]{1,0:T(8,128)(2,1)S(1)}, bf16[64,2048]{1,0:T(8,128)(2,1)S(1)}, u32[]{:S(2)}, u32[]{:S(2)}) collective-permute-start(bf16[64,2048]{1,0:T(8,128)(2,1)S(1)} %get-tuple-element.66), channel_id=1, source_target_pairs={{0,4},{4,0},{8,12},{12,8},{1,5},{5,1},{9,13},{13,9},{2,6},{6,2},{1... | collective-permute-start | bytes 786440 | tf_op jit(solution)/shard_map/ppermute | solution.py:561
  65.4 2.5 %collective-permute-start.20 = (bf16[64,2048]{1,0:T(8,128)(2,1)S(1)}, bf16[64,2048]{1,0:T(8,128)(2,1)S(1)}, u32[]{:S(2)}, u32[]{:S(2)}) collective-permute-start(bf16[64,2048]{1,0:T(8,128)(2,1)S(1)} %get-tuple-element.67), channel_id=1, source_target_pairs={{0,4},{4,0},{8,12},{12,8},{1,5},{5,1},{9,13},{13,9},{2,6},{6,2},{1... | collective-permute-start | bytes 786440 | tf_op jit(solution)/shard_map/ppermute | solution.py:561
  65.4 2.5 %collective-permute-start.21 = (bf16[64,2048]{1,0:T(8,128)(2,1)S(1)}, bf16[64,2048]{1,0:T(8,128)(2,1)S(1)}, u32[]{:S(2)}, u32[]{:S(2)}) collective-permute-start(bf16[64,2048]{1,0:T(8,128)(2,1)S(1)} %get-tuple-element.68), channel_id=1, source_target_pairs={{0,4},{4,0},{8,12},{12,8},{1,5},{5,1},{9,13},{13,9},{2,6},{6,2},{1... | collective-permute-start | bytes 786440 | tf_op jit(solution)/shard_map/ppermute | solution.py:561
  65.9 2.0 %collective-permute-start.22 = (bf16[64,2048]{1,0:T(8,128)(2,1)S(1)}, bf16[64,2048]{1,0:T(8,128)(2,1)S(1)}, u32[]{:S(2)}, u32[]{:S(2)}) collective-permute-start(bf16[64,2048]{1,0:T(8,128)(2,1)S(1)} %get-tuple-element.69), channel_id=1, source_target_pairs={{0,4},{4,0},{8,12},{12,8},{1,5},{5,1},{9,13},{13,9},{2,6},{6,2},{1... | collective-permute-start | bytes 786440 | tf_op jit(solution)/shard_map/ppermute | solution.py:561
  67.2 14.0 %collective-permute-start.23 = (bf16[128,2048]{1,0:T(8,128)(2,1)S(1)}, bf16[128,2048]{1,0:T(8,128)(2,1)S(1)}, u32[]{:S(2)}, u32[]{:S(2)}) collective-permute-start(bf16[128,2048]{1,0:T(8,128)(2,1)S(1)} %project.10), channel_id=1, source_target_pairs={{0,8},{4,12},{8,0},{12,4},{1,9},{5,13},{9,1},{13,5},{2,10},{6,14},... | collective-permute-start | bytes 1572872 | tf_op jit(solution)/shard_map/ppermute | solution.py:565
  81.2 1.3 %copy-start.1 = (bf16[1,2,512,512]{3,2,1,0:T(8,128)(2,1)S(1)}, bf16[1,2,512,512]{3,2,1,0:T(8,128)(2,1)}, u32[]{:S(2)}) copy-start(bf16[1,2,512,512]{3,2,1,0:T(8,128)(2,1)} %param.19) | copy-start | bytes 3145732

commit v5 on v4

--- a/solution.py
+++ b/solution.py
@@ -662,9 +662,9 @@
             last = after(attended[-1], *sent)
             others.append([to_core(x) for x in sent])
         if half == HALVES - 1:
-            terms = project(attended[:-1] + [last], w_held, 0, width, [half_rows // 2] * (2 * HALVES))
+            terms = project(attended[:-1] + [last], w_held, 0, width, [half_rows] * HALVES)
             one = after(one, *terms)
-            spacer = [to_core(after(memories[0], *outs[0], *terms))]
+            spacer = [to_core(after(stat, *outs[0], *terms))]
             terms = [to_core(x) for x in terms]
         for at, size in enumerate(cuts[half]):
             for ahead, other in zip(away, others):

time: 82.8 us -> 82.5 us (level)
    ppermute x13 -> x11, waiting for transfers between devices: 2 us -> 2.59 us  [to_core(): return lax.ppermute(x, 'tensor', [(i, i ^ 1) for i in range(n_tensor)])]
    ppermute x13 -> x11, starting transfers between devices: 2.28 us -> 1.91 us  [to_core(): return lax.ppermute(x, 'tensor', [(i, i ^ 1) for i in range(n_tensor)])]
  transfers between devices with their start and end apart: 24 -> 22, of which waited for: 9 -> 8; matrix products, arithmetic and copies ran while one was open for 3% -> 3% of each run, Pallas kernels for 45% -> 45%
where the time goes in v5:
time: 82.5 us; the launch traced here: 82.3 us
  Pallas kernels  37.8 us (46%)
  waiting for transfers between devices  26.8 us (32%)
  starting transfers between devices  13.2 us (16%)
  other arithmetic  3.02 us (4%)
  local copies, waits for them, and re-layouts  1.13 us (1%)
    ppermute x6, waiting for transfers between devices, to_chip(): return lax.ppermute(x, 'tensor', pairs)  19.5 us
    pallas_call x2, Pallas kernels, query_far(): pl.pallas_call(body, out_shape=[query, placed(pltpu.VMEM, held_shape)], g...  9.31 us
    pallas_call x2, Pallas kernels, attend_half(): pl.pallas_call(functools.partial(attend_kernel, half, len(memories)), out...  6.78 us
    ppermute x6, starting transfers between devices, to_chip(): return lax.ppermute(x, 'tensor', pairs)  5.8 us
    pallas_call x6, Pallas kernels, project(): pl.pallas_call(body, out_shape=[jax.ShapeDtypeStruct((size, width), kind)...  5.65 us
    ppermute x5, starting transfers between devices, up(): lax.ppermute(x, 'rows', [(i, (i + 1) % n_rows) for i in range(n_rows)])  5.45 us
    pallas_call x1, Pallas kernels, query_near(): pl.pallas_call(body, out_shape=placed(pltpu.VMEM, (rows, columns), f32),...  5.43 us
    ppermute x5, waiting for transfers between devices, up(): lax.ppermute(x, 'rows', [(i, (i + 1) % n_rows) for i in range(n_rows)])  4.76 us
  transfers between devices with their start and end apart: 22, of which 8 were waited for; matrix products, arithmetic and copies ran while one was open for 3% of the time, Pallas kernels for 45%

profile of v5, /device:TPU:0, one launch (start us, length us, event | category | flops | bytes accessed | tf_op | source)
XLA Modules:
  0.0 82.3 jit_solution(8045083519574557687)
XLA Ops:
  0.5 2.2 %prep.1 = (bf16[128,2048]{1,0:T(8,128)(2,1)}, bf16[128,2048]{1,0:T(8,128)(2,1)}, bf16[256,2048]{1,0:T(8,128)(2,1)S(1)}, f32[8,256]{1,0:T(8,128)S(1)}) custom-call(bf16[256,2048]{1,0:T(8,128)(2,1)} %x_ref.1), custom_call_target="tpu_custom_call" | custom-call | flops 10485 | bytes 20971 | tf_op jit(solution)/shard_map/prep/pallas_call | solution.py:106
  2.7 2.7 %collective-permute-start.1 = (f32[8,256]{1,0:T(8,128)S(1)}, f32[8,256]{1,0:T(8,128)S(1)}, u32[]{:S(2)}, u32[]{:S(2)}) collective-permute-start(f32[8,256]{1,0:T(8,128)S(1)} %get-tuple-element.67.refs_0_), channel_id=1, source_target_pairs={{0,8},{4,12},{8,0},{12,4},{1,9},{5,13},{9,1},{13,5},{2,10},{6,14},... | collective-permute-start | bytes 24584 | tf_op jit(solution)/shard_map/ppermute | solution.py:565
  5.5 1.6 %collective-permute-start.3 = (bf16[2,512,128]{2,1,0:T(8,128)(2,1)S(1)}, bf16[2,512,128]{2,1,0:T(8,128)(2,1)S(1)}, u32[]{:S(2)}, u32[]{:S(2)}) collective-permute-start(bf16[2,512,128]{2,1,0:T(8,128)(2,1)S(1)} %dynamic-slice_bitcast_fusion.refs_3_), channel_id=1, source_target_pairs={{0,1},{1,2},{2,3},{3,0},{4,5},{5,6},{6,7},{7,4},{8,9},{9,10},{10,1... | collective-permute-start | bytes 786440 | tf_op jit(solution)/shard_map/ppermute | solution.py:568
  7.7 0.8 pad_dynamic-slice_fusion
  8.7 0.7 broadcast_in_dim.43
  9.4 2.2 %load.1 = (bf16[2048,512]{1,0:T(8,128)(2,1)S(1)}, bf16[2048,512]{1,0:T(8,128)(2,1)S(1)}) custom-call(bf16[2048,512]{1,0:T(8,128)(2,1)} %refs_0_, bf16[2048,512]{1,0:T(8,128)(2,1)} %refs_1_.1), custom_call_target="tpu_custom_call" | custom-call | bytes 41943 | tf_op jit(solution)/shard_map/load/pallas_call | solution.py:143
  11.7 2.1 %kv_partial.1 = (bf16[2,256,256]{2,1,0:T(8,128)(2,1)S(1)}, bf16[2,256,256]{2,1,0:T(8,128)(2,1)S(1)}) custom-call(s32[5]{0:T(128)S(1)} %pad_add_fusion.4.scalars_ref, f32[8,256]{1,0:T(8,128)S(1)} %get-tuple-element.67.refs_0_, f32[8,256]{1,0:T(8,128)S(1)} %collective-permute-done.refs_1_, f32[8,256]{1,0:T(8,128)S(1)} %collective-permute-done.1.refs_2_, ...), custom_call_target="tpu_custom_call" | custom-call | flops 10737418 | bytes 10485 | tf_op jit(solution)/shard_map/kv_partial/pallas_call | solution.py:181
  13.7 2.3 %collective-permute-done.3.refs_4_ = bf16[2,512,128]{2,1,0:T(8,128)(2,1)S(1)} collective-permute-done((bf16[2,512,128]{2,1,0:T(8,128)(2,1)S(1)}, bf16[2,512,128]{2,1,0:T(8,128)(2,1)S(1)}, u32[]{:S(2)}, u32[]{:S(2)}) %collective-permute-start.3) | collective-permute-done | bytes 262176 | tf_op jit(solution)/shard_map/ppermute | solution.py:568
  16.7 4.7 %collective-permute-done.5.refs_6_ = bf16[128,2048]{1,0:T(8,128)(2,1)} collective-permute-done((bf16[128,2048]{1,0:T(8,128)(2,1)}, bf16[128,2048]{1,0:T(8,128)(2,1)}, u32[]{:S(2)}, u32[]{:S(2)}) %collective-permute-start.5) | collective-permute-done | bytes 524320 | tf_op jit(solution)/shard_map/ppermute | solution.py:565
  22.3 4.0 %load_columns.1.refs_1_ = bf16[1024,4096]{1,0:T(8,128)(2,1)S(1)} custom-call(s32[2]{0:T(128)S(1)} %pad_add_fusion.3.scalars_ref, bf16[1024,8192]{1,0:T(8,128)(2,1)} %refs_11_.1), custom_call_target="tpu_custom_call" | custom-call | bytes 83886 | tf_op jit(solution)/shard_map/load_columns/pallas_call | solution.py:251
  26.3 0.9 %collective-permute-done.6.refs_5_ = bf16[2,512,128]{2,1,0:T(8,128)(2,1)S(1)} collective-permute-done((bf16[2,512,128]{2,1,0:T(8,128)(2,1)S(1)}, bf16[2,512,128]{2,1,0:T(8,128)(2,1)S(1)}, u32[]{:S(2)}, u32[]{:S(2)}) %collective-permute-start.6) | collective-permute-done | bytes 262176 | tf_op jit(solution)/shard_map/ppermute | solution.py:568
  27.3 0.7 collective-permute-start.13
  28.1 1.6 %collective-permute-start.10 = (bf16[256,256]{1,0:T(8,128)(2,1)S(1)}, bf16[256,256]{1,0:T(8,128)(2,1)S(1)}, u32[]{:S(2)}, u32[]{:S(2)}) collective-permute-start(bf16[256,256]{1,0:T(8,128)(2,1)S(1)} %kv_final.1.refs_2_), channel_id=1, source_target_pairs={{0,1},{1,2},{2,3},{3,0},{4,5},{5,6},{6,7},{7,4},{8,9},{9,10},{10,1... | collective-permute-start | bytes 393224 | tf_op jit(solution)/shard_map/ppermute | solution.py:568
  29.7 1.6 %collective-permute-start.12 = (bf16[2,512,128]{2,1,0:T(8,128)(2,1)S(1)}, bf16[2,512,128]{2,1,0:T(8,128)(2,1)S(1)}, u32[]{:S(2)}, u32[]{:S(2)}) collective-permute-start(bf16[2,512,128]{2,1,0:T(8,128)(2,1)S(1)} %collective-permute-done.6.refs_5_), channel_id=1, source_target_pairs={{0,1},{1,2},{2,3},{3,0},{4,5},{5,6},{6,7},{7,4},{8,9},{9,10},{10,1... | collective-permute-start | bytes 786440 | tf_op jit(solution)/shard_map/ppermute | solution.py:568
  31.2 5.4 %query_near.1.refs_5_ = f32[256,1024]{1,0:T(8,128)S(1)} custom-call(s32[2]{0:T(128)S(1)} %pad_add_fusion.2.scalars_ref, f32[8,256]{1,0:T(8,128)S(1)} %get-tuple-element.67.refs_0_, f32[8,256]{1,0:T(8,128)S(1)} %collective-permute-done.refs_1_, f32[8,256]{1,0:T(8,128)S(1)} %collective-permute-done.1.refs_2_, f32[8,256]{1,0:T(8,128)S(1)} %collective-permute-done.2.refs_3_, ...), custom_call_target="tpu_custom_call" | custom-call | flops 21474836 | bytes 83886 | tf_op jit(solution)/shard_map/query_near/pallas_call | solution.py:303
  37.3 5.0 %query_far.2 = (bf16[128,1024]{1,0:T(8,128)(2,1)S(1)}, bf16[4096,1024]{1,0:T(8,128)(2,1)S(1)}) custom-call(s32[4]{0:T(128)S(1)} %pad_add_fusion.1.scalars_ref, f32[8,256]{1,0:T(8,128)S(1)} %get-tuple-element.67.refs_0_, f32[8,256]{1,0:T(8,128)S(1)} %collective-permute-done.refs_1_, f32[8,256]{1,0:T(8,128)S(1)} %collective-permute-done.1.refs_2_, ...), custom_call_target="tpu_custom_call" | custom-call | flops 10737418 | bytes 83886 | tf_op jit(solution)/shard_map/query_far/pallas_call | solution.py:398
  42.3 1.6 %collective-permute-done.11.refs_0_ = bf16[256,256]{1,0:T(8,128)(2,1)S(1)} collective-permute-done((bf16[256,256]{1,0:T(8,128)(2,1)S(1)}, bf16[256,256]{1,0:T(8,128)(2,1)S(1)}, u32[]{:S(2)}, u32[]{:S(2)}) %collective-permute-start.11) | collective-permute-done | bytes 131104 | tf_op jit(solution)/shard_map/ppermute | solution.py:568
  43.9 3.4 %attend_half.2.refs_0_ = bf16[128,1024]{1,0:T(8,128)(2,1)S(1)} custom-call(s32[21]{0:T(128)S(1)} %pad_add_fusion.pick_ref, bf16[128,1024]{1,0:T(8,128)(2,1)S(1)} %get-tuple-element.53.q_ref, s32[256,128]{1,0:T(8,128)S(1)} %broadcast_in_dim.39.qdoc_ref, s32[1,768]{1,0:T(1,128)S(1)} %broadcast_in_dim.37.kdoc_ref, ...), custom_call_target="tpu_custom_call" | custom-call | flops 6710886 | bytes 5242 | tf_op jit(solution)/shard_map/attend_half/pallas_call | solution.py:487
  47.3 0.7 project.6
  48.7 1.4 %collective-permute-done.14.refs_2_ = bf16[128,2048]{1,0:T(8,128)(2,1)S(1)} collective-permute-done((bf16[128,2048]{1,0:T(8,128)(2,1)S(1)}, bf16[128,2048]{1,0:T(8,128)(2,1)S(1)}, u32[]{:S(2)}, u32[]{:S(2)}) %collective-permute-start.14) | collective-permute-done | bytes 524320 | tf_op jit(solution)/shard_map/ppermute | solution.py:561
  50.1 0.8 project.7
  50.8 0.6 collective-permute-start.17
  51.5 4.3 %query_far.3 = (bf16[128,1024]{1,0:T(8,128)(2,1)S(1)}, bf16[1024,4096]{1,0:T(8,128)(2,1)S(1)}) custom-call(s32[4]{0:T(128)S(1)} %pad_add_fusion.1.scalars_ref, f32[8,256]{1,0:T(8,128)S(1)} %get-tuple-element.67.refs_0_, f32[8,256]{1,0:T(8,128)S(1)} %collective-permute-done.refs_1_, f32[8,256]{1,0:T(8,128)S(1)} %collective-permute-done.1.refs_2_, ...), custom_call_target="tpu_custom_call" | custom-call | flops 10737418 | bytes 83886 | tf_op jit(solution)/shard_map/query_far/pallas_call | solution.py:398
  55.8 3.4 %attend_half.3.refs_0_.refs_1_ = bf16[128,1024]{1,0:T(8,128)(2,1)S(1)} custom-call(s32[21]{0:T(128)S(1)} %pad_add_fusion.pick_ref, bf16[128,1024]{1,0:T(8,128)(2,1)S(1)} %get-tuple-element.61.q_ref, s32[256,128]{1,0:T(8,128)S(1)} %broadcast_in_dim.39.qdoc_ref, s32[1,768]{1,0:T(1,128)S(1)} %broadcast_in_dim.37.kdoc_ref, ...), custom_call_target="tpu_custom_call" | custom-call | flops 6710886 | bytes 5242 | tf_op jit(solution)/shard_map/attend_half/pallas_call | solution.py:487
  59.2 0.7 project.8
  60.1 1.3 %project.9 = (bf16[128,2048]{1,0:T(8,128)(2,1)S(1)}, bf16[128,2048]{1,0:T(8,128)(2,1)S(1)}) custom-call(bf16[128,1024]{1,0:T(8,128)(2,1)S(1)} %attend_half.2.refs_0_, bf16[128,1024]{1,0:T(8,128)(2,1)S(1)} %attend_half.3.refs_0_.refs_1_, bf16[1024,4096]{1,0:T(8,128)(2,1)S(1)} %get-tuple-element.63.refs_2_), custom_call_target="tpu_custom_call" | custom-call | flops 10737418 | bytes 15728 | tf_op jit(solution)/shard_map/project/pallas_call | solution.py:537
  62.0 2.9 %collective-permute-done.17 = bf16[128,2048]{1,0:T(8,128)(2,1)S(1)} collective-permute-done((bf16[128,2048]{1,0:T(8,128)(2,1)S(1)}, bf16[128,2048]{1,0:T(8,128)(2,1)S(1)}, u32[]{:S(2)}, u32[]{:S(2)}) %collective-permute-start.17) | collective-permute-done | bytes 524320 | tf_op jit(solution)/shard_map/ppermute | solution.py:565
  64.9 1.2 %collective-permute-done.18.refs_3_ = f32[8,256]{1,0:T(8,128)S(1)} collective-permute-done((f32[8,256]{1,0:T(8,128)S(1)}, f32[8,256]{1,0:T(8,128)S(1)}, u32[]{:S(2)}, u32[]{:S(2)}) %collective-permute-start.18) | collective-permute-done | bytes 8224 | tf_op jit(solution)/shard_map/ppermute | solution.py:561
  66.0 0.8 project.10
  67.5 1.3 %project.11 = (f32[128,2048]{1,0:T(8,128)S(1)}, f32[128,2048]{1,0:T(8,128)S(1)}) custom-call(bf16[128,1024]{1,0:T(8,128)(2,1)S(1)} %attend_half.2.refs_0_, bf16[128,1024]{1,0:T(8,128)(2,1)S(1)} %attend_half.3.refs_0_.refs_1_, bf16[1024,4096]{1,0:T(8,128)(2,1)S(1)} %get-tuple-element.63.refs_2_, bf16[128,2048]{1,0:T(8,128)(2,1)S(1)} %collective-permute-done.19.refs_3_, ...), custom_call_target="tpu_custom_call" | custom-call | flops 10737418 | bytes 15728 | tf_op jit(solution)/shard_map/project/pallas_call | solution.py:537
  69.0 11.9 %collective-permute-done.21 = bf16[128,2048]{1,0:T(8,128)(2,1)S(1)} collective-permute-done((bf16[128,2048]{1,0:T(8,128)(2,1)S(1)}, bf16[128,2048]{1,0:T(8,128)(2,1)S(1)}, u32[]{:S(2)}, u32[]{:S(2)}) %collective-permute-start.21) | collective-permute-done | bytes 524320 | tf_op jit(solution)/shard_map/ppermute | solution.py:565
  81.0 1.1 %pad_maximum_fusion = bf16[256,2048]{1,0:T(8,128)(2,1)} fusion(bf16[128,2048]{1,0:T(8,128)(2,1)S(1)} %add_convert_fusion, bf16[128,2048]{1,0:T(8,128)(2,1)S(1)} %add_convert_fusion.1), kind=kLoop, calls=%fused_computation | loop fusion | flops 2097152 | bytes 2097152 | tf_op jit(solution)/shard_map/concatenate | solution.py:685
  (61 shorter events, 6.0 us)
Async XLA Ops:
  0.0 5.5 %copy-start = (bf16[1,2,512,512]{3,2,1,0:T(8,128)(2,1)S(1)}, bf16[1,2,512,512]{3,2,1,0:T(8,128)(2,1)}, u32[]{:S(2)}) copy-start(bf16[1,2,512,512]{3,2,1,0:T(8,128)(2,1)} %param.19) | copy-start | bytes 3145732
  0.0 31.2 %collective-permute-start.8 = (bf16[256,2048]{1,0:T(8,128)(2,1)}, bf16[256,2048]{1,0:T(8,128)(2,1)S(1)}, u32[]{:S(2)}, u32[]{:S(2)}) collective-permute-start(bf16[256,2048]{1,0:T(8,128)(2,1)} %x_ref.1), channel_id=1, source_target_pairs={{0,4},{4,0},{8,12},{12,8},{1,5},{5,1},{9,13},{13,9},{2,6},{6,2},{1... | collective-permute-start | bytes 3145736 | tf_op jit(solution)/shard_map/ppermute | solution.py:561
  2.7 5.9 %collective-permute-start.1 = (f32[8,256]{1,0:T(8,128)S(1)}, f32[8,256]{1,0:T(8,128)S(1)}, u32[]{:S(2)}, u32[]{:S(2)}) collective-permute-start(f32[8,256]{1,0:T(8,128)S(1)} %get-tuple-element.67.refs_0_), channel_id=1, source_target_pairs={{0,8},{4,12},{8,0},{12,4},{1,9},{5,13},{9,1},{13,5},{2,10},{6,14},... | collective-permute-start | bytes 24584 | tf_op jit(solution)/shard_map/ppermute | solution.py:565
  5.3 6.3 %collective-permute-start = (f32[8,256]{1,0:T(8,128)S(1)}, f32[8,256]{1,0:T(8,128)S(1)}, u32[]{:S(2)}, u32[]{:S(2)}) collective-permute-start(f32[8,256]{1,0:T(8,128)S(1)} %get-tuple-element.67.refs_0_), channel_id=1, source_target_pairs={{0,4},{4,0},{8,12},{12,8},{1,5},{5,1},{9,13},{13,9},{2,6},{6,2},{1... | collective-permute-start | bytes 24584 | tf_op jit(solution)/shard_map/ppermute | solution.py:561
  5.5 10.5 %collective-permute-start.3 = (bf16[2,512,128]{2,1,0:T(8,128)(2,1)S(1)}, bf16[2,512,128]{2,1,0:T(8,128)(2,1)S(1)}, u32[]{:S(2)}, u32[]{:S(2)}) collective-permute-start(bf16[2,512,128]{2,1,0:T(8,128)(2,1)S(1)} %dynamic-slice_bitcast_fusion.refs_3_), channel_id=1, source_target_pairs={{0,1},{1,2},{2,3},{3,0},{4,5},{5,6},{6,7},{7,4},{8,9},{9,10},{10,1... | collective-permute-start | bytes 786440 | tf_op jit(solution)/shard_map/ppermute | solution.py:568
  7.2 14.2 %collective-permute-start.5 = (bf16[128,2048]{1,0:T(8,128)(2,1)}, bf16[128,2048]{1,0:T(8,128)(2,1)}, u32[]{:S(2)}, u32[]{:S(2)}) collective-permute-start(bf16[128,2048]{1,0:T(8,128)(2,1)} %get-tuple-element.47), channel_id=1, source_target_pairs={{0,8},{4,12},{8,0},{12,4},{1,9},{5,13},{9,1},{13,5},{2,10},{6,14},... | collective-permute-start | bytes 1572872 | tf_op jit(solution)/shard_map/ppermute | solution.py:565
  8.6 3.1 %collective-permute-start.2 = (f32[8,256]{1,0:T(8,128)S(1)}, f32[8,256]{1,0:T(8,128)S(1)}, u32[]{:S(2)}, u32[]{:S(2)}) collective-permute-start(f32[8,256]{1,0:T(8,128)S(1)} %collective-permute-done.1.refs_2_), channel_id=1, source_target_pairs={{0,4},{4,0},{8,12},{12,8},{1,5},{5,1},{9,13},{13,9},{2,6},{6,2},{1... | collective-permute-start | bytes 24584 | tf_op jit(solution)/shard_map/ppermute | solution.py:561
  11.6 10.4 %copy-start.4 = (s32[16,1]{0,1:T(1,128)S(1)}, s32[16,1]{0,1:T(1,128)}, u32[]{:S(2)}) copy-start(s32[16,1]{0,1:T(1,128)} %param.17) | copy-start | bytes 196
  11.7 10.4 %copy-start.5 = (s32[4]{0:T(128)S(1)}, s32[4]{0:T(128)}, u32[]{:S(2)}) copy-start(s32[4]{0:T(128)} %param.18) | copy-start | bytes 52
  16.0 10.3 %copy-start.2 = (bf16[2,512,128]{2,1,0:T(8,128)(2,1)}, bf16[2,512,128]{2,1,0:T(8,128)(2,1)S(1)}, u32[]{:S(2)}) copy-start(bf16[2,512,128]{2,1,0:T(8,128)(2,1)S(1)} %collective-permute-done.3.refs_4_) | copy-start | bytes 786436
  16.0 5.4 %collective-permute-start.4 = (bf16[2,256,256]{2,1,0:T(8,128)(2,1)S(1)}, bf16[2,256,256]{2,1,0:T(8,128)(2,1)S(1)}, u32[]{:S(2)}, u32[]{:S(2)}) collective-permute-start(bf16[2,256,256]{2,1,0:T(8,128)(2,1)S(1)} %get-tuple-element.46), channel_id=1, source_target_pairs={{0,4},{4,0},{8,12},{12,8},{1,5},{5,1},{9,13},{13,9},{2,6},{6,2},{1... | collective-permute-start | bytes 786440 | tf_op jit(solution)/shard_map/ppermute | solution.py:561
  16.6 10.6 %collective-permute-start.6 = (bf16[2,512,128]{2,1,0:T(8,128)(2,1)S(1)}, bf16[2,512,128]{2,1,0:T(8,128)(2,1)S(1)}, u32[]{:S(2)}, u32[]{:S(2)}) collective-permute-start(bf16[2,512,128]{2,1,0:T(8,128)(2,1)S(1)} %collective-permute-done.3.refs_4_), channel_id=1, source_target_pairs={{0,1},{1,2},{2,3},{3,0},{4,5},{5,6},{6,7},{7,4},{8,9},{9,10},{10,1... | collective-permute-start | bytes 786440 | tf_op jit(solution)/shard_map/ppermute | solution.py:568
  21.4 5.8 %collective-permute-start.7 = (bf16[256,256]{1,0:T(8,128)(2,1)S(1)}, bf16[256,256]{1,0:T(8,128)(2,1)S(1)}, u32[]{:S(2)}, u32[]{:S(2)}) collective-permute-start(bf16[256,256]{1,0:T(8,128)(2,1)S(1)} %fusion.1), channel_id=1, source_target_pairs={{0,8},{4,12},{8,0},{12,4},{1,9},{5,13},{9,1},{13,5},{2,10},{6,14},... | collective-permute-start | bytes 393224 | tf_op jit(solution)/shard_map/ppermute | solution.py:565
  22.1 15.2 %collective-permute-start.9 = (bf16[128,2048]{1,0:T(8,128)(2,1)}, bf16[128,2048]{1,0:T(8,128)(2,1)S(1)}, u32[]{:S(2)}, u32[]{:S(2)}) collective-permute-start(bf16[128,2048]{1,0:T(8,128)(2,1)} %collective-permute-done.5.refs_6_), channel_id=1, source_target_pairs={{0,4},{4,0},{8,12},{12,8},{1,5},{5,1},{9,13},{13,9},{2,6},{6,2},{1... | collective-permute-start | bytes 1572872 | tf_op jit(solution)/shard_map/ppermute | solution.py:561
  22.3 5.0 %copy-start.6 = (bf16[128,2048]{1,0:T(8,128)(2,1)S(1)}, bf16[128,2048]{1,0:T(8,128)(2,1)}, u32[]{:S(2)}) copy-start(bf16[128,2048]{1,0:T(8,128)(2,1)} %get-tuple-element.56) | copy-start | bytes 1572868
  27.3 20.0 %collective-permute-start.13 = (bf16[128,2048]{1,0:T(8,128)(2,1)S(1)}, bf16[128,2048]{1,0:T(8,128)(2,1)S(1)}, u32[]{:S(2)}, u32[]{:S(2)}) collective-permute-start(bf16[128,2048]{1,0:T(8,128)(2,1)S(1)} %copy-done.6), channel_id=1, source_target_pairs={{0,8},{4,12},{8,0},{12,4},{1,9},{5,13},{9,1},{13,5},{2,10},{6,14},... | collective-permute-start | bytes 1572872 | tf_op jit(solution)/shard_map/ppermute | solution.py:565
  28.1 8.6 %collective-permute-start.10 = (bf16[256,256]{1,0:T(8,128)(2,1)S(1)}, bf16[256,256]{1,0:T(8,128)(2,1)S(1)}, u32[]{:S(2)}, u32[]{:S(2)}) collective-permute-start(bf16[256,256]{1,0:T(8,128)(2,1)S(1)} %kv_final.1.refs_2_), channel_id=1, source_target_pairs={{0,1},{1,2},{2,3},{3,0},{4,5},{5,6},{6,7},{7,4},{8,9},{9,10},{10,1... | collective-permute-start | bytes 393224 | tf_op jit(solution)/shard_map/ppermute | solution.py:568
  29.7 12.6 %collective-permute-start.12 = (bf16[2,512,128]{2,1,0:T(8,128)(2,1)S(1)}, bf16[2,512,128]{2,1,0:T(8,128)(2,1)S(1)}, u32[]{:S(2)}, u32[]{:S(2)}) collective-permute-start(bf16[2,512,128]{2,1,0:T(8,128)(2,1)S(1)} %collective-permute-done.6.refs_5_), channel_id=1, source_target_pairs={{0,1},{1,2},{2,3},{3,0},{4,5},{5,6},{6,7},{7,4},{8,9},{9,10},{10,1... | collective-permute-start | bytes 786440 | tf_op jit(solution)/shard_map/ppermute | solution.py:568
  36.7 7.2 %copy-start.3 = (bf16[2,512,128]{2,1,0:T(8,128)(2,1)S(1)}, bf16[2,512,128]{2,1,0:T(8,128)(2,1)}, u32[]{:S(2)}) copy-start(bf16[2,512,128]{2,1,0:T(8,128)(2,1)} %copy-done.2) | copy-start | bytes 786436
  36.7 7.2 %collective-permute-start.11 = (bf16[256,256]{1,0:T(8,128)(2,1)S(1)}, bf16[256,256]{1,0:T(8,128)(2,1)S(1)}, u32[]{:S(2)}, u32[]{:S(2)}) collective-permute-start(bf16[256,256]{1,0:T(8,128)(2,1)S(1)} %collective-permute-done.10.refs_1_), channel_id=1, source_target_pairs={{0,1},{1,2},{2,3},{3,0},{4,5},{5,6},{6,7},{7,4},{8,9},{9,10},{10,1... | collective-permute-start | bytes 393224 | tf_op jit(solution)/shard_map/ppermute | solution.py:568
  48.1 2.0 %collective-permute-start.14 = (bf16[128,2048]{1,0:T(8,128)(2,1)S(1)}, bf16[128,2048]{1,0:T(8,128)(2,1)S(1)}, u32[]{:S(2)}, u32[]{:S(2)}) collective-permute-start(bf16[128,2048]{1,0:T(8,128)(2,1)S(1)} %project.6), channel_id=1, source_target_pairs={{0,4},{4,0},{8,12},{12,8},{1,5},{5,1},{9,13},{13,9},{2,6},{6,2},{1... | collective-permute-start | bytes 1572872 | tf_op jit(solution)/shard_map/ppermute | solution.py:561
  48.2 3.3 %collective-permute-start.15 = (bf16[128,2048]{1,0:T(8,128)(2,1)S(1)}, bf16[128,2048]{1,0:T(8,128)(2,1)S(1)}, u32[]{:S(2)}, u32[]{:S(2)}) collective-permute-start(bf16[128,2048]{1,0:T(8,128)(2,1)S(1)} %collective-permute-done.13.refs_6_), channel_id=1, source_target_pairs={{0,4},{4,0},{8,12},{12,8},{1,5},{5,1},{9,13},{13,9},{2,6},{6,2},{1... | collective-permute-start | bytes 1572872 | tf_op jit(solution)/shard_map/ppermute | solution.py:561
  50.8 14.0 %collective-permute-start.17 = (bf16[128,2048]{1,0:T(8,128)(2,1)S(1)}, bf16[128,2048]{1,0:T(8,128)(2,1)S(1)}, u32[]{:S(2)}, u32[]{:S(2)}) collective-permute-start(bf16[128,2048]{1,0:T(8,128)(2,1)S(1)} %project.7), channel_id=1, source_target_pairs={{0,8},{4,12},{8,0},{12,4},{1,9},{5,13},{9,1},{13,5},{2,10},{6,14},... | collective-permute-start | bytes 1572872 | tf_op jit(solution)/shard_map/ppermute | solution.py:565
  60.0 4.9 %collective-permute-start.16 = (bf16[128,2048]{1,0:T(8,128)(2,1)S(1)}, bf16[128,2048]{1,0:T(8,128)(2,1)S(1)}, u32[]{:S(2)}, u32[]{:S(2)}) collective-permute-start(bf16[128,2048]{1,0:T(8,128)(2,1)S(1)} %project.8), channel_id=1, source_target_pairs={{0,4},{4,0},{8,12},{12,8},{1,5},{5,1},{9,13},{13,9},{2,6},{6,2},{1... | collective-permute-start | bytes 1572872 | tf_op jit(solution)/shard_map/ppermute | solution.py:561
  61.4 6.1 %collective-permute-start.19 = (bf16[128,2048]{1,0:T(8,128)(2,1)S(1)}, bf16[128,2048]{1,0:T(8,128)(2,1)S(1)}, u32[]{:S(2)}, u32[]{:S(2)}) collective-permute-start(bf16[128,2048]{1,0:T(8,128)(2,1)S(1)} %get-tuple-element.64), channel_id=1, source_target_pairs={{0,4},{4,0},{8,12},{12,8},{1,5},{5,1},{9,13},{13,9},{2,6},{6,2},{1... | collective-permute-start | bytes 1572872 | tf_op jit(solution)/shard_map/ppermute | solution.py:561
  61.9 5.5 %collective-permute-start.20 = (bf16[128,2048]{1,0:T(8,128)(2,1)S(1)}, bf16[128,2048]{1,0:T(8,128)(2,1)S(1)}, u32[]{:S(2)}, u32[]{:S(2)}) collective-permute-start(bf16[128,2048]{1,0:T(8,128)(2,1)S(1)} %get-tuple-element.65), channel_id=1, source_target_pairs={{0,4},{4,0},{8,12},{12,8},{1,5},{5,1},{9,13},{13,9},{2,6},{6,2},{1... | collective-permute-start | bytes 1572872 | tf_op jit(solution)/shard_map/ppermute | solution.py:561
  64.9 1.2 %collective-permute-start.18 = (f32[8,256]{1,0:T(8,128)S(1)}, f32[8,256]{1,0:T(8,128)S(1)}, u32[]{:S(2)}, u32[]{:S(2)}) collective-permute-start(f32[8,256]{1,0:T(8,128)S(1)} %get-tuple-element.67.refs_0_), channel_id=1, source_target_pairs={{0,4},{4,0},{8,12},{12,8},{1,5},{5,1},{9,13},{13,9},{2,6},{6,2},{1... | collective-permute-start | bytes 24584 | tf_op jit(solution)/shard_map/ppermute | solution.py:561
  66.8 14.1 %collective-permute-start.21 = (bf16[128,2048]{1,0:T(8,128)(2,1)S(1)}, bf16[128,2048]{1,0:T(8,128)(2,1)S(1)}, u32[]{:S(2)}, u32[]{:S(2)}) collective-permute-start(bf16[128,2048]{1,0:T(8,128)(2,1)S(1)} %project.10), channel_id=1, source_target_pairs={{0,8},{4,12},{8,0},{12,4},{1,9},{5,13},{9,1},{13,5},{2,10},{6,14},... | collective-permute-start | bytes 1572872 | tf_op jit(solution)/shard_map/ppermute | solution.py:565
  80.9 1.4 %copy-start.1 = (bf16[1,2,512,512]{3,2,1,0:T(8,128)(2,1)S(1)}, bf16[1,2,512,512]{3,2,1,0:T(8,128)(2,1)}, u32[]{:S(2)}) copy-start(bf16[1,2,512,512]{3,2,1,0:T(8,128)(2,1)} %param.19) | copy-start | bytes 3145732
